TPU v7x, 32 devices: a whole 2x2x4 slice. The times are simulated.
32 devices in a mesh: pairs: 8 (over z, core), cols: 4 (over y, x).
Axes of the slice: x: 2, y: 2, z: 4, core: 2. Of those that a mesh axis runs over, the one named last changes fastest.
Arguments:
- pair_list: int32 [48, 5], P('pairs'), may hold values from 0 to 7, as said below
- near_tile_block: bfloat16 [48, 2048, 2048], P('pairs', None, 'cols'), may hold values from -0.0546875 to 0.0546875
- history: float32 [4, 16, 32, 2048], P(None, 'pairs', None, 'cols'), may hold values from -6 to 6
- excitation: float32 [4, 16, 32, 2048], P(None, 'pairs', None, 'cols'), may hold values from -6 to 6
- diagonal: float32 [16, 2048], P('pairs', 'cols'), may hold values from 2 to 4
Outputs:
- densities: float32 [4, 16, 32, 2048], P(None, 'pairs', None, 'cols')
Inputs may be any that keep to these rules, and one draw needn't show every extreme that they name: `pair_list`: rows s * 6 to s * 6 + 5 are the slots of index s of pairs. Column 0 and column 2 are below 2, column 1 below 8, column 3 below 4, column 4 is 0 or 1. The live slots of a device come first and number at least 3; among them no value of column 1 appears more than 3 times, and some value exactly 3 times. One device has all 6 slots live.
All inputs are finite; a program needn't handle non-finite values.
Results may differ from a plain program's by a relative error of at most 0.0018.
Values may be sent and summed in bfloat16 or wider, within the bound.
No kernel may reach another device: no remote copies, remote signals or barrier semaphores. Data moves between devices by JAX's collectives and lax.ppermute only.
A program may use at most 64 MiB of HBM per device.

v0:
```python
import functools

import jax
import jax.numpy as jnp
from jax import lax
from jax.experimental import pallas as pl
from jax.experimental.pallas import tpu as pltpu
from jax.sharding import PartitionSpec as P

STEPS = 4
CORES = 2
F32 = jnp.float32
BF16 = jnp.bfloat16


def swapped(n, bits):
    return [(i, i ^ bits) for i in range(n)]


def far_first(n):
    return sorted(range(1, n), key=lambda k: -bin(k).count("1") * n - k)


def pick(step, delays, slot_delay, slot_cluster, old, new, put):
    for delay in range(delays):

        @pl.when(slot_delay == delay)
        def _(delay=delay):
            if delay < step:
                put([ref[slot_cluster] for ref in new[step - 1 - delay]])
            else:
                put([ref[delay - step, slot_cluster] for ref in old])


def backward_kernel(step, groups, cols, pairs_ref, place_ref, tile_ref, *refs):
    old = refs[:cols]
    new = [refs[cols * (1 + j) : cols * (2 + j)] for j in range(step)]
    same_ref, other_ref, rows_ref, sum_ref = refs[cols * (1 + step) :]
    slots, _, width = tile_ref.shape
    me, col = place_ref[0], place_ref[1]
    sum_ref[...] = jnp.zeros_like(sum_ref)
    for s in range(slots):

        def put(blocks, s=s):
            for k in range(cols):
                rows_ref[s, k] = blocks[k]

        pick(step, old[0].shape[0], pairs_ref[s, 3], pairs_ref[s, 0], old, new, put)
    for s in range(slots):

        @pl.when(pairs_ref[s, 4] == 1)
        def _(s=s):
            total = None
            for k in range(cols):
                start = pl.multiple_of((col ^ k) * width, width)
                part = jnp.dot(
                    rows_ref[s, k],
                    tile_ref[s, pl.ds(start, width), :],
                    preferred_element_type=F32,
                )
                total = part if total is None else total + part
            piece = pairs_ref[s, 1] ^ me
            sum_ref[piece, pairs_ref[s, 2]] += total

    for k in range(groups // CORES):
        same_ref[k] = sum_ref[CORES * k]
        other_ref[k] = sum_ref[CORES * k + 1].astype(other_ref.dtype)


def forward_kernel(step, groups, cols, pairs_ref, place_ref, tile_ref, *refs):
    old = refs[:groups]
    new = [refs[groups * (1 + j) : groups * (2 + j)] for j in range(step)]
    rest = refs[groups * (1 + step) :]
    outs, near_ref, sum_ref = rest[:cols], rest[cols], rest[cols + 1]
    slots, _, width = tile_ref.shape
    me, col = place_ref[0], place_ref[1]
    sum_ref[...] = jnp.zeros_like(sum_ref)
    for s in range(slots):
        piece = pairs_ref[s, 1] ^ me
        for p in range(groups):

            @pl.when(piece == p)
            def _(s=s, p=p):
                def put(blocks):
                    near_ref[s] = blocks[0]

                pick(
                    step,
                    old[0].shape[0],
                    pairs_ref[s, 3],
                    pairs_ref[s, 2],
                    [old[p]],
                    [[n[p]] for n in new],
                    put,
                )

    for s in range(slots):

        @pl.when(pairs_ref[s, 4] == 1)
        def _(s=s):
            for k in range(cols):
                start = pl.multiple_of((col ^ k) * width, width)
                part = lax.dot_general(
                    near_ref[s],
                    tile_ref[s, pl.ds(start, width), :],
                    (((1,), (1,)), ((), ())),
                    preferred_element_type=F32,
                )
                sum_ref[k, pairs_ref[s, 0]] += part

    for k in range(cols):
        outs[k][...] = sum_ref[k].astype(outs[k].dtype)


def shards(pair_list, near_tile_block, history, excitation, diagonal):
    groups = lax.axis_size("pairs")
    cols = lax.axis_size("cols")
    planes = groups // CORES
    delays, clusters, excite, width = history.shape
    slots = pair_list.shape[0]
    block = (clusters, excite, width)
    place = jnp.stack([lax.axis_index("pairs"), lax.axis_index("cols")]).astype(jnp.int32)

    smem = pl.BlockSpec(memory_space=pltpu.SMEM)
    vmem = pl.BlockSpec(memory_space=pltpu.VMEM)
    cost = pl.CostEstimate(
        flops=2 * near_tile_block.size * excite,
        bytes_accessed=2 * near_tile_block.size,
        transcendentals=0,
    )
    limit = pltpu.CompilerParams(vmem_limit_bytes=40 * 2**20)

    def spread_cols(x):
        got = {0: x}
        for k in far_first(cols):
            got[k] = lax.ppermute(x, "cols", swapped(cols, k))
        return [got[k] for k in range(cols)]

    def spread_pairs(x):
        got = {0: x}
        for k in far_first(planes):
            got[CORES * k] = lax.ppermute(x, "pairs", swapped(groups, CORES * k))
        for k in range(planes):
            got[CORES * k + 1] = lax.ppermute(got[CORES * k], "pairs", swapped(groups, 1))
        return [got[p] for p in range(groups)]

    def backward(step, old, new):
        return pl.pallas_call(
            functools.partial(backward_kernel, step, groups, cols),
            out_shape=(
                jax.ShapeDtypeStruct((planes, *block), F32),
                jax.ShapeDtypeStruct((planes, *block), BF16),
            ),
            in_specs=[smem, smem] + [vmem] * (1 + cols * (1 + step)),
            out_specs=(vmem, vmem),
            scratch_shapes=[
                pltpu.VMEM((slots, cols, excite, width), BF16),
                pltpu.VMEM((groups, *block), F32),
            ],
            cost_estimate=cost,
            compiler_params=limit,
            name=f"backward{step}",
        )(pair_list, place, near_tile_block, *old, *[x for n in new for x in n])

    def forward(step, old, new):
        return pl.pallas_call(
            functools.partial(forward_kernel, step, groups, cols),
            out_shape=[jax.ShapeDtypeStruct(block, F32)]
            + [jax.ShapeDtypeStruct(block, BF16)] * (cols - 1),
            in_specs=[smem, smem] + [vmem] * (1 + groups * (1 + step)),
            out_specs=[vmem] * cols,
            scratch_shapes=[
                pltpu.VMEM((slots, excite, width), BF16),
                pltpu.VMEM((cols, *block), F32),
            ],
            cost_estimate=cost,
            compiler_params=limit,
            name=f"forward{step}",
        )(pair_list, place, near_tile_block, *old, *[x for n in new for x in n])

    rounded = history.astype(BF16)
    old_rows = spread_cols(rounded)
    old_near = spread_pairs(rounded)
    new_rows, new_near, results = [], [], []
    for step in range(STEPS):
        same, other = backward(step, old_rows, new_rows)
        mate = lax.ppermute(other, "pairs", swapped(groups, 1))
        field = same[0] + mate[0].astype(F32)
        for k in far_first(planes):
            sent = (same[k] + mate[k].astype(F32)).astype(BF16)
            field += lax.ppermute(sent, "pairs", swapped(groups, CORES * k)).astype(F32)
        parts = forward(step, old_near, new_near)
        field += parts[0]
        for k in far_first(cols):
            field += lax.ppermute(parts[k], "cols", swapped(cols, k)).astype(F32)
        fresh = (excitation[step] - field) / diagonal[:, None, :]
        results.append(fresh)
        if step + 1 < STEPS:
            newest = fresh.astype(BF16)
            new_rows.append(spread_cols(newest))
            new_near.append(spread_pairs(newest))
    return jnp.stack(results)


def solution(mesh):
    placed = (
        P("pairs", None),
        P("pairs", None, "cols"),
        P(None, "pairs", None, "cols"),
        P(None, "pairs", None, "cols"),
        P("pairs", "cols"),
    )
    return jax.shard_map(
        shards,
        mesh=mesh,
        in_specs=placed,
        out_specs=P(None, "pairs", None, "cols"),
        check_vma=False,
    )
```

profile of v0, /device:TPU:0, one launch (start us, length us, event | category | flops | bytes accessed | tf_op | source)
XLA Modules:
  0.0 198.6 jit_solution(7273585739224352438)
XLA Ops:
  1.1 5.1 %collective-permute-start.12 = (bf16[4,2,32,512]{3,2,1,0:T(8,128)(2,1)S(1)}, bf16[4,2,32,512]{3,2,1,0:T(8,128)(2,1)S(1)}, u32[]{:S(2)}, u32[]{:S(2)}) collective-permute-start(bf16[4,2,32,512]{3,2,1,0:T(8,128)(2,1)S(1)} %convert_element_type.220.refs_0_), channel_id=1, source_target_pairs={{0,24},{4,28},{8,16},{12,20},{16,8},{20,12},{24,0},{28,4},{1,25},{... | collective-permute-start | bytes 786440 | tf_op jit(solution)/shard_map/ppermute | solution.py:142
  6.8 2.6 %collective-permute-start.2 = (bf16[4,2,32,512]{3,2,1,0:T(8,128)(2,1)S(1)}, bf16[4,2,32,512]{3,2,1,0:T(8,128)(2,1)S(1)}, u32[]{:S(2)}, u32[]{:S(2)}) collective-permute-start(bf16[4,2,32,512]{3,2,1,0:T(8,128)(2,1)S(1)} %convert_element_type.220.refs_0_), channel_id=1, source_target_pairs={{0,3},{1,2},{2,1},{3,0},{4,7},{5,6},{6,5},{7,4},{8,11},{9,10},{10,... | collective-permute-start | bytes 786440 | tf_op jit(solution)/shard_map/ppermute | solution.py:136
  9.9 3.5 %collective-permute-done.12.refs_6_ = bf16[4,2,32,512]{3,2,1,0:T(8,128)(2,1)S(1)} collective-permute-done((bf16[4,2,32,512]{3,2,1,0:T(8,128)(2,1)S(1)}, bf16[4,2,32,512]{3,2,1,0:T(8,128)(2,1)S(1)}, u32[]{:S(2)}, u32[]{:S(2)}) %collective-permute-start.12) | collective-permute-done | bytes 262176 | tf_op jit(solution)/shard_map/ppermute | solution.py:142
  15.2 13.3 %collective-permute-done.10.refs_4_ = bf16[4,2,32,512]{3,2,1,0:T(8,128)(2,1)S(1)} collective-permute-done((bf16[4,2,32,512]{3,2,1,0:T(8,128)(2,1)S(1)}, bf16[4,2,32,512]{3,2,1,0:T(8,128)(2,1)S(1)}, u32[]{:S(2)}, u32[]{:S(2)}) %collective-permute-start.10) | collective-permute-done | bytes 262176 | tf_op jit(solution)/shard_map/ppermute | solution.py:142
  29.6 4.6 %copy-done = bf16[6,2048,512]{2,1,0:T(8,128)(2,1)S(1)} copy-done((bf16[6,2048,512]{2,1,0:T(8,128)(2,1)S(1)}, bf16[6,2048,512]{2,1,0:T(8,128)(2,1)}, u32[]{:S(2)}) %copy-start) | copy-done | bytes 12582936
  34.9 3.2 %backward0.1 = (f32[4,2,32,512]{3,2,1,0:T(8,128)S(1)}, bf16[4,2,32,512]{3,2,1,0:T(8,128)(2,1)S(1)}) custom-call(s32[6,5]{1,0:T(8,128)S(1)} %copy-done.1, s32[2]{0:T(128)S(1)} %pad_add_fusion.place_ref, bf16[6,2048,512]{2,1,0:T(8,128)(2,1)S(1)} %copy-done, bf16[4,2,32,512]{3,2,1,0:T(8,128)(2,1)S(1)} %convert_element_type.220.refs_0_, ...), custom_call_target="tpu_custom_call" | custom-call | flops 402653184 | bytes 12582912 | tf_op jit(solution)/shard_map/backward0/pallas_call | solution.py:148
  38.3 8.7 %forward0.1 = (f32[2,32,512]{2,1,0:T(8,128)S(1)}, bf16[2,32,512]{2,1,0:T(8,128)(2,1)S(1)}, bf16[2,32,512]{2,1,0:T(8,128)(2,1)S(1)}, bf16[2,32,512]{2,1,0:T(8,128)(2,1)S(1)}) custom-call(s32[6,5]{1,0:T(8,128)S(1)} %copy-done.1, s32[2]{0:T(128)S(1)} %pad_add_fusion.place_ref, bf16[6,2048,512]{2,1,0:T(8,128)(2,1)} %tile_ref.15, ...), custom_call_target="tpu_custom_call" | custom-call | flops 402653184 | bytes 12582912 | tf_op jit(solution)/shard_map/forward0/pallas_call | solution.py:166
  46.9 2.5 %collective-permute-start.14 = (bf16[2,32,512]{2,1,0:T(8,128)(2,1)S(1)}, bf16[2,32,512]{2,1,0:T(8,128)(2,1)S(1)}, u32[]{:S(2)}, u32[]{:S(2)}) collective-permute-start(bf16[2,32,512]{2,1,0:T(8,128)(2,1)S(1)} %get-tuple-element.32), channel_id=1, source_target_pairs={{0,3},{1,2},{2,1},{3,0},{4,7},{5,6},{6,5},{7,4},{8,11},{9,10},{10,... | collective-permute-start | bytes 196616 | tf_op jit(solution)/shard_map/ppermute | solution.py:195
  50.5 3.8 %collective-permute-start.4 = (bf16[2,32,512]{2,1,0:T(8,128)(2,1)S(1)}, bf16[2,32,512]{2,1,0:T(8,128)(2,1)S(1)}, u32[]{:S(2)}, u32[]{:S(2)}) collective-permute-start(bf16[2,32,512]{2,1,0:T(8,128)(2,1)S(1)} %get-tuple-element.68), channel_id=1, source_target_pairs={{0,24},{4,28},{8,16},{12,20},{16,8},{20,12},{24,0},{28,4},{1,25},{... | collective-permute-start | bytes 196616 | tf_op jit(solution)/shard_map/ppermute | solution.py:191
  59.8 2.5 %collective-permute-start.19 = (bf16[2,32,512]{2,1,0:T(8,128)(2,1)S(1)}, bf16[2,32,512]{2,1,0:T(8,128)(2,1)S(1)}, u32[]{:S(2)}, u32[]{:S(2)}) collective-permute-start(bf16[2,32,512]{2,1,0:T(8,128)(2,1)S(1)} %get-tuple-element.57.refs_4_.refs_8_), channel_id=1, source_target_pairs={{0,3},{1,2},{2,1},{3,0},{4,7},{5,6},{6,5},{7,4},{8,11},{9,10},{10,... | collective-permute-start | bytes 196616 | tf_op jit(solution)/shard_map/ppermute | solution.py:136
  67.1 7.2 %backward1.1 = (f32[4,2,32,512]{3,2,1,0:T(8,128)S(1)}, bf16[4,2,32,512]{3,2,1,0:T(8,128)(2,1)S(1)}) custom-call(s32[6,5]{1,0:T(8,128)S(1)} %copy-done.1, s32[2]{0:T(128)S(1)} %pad_add_fusion.place_ref, bf16[6,2048,512]{2,1,0:T(8,128)(2,1)} %tile_ref.15, bf16[4,2,32,512]{3,2,1,0:T(8,128)(2,1)S(1)} %convert_element_type.220.refs_0_, ...), custom_call_target="tpu_custom_call" | custom-call | flops 402653184 | bytes 12582912 | tf_op jit(solution)/shard_map/backward1/pallas_call | solution.py:148
  74.4 3.5 %collective-permute-start.29 = (bf16[2,32,512]{2,1,0:T(8,128)(2,1)S(1)}, bf16[2,32,512]{2,1,0:T(8,128)(2,1)S(1)}, u32[]{:S(2)}, u32[]{:S(2)}) collective-permute-start(bf16[2,32,512]{2,1,0:T(8,128)(2,1)S(1)} %get-tuple-element.57.refs_4_.refs_8_), channel_id=1, source_target_pairs={{0,24},{4,28},{8,16},{12,20},{16,8},{20,12},{24,0},{28,4},{1,25},{... | collective-permute-start | bytes 196616 | tf_op jit(solution)/shard_map/ppermute | solution.py:142
  85.0 8.7 %forward1.1 = (f32[2,32,512]{2,1,0:T(8,128)S(1)}, bf16[2,32,512]{2,1,0:T(8,128)(2,1)S(1)}, bf16[2,32,512]{2,1,0:T(8,128)(2,1)S(1)}, bf16[2,32,512]{2,1,0:T(8,128)(2,1)S(1)}) custom-call(s32[6,5]{1,0:T(8,128)S(1)} %copy-done.1, s32[2]{0:T(128)S(1)} %pad_add_fusion.place_ref, bf16[6,2048,512]{2,1,0:T(8,128)(2,1)} %tile_ref.15, ...), custom_call_target="tpu_custom_call" | custom-call | flops 402653184 | bytes 12582912 | tf_op jit(solution)/shard_map/forward1/pallas_call | solution.py:166
  97.4 3.4 %collective-permute-start.21 = (bf16[2,32,512]{2,1,0:T(8,128)(2,1)S(1)}, bf16[2,32,512]{2,1,0:T(8,128)(2,1)S(1)}, u32[]{:S(2)}, u32[]{:S(2)}) collective-permute-start(bf16[2,32,512]{2,1,0:T(8,128)(2,1)S(1)} %get-tuple-element.65), channel_id=1, source_target_pairs={{0,24},{4,28},{8,16},{12,20},{16,8},{20,12},{24,0},{28,4},{1,25},{... | collective-permute-start | bytes 196616 | tf_op jit(solution)/shard_map/ppermute | solution.py:191
  112.6 7.2 %backward2.1 = (f32[4,2,32,512]{3,2,1,0:T(8,128)S(1)}, bf16[4,2,32,512]{3,2,1,0:T(8,128)(2,1)S(1)}) custom-call(s32[6,5]{1,0:T(8,128)S(1)} %copy-done.1, s32[2]{0:T(128)S(1)} %pad_add_fusion.place_ref, bf16[6,2048,512]{2,1,0:T(8,128)(2,1)} %tile_ref.15, bf16[4,2,32,512]{3,2,1,0:T(8,128)(2,1)S(1)} %convert_element_type.220.refs_0_, ...), custom_call_target="tpu_custom_call" | custom-call | flops 402653184 | bytes 12582912 | tf_op jit(solution)/shard_map/backward2/pallas_call | solution.py:148
  119.9 2.7 %collective-permute-start.46 = (bf16[2,32,512]{2,1,0:T(8,128)(2,1)S(1)}, bf16[2,32,512]{2,1,0:T(8,128)(2,1)S(1)}, u32[]{:S(2)}, u32[]{:S(2)}) collective-permute-start(bf16[2,32,512]{2,1,0:T(8,128)(2,1)S(1)} %get-tuple-element.55.refs_8_.refs_16_), channel_id=1, source_target_pairs={{0,24},{4,28},{8,16},{12,20},{16,8},{20,12},{24,0},{28,4},{1,25},{... | collective-permute-start | bytes 196616 | tf_op jit(solution)/shard_map/ppermute | solution.py:142
  130.4 8.7 %forward2.1 = (f32[2,32,512]{2,1,0:T(8,128)S(1)}, bf16[2,32,512]{2,1,0:T(8,128)(2,1)S(1)}, bf16[2,32,512]{2,1,0:T(8,128)(2,1)S(1)}, bf16[2,32,512]{2,1,0:T(8,128)(2,1)S(1)}) custom-call(s32[6,5]{1,0:T(8,128)S(1)} %copy-done.1, s32[2]{0:T(128)S(1)} %pad_add_fusion.place_ref, bf16[6,2048,512]{2,1,0:T(8,128)(2,1)} %tile_ref.15, ...), custom_call_target="tpu_custom_call" | custom-call | flops 402653184 | bytes 12582912 | tf_op jit(solution)/shard_map/forward2/pallas_call | solution.py:166
  139.1 2.5 %collective-permute-start.48 = (bf16[2,32,512]{2,1,0:T(8,128)(2,1)S(1)}, bf16[2,32,512]{2,1,0:T(8,128)(2,1)S(1)}, u32[]{:S(2)}, u32[]{:S(2)}) collective-permute-start(bf16[2,32,512]{2,1,0:T(8,128)(2,1)S(1)} %get-tuple-element.44), channel_id=1, source_target_pairs={{0,3},{1,2},{2,1},{3,0},{4,7},{5,6},{6,5},{7,4},{8,11},{9,10},{10,... | collective-permute-start | bytes 196616 | tf_op jit(solution)/shard_map/ppermute | solution.py:195
  142.7 3.4 %collective-permute-start.38 = (bf16[2,32,512]{2,1,0:T(8,128)(2,1)S(1)}, bf16[2,32,512]{2,1,0:T(8,128)(2,1)S(1)}, u32[]{:S(2)}, u32[]{:S(2)}) collective-permute-start(bf16[2,32,512]{2,1,0:T(8,128)(2,1)S(1)} %get-tuple-element.62), channel_id=1, source_target_pairs={{0,24},{4,28},{8,16},{12,20},{16,8},{20,12},{24,0},{28,4},{1,25},{... | collective-permute-start | bytes 196616 | tf_op jit(solution)/shard_map/ppermute | solution.py:191
  151.5 2.5 %collective-permute-start.53 = (bf16[2,32,512]{2,1,0:T(8,128)(2,1)S(1)}, bf16[2,32,512]{2,1,0:T(8,128)(2,1)S(1)}, u32[]{:S(2)}, u32[]{:S(2)}) collective-permute-start(bf16[2,32,512]{2,1,0:T(8,128)(2,1)S(1)} %get-tuple-element.53.refs_12_.refs_24_), channel_id=1, source_target_pairs={{0,3},{1,2},{2,1},{3,0},{4,7},{5,6},{6,5},{7,4},{8,11},{9,10},{10,... | collective-permute-start | bytes 196616 | tf_op jit(solution)/shard_map/ppermute | solution.py:136
  158.8 7.2 %backward3.1 = (f32[4,2,32,512]{3,2,1,0:T(8,128)S(1)}, bf16[4,2,32,512]{3,2,1,0:T(8,128)(2,1)S(1)}) custom-call(s32[6,5]{1,0:T(8,128)S(1)} %copy-done.1, s32[2]{0:T(128)S(1)} %pad_add_fusion.place_ref, bf16[6,2048,512]{2,1,0:T(8,128)(2,1)} %tile_ref.15, bf16[4,2,32,512]{3,2,1,0:T(8,128)(2,1)S(1)} %convert_element_type.220.refs_0_, ...), custom_call_target="tpu_custom_call" | custom-call | flops 402653184 | bytes 12582912 | tf_op jit(solution)/shard_map/backward3/pallas_call | solution.py:148
  166.1 2.7 %collective-permute-start.63 = (bf16[2,32,512]{2,1,0:T(8,128)(2,1)S(1)}, bf16[2,32,512]{2,1,0:T(8,128)(2,1)S(1)}, u32[]{:S(2)}, u32[]{:S(2)}) collective-permute-start(bf16[2,32,512]{2,1,0:T(8,128)(2,1)S(1)} %get-tuple-element.53.refs_12_.refs_24_), channel_id=1, source_target_pairs={{0,24},{4,28},{8,16},{12,20},{16,8},{20,12},{24,0},{28,4},{1,25},{... | collective-permute-start | bytes 196616 | tf_op jit(solution)/shard_map/ppermute | solution.py:142
  176.6 8.7 %forward3.1 = (f32[2,32,512]{2,1,0:T(8,128)S(1)}, bf16[2,32,512]{2,1,0:T(8,128)(2,1)S(1)}, bf16[2,32,512]{2,1,0:T(8,128)(2,1)S(1)}, bf16[2,32,512]{2,1,0:T(8,128)(2,1)S(1)}) custom-call(s32[6,5]{1,0:T(8,128)S(1)} %copy-done.1, s32[2]{0:T(128)S(1)} %pad_add_fusion.place_ref, bf16[6,2048,512]{2,1,0:T(8,128)(2,1)} %tile_ref.15, ...), custom_call_target="tpu_custom_call" | custom-call | flops 402653184 | bytes 12582912 | tf_op jit(solution)/shard_map/forward3/pallas_call | solution.py:166
  188.9 3.4 %collective-permute-start.55 = (bf16[2,32,512]{2,1,0:T(8,128)(2,1)S(1)}, bf16[2,32,512]{2,1,0:T(8,128)(2,1)S(1)}, u32[]{:S(2)}, u32[]{:S(2)}) collective-permute-start(bf16[2,32,512]{2,1,0:T(8,128)(2,1)S(1)} %get-tuple-element.59), channel_id=1, source_target_pairs={{0,24},{4,28},{8,16},{12,20},{16,8},{20,12},{24,0},{28,4},{1,25},{... | collective-permute-start | bytes 196616 | tf_op jit(solution)/shard_map/ppermute | solution.py:191
  (139 shorter events, 76.7 us)
Async XLA Ops:
  1.1 12.4 %collective-permute-start.12 = (bf16[4,2,32,512]{3,2,1,0:T(8,128)(2,1)S(1)}, bf16[4,2,32,512]{3,2,1,0:T(8,128)(2,1)S(1)}, u32[]{:S(2)}, u32[]{:S(2)}) collective-permute-start(bf16[4,2,32,512]{3,2,1,0:T(8,128)(2,1)S(1)} %convert_element_type.220.refs_0_), channel_id=1, source_target_pairs={{0,24},{4,28},{8,16},{12,20},{16,8},{20,12},{24,0},{28,4},{1,25},{... | collective-permute-start | bytes 786440 | tf_op jit(solution)/shard_map/ppermute | solution.py:142
  6.2 22.3 %collective-permute-start.10 = (bf16[4,2,32,512]{3,2,1,0:T(8,128)(2,1)S(1)}, bf16[4,2,32,512]{3,2,1,0:T(8,128)(2,1)S(1)}, u32[]{:S(2)}, u32[]{:S(2)}) collective-permute-start(bf16[4,2,32,512]{3,2,1,0:T(8,128)(2,1)S(1)} %convert_element_type.220.refs_0_), channel_id=1, source_target_pairs={{0,16},{4,20},{8,24},{12,28},{16,0},{20,4},{24,8},{28,12},{1,17},{... | collective-permute-start | bytes 786440 | tf_op jit(solution)/shard_map/ppermute | solution.py:142
  6.2 22.3 %collective-permute-start.8 = (bf16[4,2,32,512]{3,2,1,0:T(8,128)(2,1)S(1)}, bf16[4,2,32,512]{3,2,1,0:T(8,128)(2,1)S(1)}, u32[]{:S(2)}, u32[]{:S(2)}) collective-permute-start(bf16[4,2,32,512]{3,2,1,0:T(8,128)(2,1)S(1)} %convert_element_type.220.refs_0_), channel_id=1, source_target_pairs={{0,8},{4,12},{8,0},{12,4},{16,24},{20,28},{24,16},{28,20},{1,9},{5... | collective-permute-start | bytes 786440 | tf_op jit(solution)/shard_map/ppermute | solution.py:142
  6.8 22.2 %collective-permute-start.2 = (bf16[4,2,32,512]{3,2,1,0:T(8,128)(2,1)S(1)}, bf16[4,2,32,512]{3,2,1,0:T(8,128)(2,1)S(1)}, u32[]{:S(2)}, u32[]{:S(2)}) collective-permute-start(bf16[4,2,32,512]{3,2,1,0:T(8,128)(2,1)S(1)} %convert_element_type.220.refs_0_), channel_id=1, source_target_pairs={{0,3},{1,2},{2,1},{3,0},{4,7},{5,6},{6,5},{7,4},{8,11},{9,10},{10,... | collective-permute-start | bytes 786440 | tf_op jit(solution)/shard_map/ppermute | solution.py:136
  9.4 19.7 %collective-permute-start.1 = (bf16[4,2,32,512]{3,2,1,0:T(8,128)(2,1)S(1)}, bf16[4,2,32,512]{3,2,1,0:T(8,128)(2,1)S(1)}, u32[]{:S(2)}, u32[]{:S(2)}) collective-permute-start(bf16[4,2,32,512]{3,2,1,0:T(8,128)(2,1)S(1)} %convert_element_type.220.refs_0_), channel_id=1, source_target_pairs={{0,2},{1,3},{2,0},{3,1},{4,6},{5,7},{6,4},{7,5},{8,10},{9,11},{10,... | collective-permute-start | bytes 786440 | tf_op jit(solution)/shard_map/ppermute | solution.py:136
  13.5 16.1 %collective-permute-start = (bf16[4,2,32,512]{3,2,1,0:T(8,128)(2,1)S(1)}, bf16[4,2,32,512]{3,2,1,0:T(8,128)(2,1)S(1)}, u32[]{:S(2)}, u32[]{:S(2)}) collective-permute-start(bf16[4,2,32,512]{3,2,1,0:T(8,128)(2,1)S(1)} %convert_element_type.220.refs_0_), channel_id=1, source_target_pairs={{0,1},{1,0},{2,3},{3,2},{4,5},{5,4},{6,7},{7,6},{8,9},{9,8},{10,11... | collective-permute-start | bytes 786440 | tf_op jit(solution)/shard_map/ppermute | solution.py:136
  28.5 9.7 %collective-permute-start.7 = (bf16[4,2,32,512]{3,2,1,0:T(8,128)(2,1)S(1)}, bf16[4,2,32,512]{3,2,1,0:T(8,128)(2,1)S(1)}, u32[]{:S(2)}, u32[]{:S(2)}) collective-permute-start(bf16[4,2,32,512]{3,2,1,0:T(8,128)(2,1)S(1)} %convert_element_type.220.refs_0_), channel_id=1, source_target_pairs={{0,4},{4,0},{8,12},{12,8},{16,20},{20,16},{24,28},{28,24},{1,5},{5... | collective-permute-start | bytes 786440 | tf_op jit(solution)/shard_map/ppermute | solution.py:144
  28.5 9.7 %collective-permute-start.13 = (bf16[4,2,32,512]{3,2,1,0:T(8,128)(2,1)S(1)}, bf16[4,2,32,512]{3,2,1,0:T(8,128)(2,1)S(1)}, u32[]{:S(2)}, u32[]{:S(2)}) collective-permute-start(bf16[4,2,32,512]{3,2,1,0:T(8,128)(2,1)S(1)} %collective-permute-done.12.refs_6_), channel_id=1, source_target_pairs={{0,4},{4,0},{8,12},{12,8},{16,20},{20,16},{24,28},{28,24},{1,5},{5... | collective-permute-start | bytes 786440 | tf_op jit(solution)/shard_map/ppermute | solution.py:144
  29.0 9.2 %collective-permute-start.11 = (bf16[4,2,32,512]{3,2,1,0:T(8,128)(2,1)S(1)}, bf16[4,2,32,512]{3,2,1,0:T(8,128)(2,1)S(1)}, u32[]{:S(2)}, u32[]{:S(2)}) collective-permute-start(bf16[4,2,32,512]{3,2,1,0:T(8,128)(2,1)S(1)} %collective-permute-done.10.refs_4_), channel_id=1, source_target_pairs={{0,4},{4,0},{8,12},{12,8},{16,20},{20,16},{24,28},{28,24},{1,5},{5... | collective-permute-start | bytes 786440 | tf_op jit(solution)/shard_map/ppermute | solution.py:144
  29.1 9.1 %collective-permute-start.9 = (bf16[4,2,32,512]{3,2,1,0:T(8,128)(2,1)S(1)}, bf16[4,2,32,512]{3,2,1,0:T(8,128)(2,1)S(1)}, u32[]{:S(2)}, u32[]{:S(2)}) collective-permute-start(bf16[4,2,32,512]{3,2,1,0:T(8,128)(2,1)S(1)} %collective-permute-done.8.refs_2_), channel_id=1, source_target_pairs={{0,4},{4,0},{8,12},{12,8},{16,20},{20,16},{24,28},{28,24},{1,5},{5... | collective-permute-start | bytes 786440 | tf_op jit(solution)/shard_map/ppermute | solution.py:144
  38.1 12.3 %collective-permute-start.3 = (bf16[4,2,32,512]{3,2,1,0:T(8,128)(2,1)S(1)}, bf16[4,2,32,512]{3,2,1,0:T(8,128)(2,1)S(1)}, u32[]{:S(2)}, u32[]{:S(2)}) collective-permute-start(bf16[4,2,32,512]{3,2,1,0:T(8,128)(2,1)S(1)} %get-tuple-element.30), channel_id=1, source_target_pairs={{0,4},{4,0},{8,12},{12,8},{16,20},{20,16},{24,28},{28,24},{1,5},{5... | collective-permute-start | bytes 786440 | tf_op jit(solution)/shard_map/ppermute | solution.py:187
  46.9 7.4 %collective-permute-start.14 = (bf16[2,32,512]{2,1,0:T(8,128)(2,1)S(1)}, bf16[2,32,512]{2,1,0:T(8,128)(2,1)S(1)}, u32[]{:S(2)}, u32[]{:S(2)}) collective-permute-start(bf16[2,32,512]{2,1,0:T(8,128)(2,1)S(1)} %get-tuple-element.32), channel_id=1, source_target_pairs={{0,3},{1,2},{2,1},{3,0},{4,7},{5,6},{6,5},{7,4},{8,11},{9,10},{10,... | collective-permute-start | bytes 196616 | tf_op jit(solution)/shard_map/ppermute | solution.py:195
  74.3 23.0 %collective-permute-start.20 = (bf16[4,2,32,512]{3,2,1,0:T(8,128)(2,1)S(1)}, bf16[4,2,32,512]{3,2,1,0:T(8,128)(2,1)S(1)}, u32[]{:S(2)}, u32[]{:S(2)}) collective-permute-start(bf16[4,2,32,512]{3,2,1,0:T(8,128)(2,1)S(1)} %get-tuple-element.36), channel_id=1, source_target_pairs={{0,4},{4,0},{8,12},{12,8},{16,20},{20,16},{24,28},{28,24},{1,5},{5... | collective-permute-start | bytes 786440 | tf_op jit(solution)/shard_map/ppermute | solution.py:187
  74.4 6.8 %collective-permute-start.29 = (bf16[2,32,512]{2,1,0:T(8,128)(2,1)S(1)}, bf16[2,32,512]{2,1,0:T(8,128)(2,1)S(1)}, u32[]{:S(2)}, u32[]{:S(2)}) collective-permute-start(bf16[2,32,512]{2,1,0:T(8,128)(2,1)S(1)} %get-tuple-element.57.refs_4_.refs_8_), channel_id=1, source_target_pairs={{0,24},{4,28},{8,16},{12,20},{16,8},{20,12},{24,0},{28,4},{1,25},{... | collective-permute-start | bytes 196616 | tf_op jit(solution)/shard_map/ppermute | solution.py:142
  93.8 7.0 %collective-permute-start.31 = (bf16[2,32,512]{2,1,0:T(8,128)(2,1)S(1)}, bf16[2,32,512]{2,1,0:T(8,128)(2,1)S(1)}, u32[]{:S(2)}, u32[]{:S(2)}) collective-permute-start(bf16[2,32,512]{2,1,0:T(8,128)(2,1)S(1)} %get-tuple-element.38), channel_id=1, source_target_pairs={{0,3},{1,2},{2,1},{3,0},{4,7},{5,6},{6,5},{7,4},{8,11},{9,10},{10,... | collective-permute-start | bytes 196616 | tf_op jit(solution)/shard_map/ppermute | solution.py:195
  95.3 6.5 %collective-permute-start.32 = (bf16[2,32,512]{2,1,0:T(8,128)(2,1)S(1)}, bf16[2,32,512]{2,1,0:T(8,128)(2,1)S(1)}, u32[]{:S(2)}, u32[]{:S(2)}) collective-permute-start(bf16[2,32,512]{2,1,0:T(8,128)(2,1)S(1)} %get-tuple-element.39), channel_id=1, source_target_pairs={{0,2},{1,3},{2,0},{3,1},{4,6},{5,7},{6,4},{7,5},{8,10},{9,11},{10,... | collective-permute-start | bytes 196616 | tf_op jit(solution)/shard_map/ppermute | solution.py:195
  119.8 22.8 %collective-permute-start.37 = (bf16[4,2,32,512]{3,2,1,0:T(8,128)(2,1)S(1)}, bf16[4,2,32,512]{3,2,1,0:T(8,128)(2,1)S(1)}, u32[]{:S(2)}, u32[]{:S(2)}) collective-permute-start(bf16[4,2,32,512]{3,2,1,0:T(8,128)(2,1)S(1)} %get-tuple-element.42), channel_id=1, source_target_pairs={{0,4},{4,0},{8,12},{12,8},{16,20},{20,16},{24,28},{28,24},{1,5},{5... | collective-permute-start | bytes 786440 | tf_op jit(solution)/shard_map/ppermute | solution.py:187
  119.9 6.8 %collective-permute-start.46 = (bf16[2,32,512]{2,1,0:T(8,128)(2,1)S(1)}, bf16[2,32,512]{2,1,0:T(8,128)(2,1)S(1)}, u32[]{:S(2)}, u32[]{:S(2)}) collective-permute-start(bf16[2,32,512]{2,1,0:T(8,128)(2,1)S(1)} %get-tuple-element.55.refs_8_.refs_16_), channel_id=1, source_target_pairs={{0,24},{4,28},{8,16},{12,20},{16,8},{20,12},{24,0},{28,4},{1,25},{... | collective-permute-start | bytes 196616 | tf_op jit(solution)/shard_map/ppermute | solution.py:142
  122.6 6.5 %collective-permute-start.42 = (bf16[2,32,512]{2,1,0:T(8,128)(2,1)S(1)}, bf16[2,32,512]{2,1,0:T(8,128)(2,1)S(1)}, u32[]{:S(2)}, u32[]{:S(2)}) collective-permute-start(bf16[2,32,512]{2,1,0:T(8,128)(2,1)S(1)} %get-tuple-element.55.refs_8_.refs_16_), channel_id=1, source_target_pairs={{0,8},{4,12},{8,0},{12,4},{16,24},{20,28},{24,16},{28,20},{1,9},{5... | collective-permute-start | bytes 196616 | tf_op jit(solution)/shard_map/ppermute | solution.py:142
  139.1 7.0 %collective-permute-start.48 = (bf16[2,32,512]{2,1,0:T(8,128)(2,1)S(1)}, bf16[2,32,512]{2,1,0:T(8,128)(2,1)S(1)}, u32[]{:S(2)}, u32[]{:S(2)}) collective-permute-start(bf16[2,32,512]{2,1,0:T(8,128)(2,1)S(1)} %get-tuple-element.44), channel_id=1, source_target_pairs={{0,3},{1,2},{2,1},{3,0},{4,7},{5,6},{6,5},{7,4},{8,11},{9,10},{10,... | collective-permute-start | bytes 196616 | tf_op jit(solution)/shard_map/ppermute | solution.py:195
  166.0 22.8 %collective-permute-start.54 = (bf16[4,2,32,512]{3,2,1,0:T(8,128)(2,1)S(1)}, bf16[4,2,32,512]{3,2,1,0:T(8,128)(2,1)S(1)}, u32[]{:S(2)}, u32[]{:S(2)}) collective-permute-start(bf16[4,2,32,512]{3,2,1,0:T(8,128)(2,1)S(1)} %get-tuple-element.48), channel_id=1, source_target_pairs={{0,4},{4,0},{8,12},{12,8},{16,20},{20,16},{24,28},{28,24},{1,5},{5... | collective-permute-start | bytes 786440 | tf_op jit(solution)/shard_map/ppermute | solution.py:187
  166.1 6.8 %collective-permute-start.63 = (bf16[2,32,512]{2,1,0:T(8,128)(2,1)S(1)}, bf16[2,32,512]{2,1,0:T(8,128)(2,1)S(1)}, u32[]{:S(2)}, u32[]{:S(2)}) collective-permute-start(bf16[2,32,512]{2,1,0:T(8,128)(2,1)S(1)} %get-tuple-element.53.refs_12_.refs_24_), channel_id=1, source_target_pairs={{0,24},{4,28},{8,16},{12,20},{16,8},{20,12},{24,0},{28,4},{1,25},{... | collective-permute-start | bytes 196616 | tf_op jit(solution)/shard_map/ppermute | solution.py:142
  185.3 7.0 %collective-permute-start.65 = (bf16[2,32,512]{2,1,0:T(8,128)(2,1)S(1)}, bf16[2,32,512]{2,1,0:T(8,128)(2,1)S(1)}, u32[]{:S(2)}, u32[]{:S(2)}) collective-permute-start(bf16[2,32,512]{2,1,0:T(8,128)(2,1)S(1)} %get-tuple-element.50), channel_id=1, source_target_pairs={{0,3},{1,2},{2,1},{3,0},{4,7},{5,6},{6,5},{7,4},{8,11},{9,10},{10,... | collective-permute-start | bytes 196616 | tf_op jit(solution)/shard_map/ppermute | solution.py:195
  186.9 6.5 %collective-permute-start.66 = (bf16[2,32,512]{2,1,0:T(8,128)(2,1)S(1)}, bf16[2,32,512]{2,1,0:T(8,128)(2,1)S(1)}, u32[]{:S(2)}, u32[]{:S(2)}) collective-permute-start(bf16[2,32,512]{2,1,0:T(8,128)(2,1)S(1)} %get-tuple-element.51), channel_id=1, source_target_pairs={{0,2},{1,3},{2,0},{3,1},{4,6},{5,7},{6,4},{7,5},{8,10},{9,11},{10,... | collective-permute-start | bytes 196616 | tf_op jit(solution)/shard_map/ppermute | solution.py:195
  (48 other events, 258.9 us)
where the time goes:
time: 200 us; the launch traced here: 199 us
  starting transfers between devices  69.4 us (35%)
  waiting for transfers between devices  61.6 us (31%)
  Pallas kernels  59.6 us (30%)
  local copies, waits for them, and re-layouts  5.27 us (3%)
  other arithmetic  2.53 us (1%)
    pallas_call x4, Pallas kernels, forward(): pl.pallas_call(functools.partial(forward_kernel, step, groups, cols), out...  34.7 us
    ppermute x12, waiting for transfers between devices, spread_pairs(): got[CORES * k] = lax.ppermute(x, 'pairs', swapped(groups, CORES * k))  31.1 us
    pallas_call x4, Pallas kernels, backward(): pl.pallas_call(functools.partial(backward_kernel, step, groups, cols), ou...  24.9 us
    ppermute x12, starting transfers between devices, spread_pairs(): got[CORES * k] = lax.ppermute(x, 'pairs', swapped(groups, CORES * k))  19.1 us
    ppermute x12, starting transfers between devices, shards(): field += lax.ppermute(sent, 'pairs', swapped(groups, CORES * k)).astype(F32)  17.8 us
    ppermute x12, waiting for transfers between devices, shards(): field += lax.ppermute(sent, 'pairs', swapped(groups, CORES * k)).astype(F32)  17.6 us
    ppermute x12, starting transfers between devices, spread_cols(): got[k] = lax.ppermute(x, 'cols', swapped(cols, k))  15.5 us
    ppermute x12, starting transfers between devices, shards(): field += lax.ppermute(parts[k], 'cols', swapped(cols, k)).astype(F32)  14.2 us
  transfers between devices with their start and end apart: 68, of which 36 were waited for; matrix products, arithmetic and copies ran while one was open for 0% of the time, Pallas kernels for 19%

commit v1 on v0

v1 whole, which is shorter than its diff:
```python
import functools

import jax
import jax.numpy as jnp
from jax import lax
from jax.experimental import pallas as pl
from jax.experimental.pallas import tpu as pltpu
from jax.sharding import PartitionSpec as P

STEPS = 4
CORES = 2
F32 = jnp.float32
BF16 = jnp.bfloat16


def swapped(n, bits):
    return [(i, i ^ bits) for i in range(n)]


def far_first(n):
    return sorted(range(1, n), key=lambda k: -bin(k).count("1") * n - k)


def pick(step, delays, slot_delay, slot_cluster, old, new, put):
    for delay in range(delays):

        @pl.when(slot_delay == delay)
        def _(delay=delay):
            if delay < step:
                put([ref[slot_cluster] for ref in new[step - 1 - delay]])
            else:
                put([ref[delay - step, slot_cluster] for ref in old])


def turn_kernel(tile_ref, turned_ref):
    slots, rows, width = tile_ref.shape
    part = min(rows, 256)
    for s in range(slots):

        @pl.loop(0, rows // part)
        def _(i, s=s):
            start = pl.multiple_of(i * part, part)
            turned_ref[s, :, pl.ds(start, part)] = tile_ref[s, pl.ds(start, part), :].T


def backward_kernel(step, groups, cols, pairs_ref, place_ref, tile_ref, *refs):
    old = refs[:cols]
    new = [refs[cols * (1 + j) : cols * (2 + j)] for j in range(step)]
    same_ref, other_ref, rows_ref, sum_ref = refs[-4:]
    slots, _, width = tile_ref.shape
    me, col = place_ref[0], place_ref[1]
    sum_ref[...] = jnp.zeros_like(sum_ref)
    for s in range(slots):

        def put(blocks, s=s):
            for k in range(cols):
                start = pl.multiple_of((col ^ k) * width, width)
                rows_ref[s, :, pl.ds(start, width)] = blocks[k]

        pick(step, old[0].shape[0], pairs_ref[s, 3], pairs_ref[s, 0], old, new, put)
    for s in range(slots):

        @pl.when(pairs_ref[s, 4] == 1)
        def _(s=s):
            piece = pairs_ref[s, 1] ^ me
            sum_ref[piece, pairs_ref[s, 2]] += jnp.dot(
                rows_ref[s], tile_ref[s], preferred_element_type=F32
            )

    for k in range(groups // CORES):
        same_ref[k] = sum_ref[CORES * k]
        other_ref[k] = sum_ref[CORES * k + 1].astype(other_ref.dtype)


def forward_kernel(step, groups, cols, pairs_ref, place_ref, turned_ref, *refs):
    old = refs[:groups]
    new = [refs[groups * (1 + j) : groups * (2 + j)] for j in range(step)]
    outs, near_ref, sum_ref = refs[-2 - cols : -2], refs[-2], refs[-1]
    slots, width, _ = turned_ref.shape
    me, col = place_ref[0], place_ref[1]
    sum_ref[...] = jnp.zeros_like(sum_ref)
    for s in range(slots):
        piece = pairs_ref[s, 1] ^ me
        for p in range(groups):

            @pl.when(piece == p)
            def _(s=s, p=p):
                def put(blocks):
                    near_ref[s] = blocks[0]

                pick(
                    step,
                    old[0].shape[0],
                    pairs_ref[s, 3],
                    pairs_ref[s, 2],
                    [old[p]],
                    [[n[p]] for n in new],
                    put,
                )

    for s in range(slots):

        @pl.when(pairs_ref[s, 4] == 1)
        def _(s=s):
            sum_ref[pairs_ref[s, 0]] += jnp.dot(
                near_ref[s], turned_ref[s], preferred_element_type=F32
            )

    for k in range(cols):
        start = pl.multiple_of((col ^ k) * width, width)
        outs[k][...] = sum_ref[:, :, pl.ds(start, width)].astype(outs[k].dtype)


def shards(pair_list, near_tile_block, history, excitation, diagonal):
    groups = lax.axis_size("pairs")
    cols = lax.axis_size("cols")
    planes = groups // CORES
    delays, clusters, excite, width = history.shape
    slots = pair_list.shape[0]
    block = (clusters, excite, width)
    place = jnp.stack([lax.axis_index("pairs"), lax.axis_index("cols")]).astype(jnp.int32)

    smem = pl.BlockSpec(memory_space=pltpu.SMEM)
    vmem = pl.BlockSpec(memory_space=pltpu.VMEM)
    anywhere = pl.BlockSpec(memory_space=pl.ANY)
    rows = near_tile_block.shape[1]
    cost = pl.CostEstimate(
        flops=2 * near_tile_block.size * excite,
        bytes_accessed=2 * near_tile_block.size,
        transcendentals=0,
    )
    limit = pltpu.CompilerParams(vmem_limit_bytes=16 * 2**20)
    turned = pl.pallas_call(
        turn_kernel,
        out_shape=pltpu.VMEM((slots, width, rows), BF16),
        in_specs=[vmem],
        out_specs=vmem,
        cost_estimate=cost,
        compiler_params=limit,
        name="turn",
    )(near_tile_block)

    def spread_cols(x):
        got = {0: x}
        for k in far_first(cols):
            got[k] = lax.ppermute(x, "cols", swapped(cols, k))
        return [got[k] for k in range(cols)]

    def spread_pairs(x, before=None):
        got = {0: x}
        for k in far_first(planes):
            got[CORES * k] = lax.ppermute(x, "pairs", swapped(groups, CORES * k))
        if before is not None:
            got, before = lax.optimization_barrier((got, before))
        for k in range(planes):
            got[CORES * k + 1] = lax.ppermute(got[CORES * k], "pairs", swapped(groups, 1))
        got = [got[p] for p in range(groups)]
        return got if before is None else (got, before)

    def backward(step, old, new, after):
        return pl.pallas_call(
            functools.partial(backward_kernel, step, groups, cols),
            out_shape=(
                jax.ShapeDtypeStruct((planes, *block), F32),
                jax.ShapeDtypeStruct((planes, *block), BF16),
            ),
            in_specs=[smem, smem]
            + [vmem] * (1 + cols * (1 + step))
            + [anywhere] * len(after),
            out_specs=(vmem, vmem),
            scratch_shapes=[
                pltpu.VMEM((slots, excite, rows), BF16),
                pltpu.VMEM((groups, *block), F32),
            ],
            cost_estimate=cost,
            compiler_params=limit,
            name=f"backward{step}",
        )(pair_list, place, near_tile_block, *old, *[x for n in new for x in n], *after)

    def forward(step, old, new, after):
        return pl.pallas_call(
            functools.partial(forward_kernel, step, groups, cols),
            out_shape=[jax.ShapeDtypeStruct(block, F32)]
            + [jax.ShapeDtypeStruct(block, BF16)] * (cols - 1),
            in_specs=[smem, smem]
            + [vmem] * (1 + groups * (1 + step))
            + [anywhere] * len(after),
            out_specs=[vmem] * cols,
            scratch_shapes=[
                pltpu.VMEM((slots, excite, width), BF16),
                pltpu.VMEM((clusters, excite, rows), F32),
            ],
            cost_estimate=cost,
            compiler_params=limit,
            name=f"forward{step}",
        )(pair_list, place, turned, *old, *[x for n in new for x in n], *after)

    rounded = history.astype(BF16)
    old_rows = spread_cols(rounded)
    old_near, turned = spread_pairs(rounded, turned)
    new_rows, new_near, results = [], [], []
    for step in range(STEPS):
        same, other = backward(step, old_rows, new_rows, new_near[-1][::CORES] if step else [])
        mate = lax.ppermute(other, "pairs", swapped(groups, 1))
        field = same[0] + mate[0].astype(F32)
        for k in far_first(planes):
            sent = (same[k] + mate[k].astype(F32)).astype(BF16)
            field += lax.ppermute(sent, "pairs", swapped(groups, CORES * k)).astype(F32)
        parts = forward(step, old_near, new_near, [same])
        field += parts[0]
        for k in far_first(cols):
            field += lax.ppermute(parts[k], "cols", swapped(cols, k)).astype(F32)
        fresh = (excitation[step] - field) / diagonal[:, None, :]
        results.append(fresh)
        if step + 1 < STEPS:
            newest = fresh.astype(BF16)
            new_rows.append(spread_cols(newest))
            new_near.append(spread_pairs(newest))
    return jnp.stack(results)


def solution(mesh):
    placed = (
        P("pairs", None),
        P("pairs", None, "cols"),
        P(None, "pairs", None, "cols"),
        P(None, "pairs", None, "cols"),
        P("pairs", "cols"),
    )
    return jax.shard_map(
        shards,
        mesh=mesh,
        in_specs=placed,
        out_specs=P(None, "pairs", None, "cols"),
        check_vma=False,
    )
```

time: 200 us -> 151 us (0.76)
  Pallas kernels: 59.6 us -> 25.4 us
  waiting for transfers between devices: 61.6 us -> 40.9 us
  starting transfers between devices: 69.4 us -> 76.2 us
    pallas_call x4, Pallas kernels: 34.7 us -> 10 us  [forward(): pl.pallas_call(functools.partial(forward_kernel, step, groups, cols), out...]
    pallas_call x4, Pallas kernels: 24.9 us -> 9.31 us  [backward(): pl.pallas_call(functools.partial(backward_kernel, step, groups, cols), ou...]
    ppermute x12, waiting for transfers between devices: 31.1 us -> 18.9 us  [spread_pairs(): got[CORES * k] = lax.ppermute(x, 'pairs', swapped(groups, CORES * k))]
    ppermute x12, waiting for transfers between devices: 10.2 us -> 0.03 us  [spread_cols(): got[k] = lax.ppermute(x, 'cols', swapped(cols, k))]
    pallas_call x0 -> x1, Pallas kernels: none -> 6.08 us  [shards(): pl.pallas_call(turn_kernel, out_shape=pltpu.VMEM((slots, width, rows), BF...]
    ppermute x12, starting transfers between devices: 17.8 us -> 21.5 us  [shards(): field += lax.ppermute(sent, 'pairs', swapped(groups, CORES * k)).astype(F32)]
    unnamed x8 -> x14, local copies, waits for them, and re-layouts: 5.27 us -> 4.6 us
  transfers between devices with their start and end apart: 68 -> 68, of which waited for: 36 -> 27; matrix products, arithmetic and copies ran while one was open for 0% -> 0% of each run, Pallas kernels for 19% -> 12%
where the time goes in v1:
time: 151 us; the launch traced here: 150 us
  starting transfers between devices  76.2 us (50%)
  waiting for transfers between devices  40.9 us (27%)
  Pallas kernels  25.4 us (17%)
  local copies, waits for them, and re-layouts  4.6 us (3%)
  other arithmetic  2.54 us (2%)
    ppermute x12, starting transfers between devices, shards(): field += lax.ppermute(sent, 'pairs', swapped(groups, CORES * k)).astype(F32)  21.5 us
    ppermute x12, waiting for transfers between devices, spread_pairs(): got[CORES * k] = lax.ppermute(x, 'pairs', swapped(groups, CORES * k))  18.9 us
    ppermute x12, starting transfers between devices, spread_pairs(): got[CORES * k] = lax.ppermute(x, 'pairs', swapped(groups, CORES * k))  18.8 us
    ppermute x12, waiting for transfers between devices, shards(): field += lax.ppermute(sent, 'pairs', swapped(groups, CORES * k)).astype(F32)  18.4 us
    ppermute x12, starting transfers between devices, spread_cols(): got[k] = lax.ppermute(x, 'cols', swapped(cols, k))  16.5 us
    ppermute x12, starting transfers between devices, shards(): field += lax.ppermute(parts[k], 'cols', swapped(cols, k)).astype(F32)  14.2 us
    pallas_call x4, Pallas kernels, forward(): pl.pallas_call(functools.partial(forward_kernel, step, groups, cols), out...  10 us
    pallas_call x4, Pallas kernels, backward(): pl.pallas_call(functools.partial(backward_kernel, step, groups, cols), ou...  9.31 us
  transfers between devices with their start and end apart: 68, of which 27 were waited for; matrix products, arithmetic and copies ran while one was open for 0% of the time, Pallas kernels for 12%

profile of v1, /device:TPU:0, one launch (start us, length us, event | category | flops | bytes accessed | tf_op | source)
XLA Modules:
  0.0 149.9 jit_solution(11790548008519068338)
XLA Ops:
  1.1 3.1 %collective-permute-start.7 = (bf16[4,2,32,512]{3,2,1,0:T(8,128)(2,1)S(1)}, bf16[4,2,32,512]{3,2,1,0:T(8,128)(2,1)S(1)}, u32[]{:S(2)}, u32[]{:S(2)}) collective-permute-start(bf16[4,2,32,512]{3,2,1,0:T(8,128)(2,1)S(1)} %convert_element_type.220.refs_0_), channel_id=1, source_target_pairs={{0,8},{4,12},{8,0},{12,4},{16,24},{20,28},{24,16},{28,20},{1,9},{5... | collective-permute-start | bytes 786440 | tf_op jit(solution)/shard_map/ppermute | solution.py:152
  4.2 2.6 %collective-permute-start.8 = (bf16[4,2,32,512]{3,2,1,0:T(8,128)(2,1)S(1)}, bf16[4,2,32,512]{3,2,1,0:T(8,128)(2,1)S(1)}, u32[]{:S(2)}, u32[]{:S(2)}) collective-permute-start(bf16[4,2,32,512]{3,2,1,0:T(8,128)(2,1)S(1)} %convert_element_type.220.refs_0_), channel_id=1, source_target_pairs={{0,16},{4,20},{8,24},{12,28},{16,0},{20,4},{24,8},{28,12},{1,17},{... | collective-permute-start | bytes 786440 | tf_op jit(solution)/shard_map/ppermute | solution.py:152
  10.0 5.3 %collective-permute-done.7.refs_2_ = bf16[4,2,32,512]{3,2,1,0:T(8,128)(2,1)S(1)} collective-permute-done((bf16[4,2,32,512]{3,2,1,0:T(8,128)(2,1)S(1)}, bf16[4,2,32,512]{3,2,1,0:T(8,128)(2,1)S(1)}, u32[]{:S(2)}, u32[]{:S(2)}) %collective-permute-start.7) | collective-permute-done | bytes 262176 | tf_op jit(solution)/shard_map/ppermute | solution.py:152
  15.3 2.6 %collective-permute-start.2 = (bf16[4,2,32,512]{3,2,1,0:T(8,128)(2,1)S(1)}, bf16[4,2,32,512]{3,2,1,0:T(8,128)(2,1)S(1)}, u32[]{:S(2)}, u32[]{:S(2)}) collective-permute-start(bf16[4,2,32,512]{3,2,1,0:T(8,128)(2,1)S(1)} %convert_element_type.220.refs_0_), channel_id=1, source_target_pairs={{0,3},{1,2},{2,1},{3,0},{4,7},{5,6},{6,5},{7,4},{8,11},{9,10},{10,... | collective-permute-start | bytes 786440 | tf_op jit(solution)/shard_map/ppermute | solution.py:146
  17.9 4.6 %copy-done = bf16[6,2048,512]{2,1,0:T(8,128)(2,1)S(1)} copy-done((bf16[6,2048,512]{2,1,0:T(8,128)(2,1)S(1)}, bf16[6,2048,512]{2,1,0:T(8,128)(2,1)}, u32[]{:S(2)}) %copy-start) | copy-done | bytes 12582936
  22.5 6.1 %turn.1.turned_ref = bf16[6,512,2048]{2,1,0:T(8,128)(2,1)S(1)} custom-call(bf16[6,2048,512]{2,1,0:T(8,128)(2,1)S(1)} %copy-done), custom_call_target="tpu_custom_call" | custom-call | flops 402653184 | bytes 12582912 | tf_op jit(solution)/shard_map/turn/pallas_call | solution.py:133
  32.8 2.5 %forward0.1 = (f32[2,32,512]{2,1,0:T(8,128)S(1)}, bf16[2,32,512]{2,1,0:T(8,128)(2,1)S(1)}, bf16[2,32,512]{2,1,0:T(8,128)(2,1)S(1)}, bf16[2,32,512]{2,1,0:T(8,128)(2,1)S(1)}) custom-call(s32[6,5]{1,0:T(8,128)S(1)} %copy-done.1, s32[2]{0:T(128)S(1)} %pad_add_fusion.place_ref, bf16[6,512,2048]{2,1,0:T(8,128)(2,1)S(1)} %turn.1.turned_ref, ...), custom_call_target="tpu_custom_call" | custom-call | flops 402653184 | bytes 12582912 | tf_op jit(solution)/shard_map/forward0/pallas_call | solution.py:181
  38.9 5.4 %collective-permute-start.4 = (bf16[2,32,512]{2,1,0:T(8,128)(2,1)S(1)}, bf16[2,32,512]{2,1,0:T(8,128)(2,1)S(1)}, u32[]{:S(2)}, u32[]{:S(2)}) collective-permute-start(bf16[2,32,512]{2,1,0:T(8,128)(2,1)S(1)} %get-tuple-element.78), channel_id=1, source_target_pairs={{0,24},{4,28},{8,16},{12,20},{16,8},{20,12},{24,0},{28,4},{1,25},{... | collective-permute-start | bytes 196616 | tf_op jit(solution)/shard_map/ppermute | solution.py:208
  47.0 2.7 %collective-permute-done.5 = bf16[2,32,512]{2,1,0:T(8,128)(2,1)S(1)} collective-permute-done((bf16[2,32,512]{2,1,0:T(8,128)(2,1)S(1)}, bf16[2,32,512]{2,1,0:T(8,128)(2,1)S(1)}, u32[]{:S(2)}, u32[]{:S(2)}) %collective-permute-start.5) | collective-permute-done | bytes 65568 | tf_op jit(solution)/shard_map/ppermute | solution.py:208
  53.7 2.7 %collective-permute-start.21 = (bf16[2,32,512]{2,1,0:T(8,128)(2,1)S(1)}, bf16[2,32,512]{2,1,0:T(8,128)(2,1)S(1)}, u32[]{:S(2)}, u32[]{:S(2)}) collective-permute-start(bf16[2,32,512]{2,1,0:T(8,128)(2,1)S(1)} %get-tuple-element.67.refs_4_.refs_8_), channel_id=1, source_target_pairs={{0,16},{4,20},{8,24},{12,28},{16,0},{20,4},{24,8},{28,12},{1,17},{... | collective-permute-start | bytes 196616 | tf_op jit(solution)/shard_map/ppermute | solution.py:152
  59.5 3.0 %collective-permute-done.22.refs_11_.refs_14_ = bf16[2,32,512]{2,1,0:T(8,128)(2,1)S(1)} collective-permute-done((bf16[2,32,512]{2,1,0:T(8,128)(2,1)S(1)}, bf16[2,32,512]{2,1,0:T(8,128)(2,1)S(1)}, u32[]{:S(2)}, u32[]{:S(2)}) %collective-permute-start.22) | collective-permute-done | bytes 65568 | tf_op jit(solution)/shard_map/ppermute | solution.py:152
  67.2 2.6 %forward1.1 = (f32[2,32,512]{2,1,0:T(8,128)S(1)}, bf16[2,32,512]{2,1,0:T(8,128)(2,1)S(1)}, bf16[2,32,512]{2,1,0:T(8,128)(2,1)S(1)}, bf16[2,32,512]{2,1,0:T(8,128)(2,1)S(1)}) custom-call(s32[6,5]{1,0:T(8,128)S(1)} %copy-done.1, s32[2]{0:T(128)S(1)} %pad_add_fusion.place_ref, bf16[6,512,2048]{2,1,0:T(8,128)(2,1)S(1)} %turn.1.turned_ref, ...), custom_call_target="tpu_custom_call" | custom-call | flops 402653184 | bytes 12582912 | tf_op jit(solution)/shard_map/forward1/pallas_call | solution.py:181
  73.4 4.3 %collective-permute-start.24 = (bf16[2,32,512]{2,1,0:T(8,128)(2,1)S(1)}, bf16[2,32,512]{2,1,0:T(8,128)(2,1)S(1)}, u32[]{:S(2)}, u32[]{:S(2)}) collective-permute-start(bf16[2,32,512]{2,1,0:T(8,128)(2,1)S(1)} %get-tuple-element.75), channel_id=1, source_target_pairs={{0,24},{4,28},{8,16},{12,20},{16,8},{20,12},{24,0},{28,4},{1,25},{... | collective-permute-start | bytes 196616 | tf_op jit(solution)/shard_map/ppermute | solution.py:208
  79.9 2.9 %collective-permute-done.25 = bf16[2,32,512]{2,1,0:T(8,128)(2,1)S(1)} collective-permute-done((bf16[2,32,512]{2,1,0:T(8,128)(2,1)S(1)}, bf16[2,32,512]{2,1,0:T(8,128)(2,1)S(1)}, u32[]{:S(2)}, u32[]{:S(2)}) %collective-permute-start.25) | collective-permute-done | bytes 65568 | tf_op jit(solution)/shard_map/ppermute | solution.py:208
  87.0 2.4 %collective-permute-start.38 = (bf16[2,32,512]{2,1,0:T(8,128)(2,1)S(1)}, bf16[2,32,512]{2,1,0:T(8,128)(2,1)S(1)}, u32[]{:S(2)}, u32[]{:S(2)}) collective-permute-start(bf16[2,32,512]{2,1,0:T(8,128)(2,1)S(1)} %get-tuple-element.65.refs_8_.refs_12_.refs_16_), channel_id=1, source_target_pairs={{0,16},{4,20},{8,24},{12,28},{16,0},{20,4},{24,8},{28,12},{1,17},{... | collective-permute-start | bytes 196616 | tf_op jit(solution)/shard_map/ppermute | solution.py:152
  92.4 3.1 %collective-permute-done.39.refs_15_.refs_22_ = bf16[2,32,512]{2,1,0:T(8,128)(2,1)S(1)} collective-permute-done((bf16[2,32,512]{2,1,0:T(8,128)(2,1)S(1)}, bf16[2,32,512]{2,1,0:T(8,128)(2,1)S(1)}, u32[]{:S(2)}, u32[]{:S(2)}) %collective-permute-start.39) | collective-permute-done | bytes 65568 | tf_op jit(solution)/shard_map/ppermute | solution.py:152
  95.5 2.3 %backward2.1 = (f32[4,2,32,512]{3,2,1,0:T(8,128)S(1)}, bf16[4,2,32,512]{3,2,1,0:T(8,128)(2,1)S(1)}) custom-call(s32[6,5]{1,0:T(8,128)S(1)} %copy-done.1, s32[2]{0:T(128)S(1)} %pad_add_fusion.place_ref, bf16[6,2048,512]{2,1,0:T(8,128)(2,1)S(1)} %bitcast.122, bf16[4,2,32,512]{3,2,1,0:T(8,128)(2,1)S(1)} %convert_element_type.220.refs_0_, ...), custom_call_target="tpu_custom_call" | custom-call | flops 402653184 | bytes 12582912 | tf_op jit(solution)/shard_map/backward2/pallas_call | solution.py:161
  100.1 2.5 %forward2.1 = (f32[2,32,512]{2,1,0:T(8,128)S(1)}, bf16[2,32,512]{2,1,0:T(8,128)(2,1)S(1)}, bf16[2,32,512]{2,1,0:T(8,128)(2,1)S(1)}, bf16[2,32,512]{2,1,0:T(8,128)(2,1)S(1)}) custom-call(s32[6,5]{1,0:T(8,128)S(1)} %copy-done.1, s32[2]{0:T(128)S(1)} %pad_add_fusion.place_ref, bf16[6,512,2048]{2,1,0:T(8,128)(2,1)S(1)} %turn.1.turned_ref, ...), custom_call_target="tpu_custom_call" | custom-call | flops 402653184 | bytes 12582912 | tf_op jit(solution)/shard_map/forward2/pallas_call | solution.py:181
  106.2 4.5 %collective-permute-start.41 = (bf16[2,32,512]{2,1,0:T(8,128)(2,1)S(1)}, bf16[2,32,512]{2,1,0:T(8,128)(2,1)S(1)}, u32[]{:S(2)}, u32[]{:S(2)}) collective-permute-start(bf16[2,32,512]{2,1,0:T(8,128)(2,1)S(1)} %get-tuple-element.72), channel_id=1, source_target_pairs={{0,24},{4,28},{8,16},{12,20},{16,8},{20,12},{24,0},{28,4},{1,25},{... | collective-permute-start | bytes 196616 | tf_op jit(solution)/shard_map/ppermute | solution.py:208
  113.6 2.3 %collective-permute-done.42 = bf16[2,32,512]{2,1,0:T(8,128)(2,1)S(1)} collective-permute-done((bf16[2,32,512]{2,1,0:T(8,128)(2,1)S(1)}, bf16[2,32,512]{2,1,0:T(8,128)(2,1)S(1)}, u32[]{:S(2)}, u32[]{:S(2)}) %collective-permute-start.42) | collective-permute-done | bytes 65568 | tf_op jit(solution)/shard_map/ppermute | solution.py:208
  125.3 3.1 %collective-permute-done.56.refs_19_.refs_30_ = bf16[2,32,512]{2,1,0:T(8,128)(2,1)S(1)} collective-permute-done((bf16[2,32,512]{2,1,0:T(8,128)(2,1)S(1)}, bf16[2,32,512]{2,1,0:T(8,128)(2,1)S(1)}, u32[]{:S(2)}, u32[]{:S(2)}) %collective-permute-start.56) | collective-permute-done | bytes 65568 | tf_op jit(solution)/shard_map/ppermute | solution.py:152
  128.3 2.3 %backward3.1 = (f32[4,2,32,512]{3,2,1,0:T(8,128)S(1)}, bf16[4,2,32,512]{3,2,1,0:T(8,128)(2,1)S(1)}) custom-call(s32[6,5]{1,0:T(8,128)S(1)} %copy-done.1, s32[2]{0:T(128)S(1)} %pad_add_fusion.place_ref, bf16[6,2048,512]{2,1,0:T(8,128)(2,1)S(1)} %bitcast.122, bf16[4,2,32,512]{3,2,1,0:T(8,128)(2,1)S(1)} %convert_element_type.220.refs_0_, ...), custom_call_target="tpu_custom_call" | custom-call | flops 402653184 | bytes 12582912 | tf_op jit(solution)/shard_map/backward3/pallas_call | solution.py:161
  133.0 2.5 %forward3.1 = (f32[2,32,512]{2,1,0:T(8,128)S(1)}, bf16[2,32,512]{2,1,0:T(8,128)(2,1)S(1)}, bf16[2,32,512]{2,1,0:T(8,128)(2,1)S(1)}, bf16[2,32,512]{2,1,0:T(8,128)(2,1)S(1)}) custom-call(s32[6,5]{1,0:T(8,128)S(1)} %copy-done.1, s32[2]{0:T(128)S(1)} %pad_add_fusion.place_ref, bf16[6,512,2048]{2,1,0:T(8,128)(2,1)S(1)} %turn.1.turned_ref, ...), custom_call_target="tpu_custom_call" | custom-call | flops 402653184 | bytes 12582912 | tf_op jit(solution)/shard_map/forward3/pallas_call | solution.py:181
  139.1 4.7 %collective-permute-start.58 = (bf16[2,32,512]{2,1,0:T(8,128)(2,1)S(1)}, bf16[2,32,512]{2,1,0:T(8,128)(2,1)S(1)}, u32[]{:S(2)}, u32[]{:S(2)}) collective-permute-start(bf16[2,32,512]{2,1,0:T(8,128)(2,1)S(1)} %get-tuple-element.69), channel_id=1, source_target_pairs={{0,24},{4,28},{8,16},{12,20},{16,8},{20,12},{24,0},{28,4},{1,25},{... | collective-permute-start | bytes 196616 | tf_op jit(solution)/shard_map/ppermute | solution.py:208
  (147 shorter events, 69.5 us)
Async XLA Ops:
  1.1 14.2 %collective-permute-start.7 = (bf16[4,2,32,512]{3,2,1,0:T(8,128)(2,1)S(1)}, bf16[4,2,32,512]{3,2,1,0:T(8,128)(2,1)S(1)}, u32[]{:S(2)}, u32[]{:S(2)}) collective-permute-start(bf16[4,2,32,512]{3,2,1,0:T(8,128)(2,1)S(1)} %convert_element_type.220.refs_0_), channel_id=1, source_target_pairs={{0,8},{4,12},{8,0},{12,4},{16,24},{20,28},{24,16},{28,20},{1,9},{5... | collective-permute-start | bytes 786440 | tf_op jit(solution)/shard_map/ppermute | solution.py:152
  4.2 24.4 %collective-permute-start.8 = (bf16[4,2,32,512]{3,2,1,0:T(8,128)(2,1)S(1)}, bf16[4,2,32,512]{3,2,1,0:T(8,128)(2,1)S(1)}, u32[]{:S(2)}, u32[]{:S(2)}) collective-permute-start(bf16[4,2,32,512]{3,2,1,0:T(8,128)(2,1)S(1)} %convert_element_type.220.refs_0_), channel_id=1, source_target_pairs={{0,16},{4,20},{8,24},{12,28},{16,0},{20,4},{24,8},{28,12},{1,17},{... | collective-permute-start | bytes 786440 | tf_op jit(solution)/shard_map/ppermute | solution.py:152
  6.8 21.9 %collective-permute-start.9 = (bf16[4,2,32,512]{3,2,1,0:T(8,128)(2,1)S(1)}, bf16[4,2,32,512]{3,2,1,0:T(8,128)(2,1)S(1)}, u32[]{:S(2)}, u32[]{:S(2)}) collective-permute-start(bf16[4,2,32,512]{3,2,1,0:T(8,128)(2,1)S(1)} %convert_element_type.220.refs_0_), channel_id=1, source_target_pairs={{0,24},{4,28},{8,16},{12,20},{16,8},{20,12},{24,0},{28,4},{1,25},{... | collective-permute-start | bytes 786440 | tf_op jit(solution)/shard_map/ppermute | solution.py:152
  6.8 22.4 %collective-permute-start = (bf16[4,2,32,512]{3,2,1,0:T(8,128)(2,1)S(1)}, bf16[4,2,32,512]{3,2,1,0:T(8,128)(2,1)S(1)}, u32[]{:S(2)}, u32[]{:S(2)}) collective-permute-start(bf16[4,2,32,512]{3,2,1,0:T(8,128)(2,1)S(1)} %convert_element_type.220.refs_0_), channel_id=1, source_target_pairs={{0,1},{1,0},{2,3},{3,2},{4,5},{5,4},{6,7},{7,6},{8,9},{9,8},{10,11... | collective-permute-start | bytes 786440 | tf_op jit(solution)/shard_map/ppermute | solution.py:146
  8.5 20.8 %collective-permute-start.1 = (bf16[4,2,32,512]{3,2,1,0:T(8,128)(2,1)S(1)}, bf16[4,2,32,512]{3,2,1,0:T(8,128)(2,1)S(1)}, u32[]{:S(2)}, u32[]{:S(2)}) collective-permute-start(bf16[4,2,32,512]{3,2,1,0:T(8,128)(2,1)S(1)} %convert_element_type.220.refs_0_), channel_id=1, source_target_pairs={{0,2},{1,3},{2,0},{3,1},{4,6},{5,7},{6,4},{7,5},{8,10},{9,11},{10,... | collective-permute-start | bytes 786440 | tf_op jit(solution)/shard_map/ppermute | solution.py:146
  15.3 14.5 %collective-permute-start.2 = (bf16[4,2,32,512]{3,2,1,0:T(8,128)(2,1)S(1)}, bf16[4,2,32,512]{3,2,1,0:T(8,128)(2,1)S(1)}, u32[]{:S(2)}, u32[]{:S(2)}) collective-permute-start(bf16[4,2,32,512]{3,2,1,0:T(8,128)(2,1)S(1)} %convert_element_type.220.refs_0_), channel_id=1, source_target_pairs={{0,3},{1,2},{2,1},{3,0},{4,7},{5,6},{6,5},{7,4},{8,11},{9,10},{10,... | collective-permute-start | bytes 786440 | tf_op jit(solution)/shard_map/ppermute | solution.py:146
  32.1 6.7 %collective-permute-start.3 = (bf16[4,2,32,512]{3,2,1,0:T(8,128)(2,1)S(1)}, bf16[4,2,32,512]{3,2,1,0:T(8,128)(2,1)S(1)}, u32[]{:S(2)}, u32[]{:S(2)}) collective-permute-start(bf16[4,2,32,512]{3,2,1,0:T(8,128)(2,1)S(1)} %get-tuple-element.35), channel_id=1, source_target_pairs={{0,4},{4,0},{8,12},{12,8},{16,20},{20,16},{24,28},{28,24},{1,5},{5... | collective-permute-start | bytes 786440 | tf_op jit(solution)/shard_map/ppermute | solution.py:204
  35.3 9.0 %collective-permute-start.14 = (bf16[2,32,512]{2,1,0:T(8,128)(2,1)S(1)}, bf16[2,32,512]{2,1,0:T(8,128)(2,1)S(1)}, u32[]{:S(2)}, u32[]{:S(2)}) collective-permute-start(bf16[2,32,512]{2,1,0:T(8,128)(2,1)S(1)} %get-tuple-element.42), channel_id=1, source_target_pairs={{0,3},{1,2},{2,1},{3,0},{4,7},{5,6},{6,5},{7,4},{8,11},{9,10},{10,... | collective-permute-start | bytes 196616 | tf_op jit(solution)/shard_map/ppermute | solution.py:212
  35.7 9.3 %collective-permute-start.15 = (bf16[2,32,512]{2,1,0:T(8,128)(2,1)S(1)}, bf16[2,32,512]{2,1,0:T(8,128)(2,1)S(1)}, u32[]{:S(2)}, u32[]{:S(2)}) collective-permute-start(bf16[2,32,512]{2,1,0:T(8,128)(2,1)S(1)} %get-tuple-element.43), channel_id=1, source_target_pairs={{0,2},{1,3},{2,0},{3,1},{4,6},{5,7},{6,4},{7,5},{8,10},{9,11},{10,... | collective-permute-start | bytes 196616 | tf_op jit(solution)/shard_map/ppermute | solution.py:212
  37.3 7.6 %collective-permute-start.16 = (bf16[2,32,512]{2,1,0:T(8,128)(2,1)S(1)}, bf16[2,32,512]{2,1,0:T(8,128)(2,1)S(1)}, u32[]{:S(2)}, u32[]{:S(2)}) collective-permute-start(bf16[2,32,512]{2,1,0:T(8,128)(2,1)S(1)} %get-tuple-element.44), channel_id=1, source_target_pairs={{0,1},{1,0},{2,3},{3,2},{4,5},{5,4},{6,7},{7,6},{8,9},{9,8},{10,11... | collective-permute-start | bytes 196616 | tf_op jit(solution)/shard_map/ppermute | solution.py:212
  38.9 8.1 %collective-permute-start.4 = (bf16[2,32,512]{2,1,0:T(8,128)(2,1)S(1)}, bf16[2,32,512]{2,1,0:T(8,128)(2,1)S(1)}, u32[]{:S(2)}, u32[]{:S(2)}) collective-permute-start(bf16[2,32,512]{2,1,0:T(8,128)(2,1)S(1)} %get-tuple-element.78), channel_id=1, source_target_pairs={{0,24},{4,28},{8,16},{12,20},{16,8},{20,12},{24,0},{28,4},{1,25},{... | collective-permute-start | bytes 196616 | tf_op jit(solution)/shard_map/ppermute | solution.py:208
  50.9 6.9 %collective-permute-start.18 = (bf16[2,32,512]{2,1,0:T(8,128)(2,1)S(1)}, bf16[2,32,512]{2,1,0:T(8,128)(2,1)S(1)}, u32[]{:S(2)}, u32[]{:S(2)}) collective-permute-start(bf16[2,32,512]{2,1,0:T(8,128)(2,1)S(1)} %get-tuple-element.67.refs_4_.refs_8_), channel_id=1, source_target_pairs={{0,2},{1,3},{2,0},{3,1},{4,6},{5,7},{6,4},{7,5},{8,10},{9,11},{10,... | collective-permute-start | bytes 196616 | tf_op jit(solution)/shard_map/ppermute | solution.py:146
  64.8 8.5 %collective-permute-start.23 = (bf16[4,2,32,512]{3,2,1,0:T(8,128)(2,1)S(1)}, bf16[4,2,32,512]{3,2,1,0:T(8,128)(2,1)S(1)}, u32[]{:S(2)}, u32[]{:S(2)}) collective-permute-start(bf16[4,2,32,512]{3,2,1,0:T(8,128)(2,1)S(1)} %get-tuple-element.46), channel_id=1, source_target_pairs={{0,4},{4,0},{8,12},{12,8},{16,20},{20,16},{24,28},{28,24},{1,5},{5... | collective-permute-start | bytes 786440 | tf_op jit(solution)/shard_map/ppermute | solution.py:204
  69.8 7.9 %collective-permute-start.31 = (bf16[2,32,512]{2,1,0:T(8,128)(2,1)S(1)}, bf16[2,32,512]{2,1,0:T(8,128)(2,1)S(1)}, u32[]{:S(2)}, u32[]{:S(2)}) collective-permute-start(bf16[2,32,512]{2,1,0:T(8,128)(2,1)S(1)} %get-tuple-element.48), channel_id=1, source_target_pairs={{0,3},{1,2},{2,1},{3,0},{4,7},{5,6},{6,5},{7,4},{8,11},{9,10},{10,... | collective-permute-start | bytes 196616 | tf_op jit(solution)/shard_map/ppermute | solution.py:212
  84.1 6.8 %collective-permute-start.35 = (bf16[2,32,512]{2,1,0:T(8,128)(2,1)S(1)}, bf16[2,32,512]{2,1,0:T(8,128)(2,1)S(1)}, u32[]{:S(2)}, u32[]{:S(2)}) collective-permute-start(bf16[2,32,512]{2,1,0:T(8,128)(2,1)S(1)} %get-tuple-element.65.refs_8_.refs_12_.refs_16_), channel_id=1, source_target_pairs={{0,2},{1,3},{2,0},{3,1},{4,6},{5,7},{6,4},{7,5},{8,10},{9,11},{10,... | collective-permute-start | bytes 196616 | tf_op jit(solution)/shard_map/ppermute | solution.py:146
  97.8 8.4 %collective-permute-start.40 = (bf16[4,2,32,512]{3,2,1,0:T(8,128)(2,1)S(1)}, bf16[4,2,32,512]{3,2,1,0:T(8,128)(2,1)S(1)}, u32[]{:S(2)}, u32[]{:S(2)}) collective-permute-start(bf16[4,2,32,512]{3,2,1,0:T(8,128)(2,1)S(1)} %get-tuple-element.52), channel_id=1, source_target_pairs={{0,4},{4,0},{8,12},{12,8},{16,20},{20,16},{24,28},{28,24},{1,5},{5... | collective-permute-start | bytes 786440 | tf_op jit(solution)/shard_map/ppermute | solution.py:204
  102.6 8.1 %collective-permute-start.48 = (bf16[2,32,512]{2,1,0:T(8,128)(2,1)S(1)}, bf16[2,32,512]{2,1,0:T(8,128)(2,1)S(1)}, u32[]{:S(2)}, u32[]{:S(2)}) collective-permute-start(bf16[2,32,512]{2,1,0:T(8,128)(2,1)S(1)} %get-tuple-element.54), channel_id=1, source_target_pairs={{0,3},{1,2},{2,1},{3,0},{4,7},{5,6},{6,5},{7,4},{8,11},{9,10},{10,... | collective-permute-start | bytes 196616 | tf_op jit(solution)/shard_map/ppermute | solution.py:212
  104.3 7.1 %collective-permute-start.49 = (bf16[2,32,512]{2,1,0:T(8,128)(2,1)S(1)}, bf16[2,32,512]{2,1,0:T(8,128)(2,1)S(1)}, u32[]{:S(2)}, u32[]{:S(2)}) collective-permute-start(bf16[2,32,512]{2,1,0:T(8,128)(2,1)S(1)} %get-tuple-element.55), channel_id=1, source_target_pairs={{0,2},{1,3},{2,0},{3,1},{4,6},{5,7},{6,4},{7,5},{8,10},{9,11},{10,... | collective-permute-start | bytes 196616 | tf_op jit(solution)/shard_map/ppermute | solution.py:212
  106.2 7.3 %collective-permute-start.41 = (bf16[2,32,512]{2,1,0:T(8,128)(2,1)S(1)}, bf16[2,32,512]{2,1,0:T(8,128)(2,1)S(1)}, u32[]{:S(2)}, u32[]{:S(2)}) collective-permute-start(bf16[2,32,512]{2,1,0:T(8,128)(2,1)S(1)} %get-tuple-element.72), channel_id=1, source_target_pairs={{0,24},{4,28},{8,16},{12,20},{16,8},{20,12},{24,0},{28,4},{1,25},{... | collective-permute-start | bytes 196616 | tf_op jit(solution)/shard_map/ppermute | solution.py:208
  117.1 6.8 %collective-permute-start.52 = (bf16[2,32,512]{2,1,0:T(8,128)(2,1)S(1)}, bf16[2,32,512]{2,1,0:T(8,128)(2,1)S(1)}, u32[]{:S(2)}, u32[]{:S(2)}) collective-permute-start(bf16[2,32,512]{2,1,0:T(8,128)(2,1)S(1)} %get-tuple-element.63.refs_12_.refs_16_.refs_24_), channel_id=1, source_target_pairs={{0,2},{1,3},{2,0},{3,1},{4,6},{5,7},{6,4},{7,5},{8,10},{9,11},{10,... | collective-permute-start | bytes 196616 | tf_op jit(solution)/shard_map/ppermute | solution.py:146
  130.7 8.4 %collective-permute-start.57 = (bf16[4,2,32,512]{3,2,1,0:T(8,128)(2,1)S(1)}, bf16[4,2,32,512]{3,2,1,0:T(8,128)(2,1)S(1)}, u32[]{:S(2)}, u32[]{:S(2)}) collective-permute-start(bf16[4,2,32,512]{3,2,1,0:T(8,128)(2,1)S(1)} %get-tuple-element.58), channel_id=1, source_target_pairs={{0,4},{4,0},{8,12},{12,8},{16,20},{20,16},{24,28},{28,24},{1,5},{5... | collective-permute-start | bytes 786440 | tf_op jit(solution)/shard_map/ppermute | solution.py:204
  135.5 8.3 %collective-permute-start.65 = (bf16[2,32,512]{2,1,0:T(8,128)(2,1)S(1)}, bf16[2,32,512]{2,1,0:T(8,128)(2,1)S(1)}, u32[]{:S(2)}, u32[]{:S(2)}) collective-permute-start(bf16[2,32,512]{2,1,0:T(8,128)(2,1)S(1)} %get-tuple-element.60), channel_id=1, source_target_pairs={{0,3},{1,2},{2,1},{3,0},{4,7},{5,6},{6,5},{7,4},{8,11},{9,10},{10,... | collective-permute-start | bytes 196616 | tf_op jit(solution)/shard_map/ppermute | solution.py:212
  137.2 7.3 %collective-permute-start.66 = (bf16[2,32,512]{2,1,0:T(8,128)(2,1)S(1)}, bf16[2,32,512]{2,1,0:T(8,128)(2,1)S(1)}, u32[]{:S(2)}, u32[]{:S(2)}) collective-permute-start(bf16[2,32,512]{2,1,0:T(8,128)(2,1)S(1)} %get-tuple-element.61), channel_id=1, source_target_pairs={{0,2},{1,3},{2,0},{3,1},{4,6},{5,7},{6,4},{7,5},{8,10},{9,11},{10,... | collective-permute-start | bytes 196616 | tf_op jit(solution)/shard_map/ppermute | solution.py:212
  139.1 7.5 %collective-permute-start.58 = (bf16[2,32,512]{2,1,0:T(8,128)(2,1)S(1)}, bf16[2,32,512]{2,1,0:T(8,128)(2,1)S(1)}, u32[]{:S(2)}, u32[]{:S(2)}) collective-permute-start(bf16[2,32,512]{2,1,0:T(8,128)(2,1)S(1)} %get-tuple-element.69), channel_id=1, source_target_pairs={{0,24},{4,28},{8,16},{12,20},{16,8},{20,12},{24,0},{28,4},{1,25},{... | collective-permute-start | bytes 196616 | tf_op jit(solution)/shard_map/ppermute | solution.py:208
  (51 other events, 335.8 us)

commit v2 on v1

--- a/solution.py
+++ b/solution.py
@@ -146,18 +146,16 @@
             got[k] = lax.ppermute(x, "cols", swapped(cols, k))
         return [got[k] for k in range(cols)]
 
-    def spread_pairs(x, before=None):
+    def spread_planes(x):
         got = {0: x}
         for k in far_first(planes):
-            got[CORES * k] = lax.ppermute(x, "pairs", swapped(groups, CORES * k))
-        if before is not None:
-            got, before = lax.optimization_barrier((got, before))
-        for k in range(planes):
-            got[CORES * k + 1] = lax.ppermute(got[CORES * k], "pairs", swapped(groups, 1))
-        got = [got[p] for p in range(groups)]
-        return got if before is None else (got, before)
-
-    def backward(step, old, new, after):
+            got[k] = lax.ppermute(x, "pairs", swapped(groups, CORES * k))
+        return [got[k] for k in range(planes)]
+
+    def spread_cores(xs):
+        return [y for x in xs for y in (x, lax.ppermute(x, "pairs", swapped(groups, 1)))]
+
+    def backward(step, old, new):
         return pl.pallas_call(
             functools.partial(backward_kernel, step, groups, cols),
             out_shape=(
@@ -165,8 +163,7 @@
                 jax.ShapeDtypeStruct((planes, *block), BF16),
             ),
             in_specs=[smem, smem]
-            + [vmem] * (1 + cols * (1 + step))
-            + [anywhere] * len(after),
+            + [vmem] * (1 + cols * (1 + step)),
             out_specs=(vmem, vmem),
             scratch_shapes=[
                 pltpu.VMEM((slots, excite, rows), BF16),
@@ -175,7 +172,7 @@
             cost_estimate=cost,
             compiler_params=limit,
             name=f"backward{step}",
-        )(pair_list, place, near_tile_block, *old, *[x for n in new for x in n], *after)
+        )(pair_list, place, near_tile_block, *old, *[x for n in new for x in n])
 
     def forward(step, old, new, after):
         return pl.pallas_call(
@@ -196,17 +193,24 @@
         )(pair_list, place, turned, *old, *[x for n in new for x in n], *after)
 
     rounded = history.astype(BF16)
-    old_rows = spread_cols(rounded)
-    old_near, turned = spread_pairs(rounded, turned)
-    new_rows, new_near, results = [], [], []
+    planes_next = spread_planes(rounded)
+    cols_next = spread_cols(rounded)
+    rows_of, near_of, results = [], [], []
     for step in range(STEPS):
-        same, other = backward(step, old_rows, new_rows, new_near[-1][::CORES] if step else [])
+        rows_of.append(cols_next)
+        same, other = backward(step, rows_of[0], rows_of[1:])
+        if step == 0:
+            planes_next, same, turned = lax.optimization_barrier((planes_next, same, turned))
+        else:
+            planes_next, same, other = lax.optimization_barrier((planes_next, same, other))
         mate = lax.ppermute(other, "pairs", swapped(groups, 1))
-        field = same[0] + mate[0].astype(F32)
+        near_of.append(spread_cores(planes_next))
+        sent = [same[k] + mate[k].astype(F32) for k in range(planes)]
+        sent[1:] = [x.astype(BF16) for x in sent[1:]]
+        field = sent[0]
         for k in far_first(planes):
-            sent = (same[k] + mate[k].astype(F32)).astype(BF16)
-            field += lax.ppermute(sent, "pairs", swapped(groups, CORES * k)).astype(F32)
-        parts = forward(step, old_near, new_near, [same])
+            field += lax.ppermute(sent[k], "pairs", swapped(groups, CORES * k)).astype(F32)
+        parts = forward(step, near_of[0], near_of[1:], sent)
         field += parts[0]
         for k in far_first(cols):
             field += lax.ppermute(parts[k], "cols", swapped(cols, k)).astype(F32)
@@ -214,8 +218,8 @@
         results.append(fresh)
         if step + 1 < STEPS:
             newest = fresh.astype(BF16)
-            new_rows.append(spread_cols(newest))
-            new_near.append(spread_pairs(newest))
+            planes_next = spread_planes(newest)
+            cols_next = spread_cols(newest)
     return jnp.stack(results)
 
 

time: 151 us -> 139 us (0.921)
  waiting for transfers between devices: 40.9 us -> 21.9 us
  Pallas kernels: 25.4 us -> 36.7 us
  starting transfers between devices: 76.2 us -> 70.2 us
    ppermute x40, waiting for transfers between devices: 40.8 us -> 4.07 us  [the longest x12 3.34 us: shards(): lax.ppermute(sent[k], 'pairs', swapped(groups, CORES * k)).astype(F32)]
    ppermute x12, waiting for transfers between devices: 0.03 us -> 11.1 us  [shards(): field += lax.ppermute(parts[k], 'cols', swapped(cols, k)).astype(F32)]
    pallas_call x4, Pallas kernels: 10 us -> 15.7 us  [forward(): pl.pallas_call(functools.partial(forward_kernel, step, groups, cols), out...]
    pallas_call x4, Pallas kernels: 9.31 us -> 14.9 us  [backward(): pl.pallas_call(functools.partial(backward_kernel, step, groups, cols), ou...]
    ppermute x12, waiting for transfers between devices: 0.03 us -> 5.43 us  [spread_cols(): got[k] = lax.ppermute(x, 'cols', swapped(cols, k))]
    ppermute x40, starting transfers between devices: 44.7 us -> 40.4 us  [the longest x12 19.3 us: spread_planes(): got[k] = lax.ppermute(x, 'pairs', swapped(groups, CORES * k))]
  transfers between devices with their start and end apart: 68 -> 68, of which waited for: 27 -> 21; matrix products, arithmetic and copies ran while one was open for 0% -> 0% of each run, Pallas kernels for 12% -> 24%
where the time goes in v2:
time: 139 us; the launch traced here: 137 us
  starting transfers between devices  70.2 us (51%)
  Pallas kernels  36.7 us (26%)
  waiting for transfers between devices  21.9 us (16%)
  local copies, waits for them, and re-layouts  5.29 us (4%)
  other arithmetic  2.57 us (2%)
    ppermute x12, starting transfers between devices, spread_planes(): got[k] = lax.ppermute(x, 'pairs', swapped(groups, CORES * k))  19.3 us
    ppermute x12, starting transfers between devices, shards(): lax.ppermute(sent[k], 'pairs', swapped(groups, CORES * k)).astype(F32)  16.8 us
    pallas_call x4, Pallas kernels, forward(): pl.pallas_call(functools.partial(forward_kernel, step, groups, cols), out...  15.7 us
    ppermute x12, starting transfers between devices, spread_cols(): got[k] = lax.ppermute(x, 'cols', swapped(cols, k))  15.3 us
    pallas_call x4, Pallas kernels, backward(): pl.pallas_call(functools.partial(backward_kernel, step, groups, cols), ou...  14.9 us
    ppermute x12, starting transfers between devices, shards(): field += lax.ppermute(parts[k], 'cols', swapped(cols, k)).astype(F32)  14.3 us
    ppermute x12, waiting for transfers between devices, shards(): field += lax.ppermute(parts[k], 'cols', swapped(cols, k)).astype(F32)  11.1 us
    pallas_call x1, Pallas kernels, shards(): pl.pallas_call(turn_kernel, out_shape=pltpu.VMEM((slots, width, rows), BF...  6.08 us
  transfers between devices with their start and end apart: 68, of which 21 were waited for; matrix products, arithmetic and copies ran while one was open for 0% of the time, Pallas kernels for 24%

profile of v2, /device:TPU:0, one launch (start us, length us, event | category | flops | bytes accessed | tf_op | source)
XLA Modules:
  0.0 137.1 jit_solution(10874078215623749315)
XLA Ops:
  1.1 4.0 %collective-permute-start.5 = (bf16[4,2,32,512]{3,2,1,0:T(8,128)(2,1)S(1)}, bf16[4,2,32,512]{3,2,1,0:T(8,128)(2,1)S(1)}, u32[]{:S(2)}, u32[]{:S(2)}) collective-permute-start(bf16[4,2,32,512]{3,2,1,0:T(8,128)(2,1)S(1)} %convert_element_type.208.refs_0_), channel_id=1, source_target_pairs={{0,3},{1,2},{2,1},{3,0},{4,7},{5,6},{6,5},{7,4},{8,11},{9,10},{10,... | collective-permute-start | bytes 786440 | tf_op jit(solution)/shard_map/ppermute | solution.py:146
  5.7 4.0 %collective-permute-start.2 = (bf16[4,2,32,512]{3,2,1,0:T(8,128)(2,1)S(1)}, bf16[4,2,32,512]{3,2,1,0:T(8,128)(2,1)S(1)}, u32[]{:S(2)}, u32[]{:S(2)}) collective-permute-start(bf16[4,2,32,512]{3,2,1,0:T(8,128)(2,1)S(1)} %convert_element_type.208.refs_0_), channel_id=1, source_target_pairs={{0,24},{4,28},{8,16},{12,20},{16,8},{20,12},{24,0},{28,4},{1,25},{... | collective-permute-start | bytes 786440 | tf_op jit(solution)/shard_map/ppermute | solution.py:152
  9.8 2.5 %collective-permute-done.5.refs_3_ = bf16[4,2,32,512]{3,2,1,0:T(8,128)(2,1)S(1)} collective-permute-done((bf16[4,2,32,512]{3,2,1,0:T(8,128)(2,1)S(1)}, bf16[4,2,32,512]{3,2,1,0:T(8,128)(2,1)S(1)}, u32[]{:S(2)}, u32[]{:S(2)}) %collective-permute-start.5) | collective-permute-done | bytes 262176 | tf_op jit(solution)/shard_map/ppermute | solution.py:146
  14.3 2.7 %collective-permute-done.4.refs_2_ = bf16[4,2,32,512]{3,2,1,0:T(8,128)(2,1)S(1)} collective-permute-done((bf16[4,2,32,512]{3,2,1,0:T(8,128)(2,1)S(1)}, bf16[4,2,32,512]{3,2,1,0:T(8,128)(2,1)S(1)}, u32[]{:S(2)}, u32[]{:S(2)}) %collective-permute-start.4) | collective-permute-done | bytes 262176 | tf_op jit(solution)/shard_map/ppermute | solution.py:146
  17.3 4.6 %copy-done = bf16[6,2048,512]{2,1,0:T(8,128)(2,1)S(1)} copy-done((bf16[6,2048,512]{2,1,0:T(8,128)(2,1)S(1)}, bf16[6,2048,512]{2,1,0:T(8,128)(2,1)}, u32[]{:S(2)}) %copy-start) | copy-done | bytes 12582936
  22.5 3.7 %backward0.1 = (f32[4,2,32,512]{3,2,1,0:T(8,128)S(1)}, bf16[4,2,32,512]{3,2,1,0:T(8,128)(2,1)S(1)}) custom-call(s32[6,5]{1,0:T(8,128)S(1)} %copy-done.1, s32[2]{0:T(128)S(1)} %pad_add_fusion.place_ref, bf16[6,2048,512]{2,1,0:T(8,128)(2,1)S(1)} %copy-done, bf16[4,2,32,512]{3,2,1,0:T(8,128)(2,1)S(1)} %convert_element_type.208.refs_0_, ...), custom_call_target="tpu_custom_call" | custom-call | flops 402653184 | bytes 12582912 | tf_op jit(solution)/shard_map/backward0/pallas_call | solution.py:159
  26.3 6.1 %turn.1.turned_ref = bf16[6,512,2048]{2,1,0:T(8,128)(2,1)S(1)} custom-call(bf16[6,2048,512]{2,1,0:T(8,128)(2,1)S(1)} %copy-done), custom_call_target="tpu_custom_call" | custom-call | flops 402653184 | bytes 12582912 | tf_op jit(solution)/shard_map/turn/pallas_call | solution.py:133
  33.7 3.2 %collective-permute-start.7 = (bf16[2,32,512]{2,1,0:T(8,128)(2,1)S(1)}, bf16[2,32,512]{2,1,0:T(8,128)(2,1)S(1)}, u32[]{:S(2)}, u32[]{:S(2)}) collective-permute-start(bf16[2,32,512]{2,1,0:T(8,128)(2,1)S(1)} %get-tuple-element.119.refs_11_), channel_id=1, source_target_pairs={{0,24},{4,28},{8,16},{12,20},{16,8},{20,12},{24,0},{28,4},{1,25},{... | collective-permute-start | bytes 196616 | tf_op jit(solution)/shard_map/ppermute | solution.py:212
  38.2 3.9 %forward0.1 = (f32[2,32,512]{2,1,0:T(8,128)S(1)}, bf16[2,32,512]{2,1,0:T(8,128)(2,1)S(1)}, bf16[2,32,512]{2,1,0:T(8,128)(2,1)S(1)}, bf16[2,32,512]{2,1,0:T(8,128)(2,1)S(1)}) custom-call(s32[6,5]{1,0:T(8,128)S(1)} %copy-done.1, s32[2]{0:T(128)S(1)} %pad_add_fusion.place_ref, bf16[6,512,2048]{2,1,0:T(8,128)(2,1)S(1)} %turn.1.turned_ref, ...), custom_call_target="tpu_custom_call" | custom-call | flops 402653184 | bytes 12582912 | tf_op jit(solution)/shard_map/forward0/pallas_call | solution.py:178
  45.6 2.1 %collective-permute-done.14 = bf16[2,32,512]{2,1,0:T(8,128)(2,1)S(1)} collective-permute-done((bf16[2,32,512]{2,1,0:T(8,128)(2,1)S(1)}, bf16[2,32,512]{2,1,0:T(8,128)(2,1)S(1)}, u32[]{:S(2)}, u32[]{:S(2)}) %collective-permute-start.14) | collective-permute-done | bytes 65568 | tf_op jit(solution)/shard_map/ppermute | solution.py:216
  53.0 2.7 %collective-permute-start.19 = (bf16[2,32,512]{2,1,0:T(8,128)(2,1)S(1)}, bf16[2,32,512]{2,1,0:T(8,128)(2,1)S(1)}, u32[]{:S(2)}, u32[]{:S(2)}) collective-permute-start(bf16[2,32,512]{2,1,0:T(8,128)(2,1)S(1)} %get-tuple-element.69.refs_4_.refs_8_), channel_id=1, source_target_pairs={{0,24},{4,28},{8,16},{12,20},{16,8},{20,12},{24,0},{28,4},{1,25},{... | collective-permute-start | bytes 196616 | tf_op jit(solution)/shard_map/ppermute | solution.py:152
  57.4 3.7 %backward1.1 = (f32[4,2,32,512]{3,2,1,0:T(8,128)S(1)}, bf16[4,2,32,512]{3,2,1,0:T(8,128)(2,1)S(1)}) custom-call(s32[6,5]{1,0:T(8,128)S(1)} %copy-done.1, s32[2]{0:T(128)S(1)} %pad_add_fusion.place_ref, bf16[6,2048,512]{2,1,0:T(8,128)(2,1)S(1)} %bitcast.61, bf16[4,2,32,512]{3,2,1,0:T(8,128)(2,1)S(1)} %convert_element_type.208.refs_0_, ...), custom_call_target="tpu_custom_call" | custom-call | flops 402653184 | bytes 12582912 | tf_op jit(solution)/shard_map/backward1/pallas_call | solution.py:159
  62.9 2.3 %collective-permute-start.24 = (bf16[2,32,512]{2,1,0:T(8,128)(2,1)S(1)}, bf16[2,32,512]{2,1,0:T(8,128)(2,1)S(1)}, u32[]{:S(2)}, u32[]{:S(2)}) collective-permute-start(bf16[2,32,512]{2,1,0:T(8,128)(2,1)S(1)} %get-tuple-element.115.refs_19_), channel_id=1, source_target_pairs={{0,24},{4,28},{8,16},{12,20},{16,8},{20,12},{24,0},{28,4},{1,25},{... | collective-permute-start | bytes 196616 | tf_op jit(solution)/shard_map/ppermute | solution.py:212
  67.3 4.0 %forward1.1 = (f32[2,32,512]{2,1,0:T(8,128)S(1)}, bf16[2,32,512]{2,1,0:T(8,128)(2,1)S(1)}, bf16[2,32,512]{2,1,0:T(8,128)(2,1)S(1)}, bf16[2,32,512]{2,1,0:T(8,128)(2,1)S(1)}) custom-call(s32[6,5]{1,0:T(8,128)S(1)} %copy-done.1, s32[2]{0:T(128)S(1)} %pad_add_fusion.place_ref, bf16[6,512,2048]{2,1,0:T(8,128)(2,1)S(1)} %turn.1.turned_ref, ...), custom_call_target="tpu_custom_call" | custom-call | flops 402653184 | bytes 12582912 | tf_op jit(solution)/shard_map/forward1/pallas_call | solution.py:178
  74.9 2.2 %collective-permute-done.31 = bf16[2,32,512]{2,1,0:T(8,128)(2,1)S(1)} collective-permute-done((bf16[2,32,512]{2,1,0:T(8,128)(2,1)S(1)}, bf16[2,32,512]{2,1,0:T(8,128)(2,1)S(1)}, u32[]{:S(2)}, u32[]{:S(2)}) %collective-permute-start.31) | collective-permute-done | bytes 65568 | tf_op jit(solution)/shard_map/ppermute | solution.py:216
  83.1 2.6 %collective-permute-start.34 = (bf16[2,32,512]{2,1,0:T(8,128)(2,1)S(1)}, bf16[2,32,512]{2,1,0:T(8,128)(2,1)S(1)}, u32[]{:S(2)}, u32[]{:S(2)}) collective-permute-start(bf16[2,32,512]{2,1,0:T(8,128)(2,1)S(1)} %get-tuple-element.81.refs_8_.refs_16_), channel_id=1, source_target_pairs={{0,8},{4,12},{8,0},{12,4},{16,24},{20,28},{24,16},{28,20},{1,9},{5... | collective-permute-start | bytes 196616 | tf_op jit(solution)/shard_map/ppermute | solution.py:152
  85.7 3.7 %backward2.1 = (f32[4,2,32,512]{3,2,1,0:T(8,128)S(1)}, bf16[4,2,32,512]{3,2,1,0:T(8,128)(2,1)S(1)}) custom-call(s32[6,5]{1,0:T(8,128)S(1)} %copy-done.1, s32[2]{0:T(128)S(1)} %pad_add_fusion.place_ref, bf16[6,2048,512]{2,1,0:T(8,128)(2,1)S(1)} %bitcast.61, bf16[4,2,32,512]{3,2,1,0:T(8,128)(2,1)S(1)} %convert_element_type.208.refs_0_, ...), custom_call_target="tpu_custom_call" | custom-call | flops 402653184 | bytes 12582912 | tf_op jit(solution)/shard_map/backward2/pallas_call | solution.py:159
  92.5 3.1 %collective-permute-start.42 = (bf16[2,32,512]{2,1,0:T(8,128)(2,1)S(1)}, bf16[2,32,512]{2,1,0:T(8,128)(2,1)S(1)}, u32[]{:S(2)}, u32[]{:S(2)}) collective-permute-start(bf16[2,32,512]{2,1,0:T(8,128)(2,1)S(1)} %get-tuple-element.113.refs_26_), channel_id=1, source_target_pairs={{0,16},{4,20},{8,24},{12,28},{16,0},{20,4},{24,8},{28,12},{1,17},{... | collective-permute-start | bytes 196616 | tf_op jit(solution)/shard_map/ppermute | solution.py:212
  95.6 3.9 %forward2.1 = (f32[2,32,512]{2,1,0:T(8,128)S(1)}, bf16[2,32,512]{2,1,0:T(8,128)(2,1)S(1)}, bf16[2,32,512]{2,1,0:T(8,128)(2,1)S(1)}, bf16[2,32,512]{2,1,0:T(8,128)(2,1)S(1)}) custom-call(s32[6,5]{1,0:T(8,128)S(1)} %copy-done.1, s32[2]{0:T(128)S(1)} %pad_add_fusion.place_ref, bf16[6,512,2048]{2,1,0:T(8,128)(2,1)S(1)} %turn.1.turned_ref, ...), custom_call_target="tpu_custom_call" | custom-call | flops 402653184 | bytes 12582912 | tf_op jit(solution)/shard_map/forward2/pallas_call | solution.py:178
  103.1 2.3 %collective-permute-done.48 = bf16[2,32,512]{2,1,0:T(8,128)(2,1)S(1)} collective-permute-done((bf16[2,32,512]{2,1,0:T(8,128)(2,1)S(1)}, bf16[2,32,512]{2,1,0:T(8,128)(2,1)S(1)}, u32[]{:S(2)}, u32[]{:S(2)}) %collective-permute-start.48) | collective-permute-done | bytes 65568 | tf_op jit(solution)/shard_map/ppermute | solution.py:216
  112.3 2.5 %collective-permute-start.51 = (bf16[2,32,512]{2,1,0:T(8,128)(2,1)S(1)}, bf16[2,32,512]{2,1,0:T(8,128)(2,1)S(1)}, u32[]{:S(2)}, u32[]{:S(2)}) collective-permute-start(bf16[2,32,512]{2,1,0:T(8,128)(2,1)S(1)} %get-tuple-element.93.refs_12_.refs_24_), channel_id=1, source_target_pairs={{0,8},{4,12},{8,0},{12,4},{16,24},{20,28},{24,16},{28,20},{1,9},{5... | collective-permute-start | bytes 196616 | tf_op jit(solution)/shard_map/ppermute | solution.py:152
  114.9 3.7 %backward3.1 = (f32[4,2,32,512]{3,2,1,0:T(8,128)S(1)}, bf16[4,2,32,512]{3,2,1,0:T(8,128)(2,1)S(1)}) custom-call(s32[6,5]{1,0:T(8,128)S(1)} %copy-done.1, s32[2]{0:T(128)S(1)} %pad_add_fusion.place_ref, bf16[6,2048,512]{2,1,0:T(8,128)(2,1)S(1)} %bitcast.61, bf16[4,2,32,512]{3,2,1,0:T(8,128)(2,1)S(1)} %convert_element_type.208.refs_0_, ...), custom_call_target="tpu_custom_call" | custom-call | flops 402653184 | bytes 12582912 | tf_op jit(solution)/shard_map/backward3/pallas_call | solution.py:159
  121.0 3.9 %forward3.1 = (f32[2,32,512]{2,1,0:T(8,128)S(1)}, bf16[2,32,512]{2,1,0:T(8,128)(2,1)S(1)}, bf16[2,32,512]{2,1,0:T(8,128)(2,1)S(1)}, bf16[2,32,512]{2,1,0:T(8,128)(2,1)S(1)}) custom-call(s32[6,5]{1,0:T(8,128)S(1)} %copy-done.1, s32[2]{0:T(128)S(1)} %pad_add_fusion.place_ref, bf16[6,512,2048]{2,1,0:T(8,128)(2,1)S(1)} %turn.1.turned_ref, ...), custom_call_target="tpu_custom_call" | custom-call | flops 402653184 | bytes 12582912 | tf_op jit(solution)/shard_map/forward3/pallas_call | solution.py:178
  130.3 2.5 %collective-permute-start.59 = (bf16[2,32,512]{2,1,0:T(8,128)(2,1)S(1)}, bf16[2,32,512]{2,1,0:T(8,128)(2,1)S(1)}, u32[]{:S(2)}, u32[]{:S(2)}) collective-permute-start(bf16[2,32,512]{2,1,0:T(8,128)(2,1)S(1)} %get-tuple-element.109.refs_34_), channel_id=1, source_target_pairs={{0,16},{4,20},{8,24},{12,28},{16,0},{20,4},{24,8},{28,12},{1,17},{... | collective-permute-start | bytes 196616 | tf_op jit(solution)/shard_map/ppermute | solution.py:212
  (147 shorter events, 56.6 us)
Async XLA Ops:
  1.1 11.1 %collective-permute-start.5 = (bf16[4,2,32,512]{3,2,1,0:T(8,128)(2,1)S(1)}, bf16[4,2,32,512]{3,2,1,0:T(8,128)(2,1)S(1)}, u32[]{:S(2)}, u32[]{:S(2)}) collective-permute-start(bf16[4,2,32,512]{3,2,1,0:T(8,128)(2,1)S(1)} %convert_element_type.208.refs_0_), channel_id=1, source_target_pairs={{0,3},{1,2},{2,1},{3,0},{4,7},{5,6},{6,5},{7,4},{8,11},{9,10},{10,... | collective-permute-start | bytes 786440 | tf_op jit(solution)/shard_map/ppermute | solution.py:146
  5.0 11.9 %collective-permute-start.4 = (bf16[4,2,32,512]{3,2,1,0:T(8,128)(2,1)S(1)}, bf16[4,2,32,512]{3,2,1,0:T(8,128)(2,1)S(1)}, u32[]{:S(2)}, u32[]{:S(2)}) collective-permute-start(bf16[4,2,32,512]{3,2,1,0:T(8,128)(2,1)S(1)} %convert_element_type.208.refs_0_), channel_id=1, source_target_pairs={{0,2},{1,3},{2,0},{3,1},{4,6},{5,7},{6,4},{7,5},{8,10},{9,11},{10,... | collective-permute-start | bytes 786440 | tf_op jit(solution)/shard_map/ppermute | solution.py:146
  5.5 11.7 %collective-permute-start.3 = (bf16[4,2,32,512]{3,2,1,0:T(8,128)(2,1)S(1)}, bf16[4,2,32,512]{3,2,1,0:T(8,128)(2,1)S(1)}, u32[]{:S(2)}, u32[]{:S(2)}) collective-permute-start(bf16[4,2,32,512]{3,2,1,0:T(8,128)(2,1)S(1)} %convert_element_type.208.refs_0_), channel_id=1, source_target_pairs={{0,1},{1,0},{2,3},{3,2},{4,5},{5,4},{6,7},{7,6},{8,9},{9,8},{10,11... | collective-permute-start | bytes 786440 | tf_op jit(solution)/shard_map/ppermute | solution.py:146
  5.7 26.8 %collective-permute-start.2 = (bf16[4,2,32,512]{3,2,1,0:T(8,128)(2,1)S(1)}, bf16[4,2,32,512]{3,2,1,0:T(8,128)(2,1)S(1)}, u32[]{:S(2)}, u32[]{:S(2)}) collective-permute-start(bf16[4,2,32,512]{3,2,1,0:T(8,128)(2,1)S(1)} %convert_element_type.208.refs_0_), channel_id=1, source_target_pairs={{0,24},{4,28},{8,16},{12,20},{16,8},{20,12},{24,0},{28,4},{1,25},{... | collective-permute-start | bytes 786440 | tf_op jit(solution)/shard_map/ppermute | solution.py:152
  9.7 22.8 %collective-permute-start.1 = (bf16[4,2,32,512]{3,2,1,0:T(8,128)(2,1)S(1)}, bf16[4,2,32,512]{3,2,1,0:T(8,128)(2,1)S(1)}, u32[]{:S(2)}, u32[]{:S(2)}) collective-permute-start(bf16[4,2,32,512]{3,2,1,0:T(8,128)(2,1)S(1)} %convert_element_type.208.refs_0_), channel_id=1, source_target_pairs={{0,16},{4,20},{8,24},{12,28},{16,0},{20,4},{24,8},{28,12},{1,17},{... | collective-permute-start | bytes 786440 | tf_op jit(solution)/shard_map/ppermute | solution.py:152
  12.2 20.3 %collective-permute-start = (bf16[4,2,32,512]{3,2,1,0:T(8,128)(2,1)S(1)}, bf16[4,2,32,512]{3,2,1,0:T(8,128)(2,1)S(1)}, u32[]{:S(2)}, u32[]{:S(2)}) collective-permute-start(bf16[4,2,32,512]{3,2,1,0:T(8,128)(2,1)S(1)} %convert_element_type.208.refs_0_), channel_id=1, source_target_pairs={{0,8},{4,12},{8,0},{12,4},{16,24},{20,28},{24,16},{28,20},{1,9},{5... | collective-permute-start | bytes 786440 | tf_op jit(solution)/shard_map/ppermute | solution.py:152
  26.2 7.4 %collective-permute-start.6 = (bf16[4,2,32,512]{3,2,1,0:T(8,128)(2,1)S(1)}, bf16[4,2,32,512]{3,2,1,0:T(8,128)(2,1)S(1)}, u32[]{:S(2)}, u32[]{:S(2)}) collective-permute-start(bf16[4,2,32,512]{3,2,1,0:T(8,128)(2,1)S(1)} %get-tuple-element.55), channel_id=1, source_target_pairs={{0,4},{4,0},{8,12},{12,8},{16,20},{20,16},{24,28},{28,24},{1,5},{5... | collective-permute-start | bytes 786440 | tf_op jit(solution)/shard_map/ppermute | solution.py:206
  33.7 11.4 %collective-permute-start.7 = (bf16[2,32,512]{2,1,0:T(8,128)(2,1)S(1)}, bf16[2,32,512]{2,1,0:T(8,128)(2,1)S(1)}, u32[]{:S(2)}, u32[]{:S(2)}) collective-permute-start(bf16[2,32,512]{2,1,0:T(8,128)(2,1)S(1)} %get-tuple-element.119.refs_11_), channel_id=1, source_target_pairs={{0,24},{4,28},{8,16},{12,20},{16,8},{20,12},{24,0},{28,4},{1,25},{... | collective-permute-start | bytes 196616 | tf_op jit(solution)/shard_map/ppermute | solution.py:212
  36.9 8.7 %collective-permute-start.9 = (bf16[2,32,512]{2,1,0:T(8,128)(2,1)S(1)}, bf16[2,32,512]{2,1,0:T(8,128)(2,1)S(1)}, u32[]{:S(2)}, u32[]{:S(2)}) collective-permute-start(bf16[2,32,512]{2,1,0:T(8,128)(2,1)S(1)} %get-tuple-element.120.refs_9_), channel_id=1, source_target_pairs={{0,8},{4,12},{8,0},{12,4},{16,24},{20,28},{24,16},{28,20},{1,9},{5... | collective-permute-start | bytes 196616 | tf_op jit(solution)/shard_map/ppermute | solution.py:212
  36.9 8.7 %collective-permute-start.8 = (bf16[2,32,512]{2,1,0:T(8,128)(2,1)S(1)}, bf16[2,32,512]{2,1,0:T(8,128)(2,1)S(1)}, u32[]{:S(2)}, u32[]{:S(2)}) collective-permute-start(bf16[2,32,512]{2,1,0:T(8,128)(2,1)S(1)} %get-tuple-element.121.refs_10_), channel_id=1, source_target_pairs={{0,16},{4,20},{8,24},{12,28},{16,0},{20,4},{24,8},{28,12},{1,17},{... | collective-permute-start | bytes 196616 | tf_op jit(solution)/shard_map/ppermute | solution.py:212
  50.9 6.5 %collective-permute-start.21 = (bf16[2,32,512]{2,1,0:T(8,128)(2,1)S(1)}, bf16[2,32,512]{2,1,0:T(8,128)(2,1)S(1)}, u32[]{:S(2)}, u32[]{:S(2)}) collective-permute-start(bf16[2,32,512]{2,1,0:T(8,128)(2,1)S(1)} %get-tuple-element.69.refs_4_.refs_8_), channel_id=1, source_target_pairs={{0,2},{1,3},{2,0},{3,1},{4,6},{5,7},{6,4},{7,5},{8,10},{9,11},{10,... | collective-permute-start | bytes 196616 | tf_op jit(solution)/shard_map/ppermute | solution.py:146
  53.0 8.2 %collective-permute-start.19 = (bf16[2,32,512]{2,1,0:T(8,128)(2,1)S(1)}, bf16[2,32,512]{2,1,0:T(8,128)(2,1)S(1)}, u32[]{:S(2)}, u32[]{:S(2)}) collective-permute-start(bf16[2,32,512]{2,1,0:T(8,128)(2,1)S(1)} %get-tuple-element.69.refs_4_.refs_8_), channel_id=1, source_target_pairs={{0,24},{4,28},{8,16},{12,20},{16,8},{20,12},{24,0},{28,4},{1,25},{... | collective-permute-start | bytes 196616 | tf_op jit(solution)/shard_map/ppermute | solution.py:152
  62.9 10.5 %collective-permute-start.24 = (bf16[2,32,512]{2,1,0:T(8,128)(2,1)S(1)}, bf16[2,32,512]{2,1,0:T(8,128)(2,1)S(1)}, u32[]{:S(2)}, u32[]{:S(2)}) collective-permute-start(bf16[2,32,512]{2,1,0:T(8,128)(2,1)S(1)} %get-tuple-element.115.refs_19_), channel_id=1, source_target_pairs={{0,24},{4,28},{8,16},{12,20},{16,8},{20,12},{24,0},{28,4},{1,25},{... | collective-permute-start | bytes 196616 | tf_op jit(solution)/shard_map/ppermute | solution.py:212
  65.2 9.7 %collective-permute-start.26 = (bf16[2,32,512]{2,1,0:T(8,128)(2,1)S(1)}, bf16[2,32,512]{2,1,0:T(8,128)(2,1)S(1)}, u32[]{:S(2)}, u32[]{:S(2)}) collective-permute-start(bf16[2,32,512]{2,1,0:T(8,128)(2,1)S(1)} %get-tuple-element.116.refs_17_), channel_id=1, source_target_pairs={{0,8},{4,12},{8,0},{12,4},{16,24},{20,28},{24,16},{28,20},{1,9},{5... | collective-permute-start | bytes 196616 | tf_op jit(solution)/shard_map/ppermute | solution.py:212
  65.2 9.7 %collective-permute-start.25 = (bf16[2,32,512]{2,1,0:T(8,128)(2,1)S(1)}, bf16[2,32,512]{2,1,0:T(8,128)(2,1)S(1)}, u32[]{:S(2)}, u32[]{:S(2)}) collective-permute-start(bf16[2,32,512]{2,1,0:T(8,128)(2,1)S(1)} %get-tuple-element.117.refs_18_), channel_id=1, source_target_pairs={{0,16},{4,20},{8,24},{12,28},{16,0},{20,4},{24,8},{28,12},{1,17},{... | collective-permute-start | bytes 196616 | tf_op jit(solution)/shard_map/ppermute | solution.py:212
  81.3 8.1 %collective-permute-start.36 = (bf16[2,32,512]{2,1,0:T(8,128)(2,1)S(1)}, bf16[2,32,512]{2,1,0:T(8,128)(2,1)S(1)}, u32[]{:S(2)}, u32[]{:S(2)}) collective-permute-start(bf16[2,32,512]{2,1,0:T(8,128)(2,1)S(1)} %get-tuple-element.81.refs_8_.refs_16_), channel_id=1, source_target_pairs={{0,24},{4,28},{8,16},{12,20},{16,8},{20,12},{24,0},{28,4},{1,25},{... | collective-permute-start | bytes 196616 | tf_op jit(solution)/shard_map/ppermute | solution.py:152
  83.1 6.4 %collective-permute-start.35 = (bf16[2,32,512]{2,1,0:T(8,128)(2,1)S(1)}, bf16[2,32,512]{2,1,0:T(8,128)(2,1)S(1)}, u32[]{:S(2)}, u32[]{:S(2)}) collective-permute-start(bf16[2,32,512]{2,1,0:T(8,128)(2,1)S(1)} %get-tuple-element.81.refs_8_.refs_16_), channel_id=1, source_target_pairs={{0,16},{4,20},{8,24},{12,28},{16,0},{20,4},{24,8},{28,12},{1,17},{... | collective-permute-start | bytes 196616 | tf_op jit(solution)/shard_map/ppermute | solution.py:152
  83.1 6.4 %collective-permute-start.34 = (bf16[2,32,512]{2,1,0:T(8,128)(2,1)S(1)}, bf16[2,32,512]{2,1,0:T(8,128)(2,1)S(1)}, u32[]{:S(2)}, u32[]{:S(2)}) collective-permute-start(bf16[2,32,512]{2,1,0:T(8,128)(2,1)S(1)} %get-tuple-element.81.refs_8_.refs_16_), channel_id=1, source_target_pairs={{0,8},{4,12},{8,0},{12,4},{16,24},{20,28},{24,16},{28,20},{1,9},{5... | collective-permute-start | bytes 196616 | tf_op jit(solution)/shard_map/ppermute | solution.py:152
  91.2 11.4 %collective-permute-start.41 = (bf16[2,32,512]{2,1,0:T(8,128)(2,1)S(1)}, bf16[2,32,512]{2,1,0:T(8,128)(2,1)S(1)}, u32[]{:S(2)}, u32[]{:S(2)}) collective-permute-start(bf16[2,32,512]{2,1,0:T(8,128)(2,1)S(1)} %get-tuple-element.111.refs_27_), channel_id=1, source_target_pairs={{0,24},{4,28},{8,16},{12,20},{16,8},{20,12},{24,0},{28,4},{1,25},{... | collective-permute-start | bytes 196616 | tf_op jit(solution)/shard_map/ppermute | solution.py:212
  92.5 10.6 %collective-permute-start.43 = (bf16[2,32,512]{2,1,0:T(8,128)(2,1)S(1)}, bf16[2,32,512]{2,1,0:T(8,128)(2,1)S(1)}, u32[]{:S(2)}, u32[]{:S(2)}) collective-permute-start(bf16[2,32,512]{2,1,0:T(8,128)(2,1)S(1)} %get-tuple-element.112.refs_25_), channel_id=1, source_target_pairs={{0,8},{4,12},{8,0},{12,4},{16,24},{20,28},{24,16},{28,20},{1,9},{5... | collective-permute-start | bytes 196616 | tf_op jit(solution)/shard_map/ppermute | solution.py:212
  92.5 10.6 %collective-permute-start.42 = (bf16[2,32,512]{2,1,0:T(8,128)(2,1)S(1)}, bf16[2,32,512]{2,1,0:T(8,128)(2,1)S(1)}, u32[]{:S(2)}, u32[]{:S(2)}) collective-permute-start(bf16[2,32,512]{2,1,0:T(8,128)(2,1)S(1)} %get-tuple-element.113.refs_26_), channel_id=1, source_target_pairs={{0,16},{4,20},{8,24},{12,28},{16,0},{20,4},{24,8},{28,12},{1,17},{... | collective-permute-start | bytes 196616 | tf_op jit(solution)/shard_map/ppermute | solution.py:212
  108.4 6.5 %collective-permute-start.55 = (bf16[2,32,512]{2,1,0:T(8,128)(2,1)S(1)}, bf16[2,32,512]{2,1,0:T(8,128)(2,1)S(1)}, u32[]{:S(2)}, u32[]{:S(2)}) collective-permute-start(bf16[2,32,512]{2,1,0:T(8,128)(2,1)S(1)} %get-tuple-element.93.refs_12_.refs_24_), channel_id=1, source_target_pairs={{0,2},{1,3},{2,0},{3,1},{4,6},{5,7},{6,4},{7,5},{8,10},{9,11},{10,... | collective-permute-start | bytes 196616 | tf_op jit(solution)/shard_map/ppermute | solution.py:146
  110.5 8.1 %collective-permute-start.53 = (bf16[2,32,512]{2,1,0:T(8,128)(2,1)S(1)}, bf16[2,32,512]{2,1,0:T(8,128)(2,1)S(1)}, u32[]{:S(2)}, u32[]{:S(2)}) collective-permute-start(bf16[2,32,512]{2,1,0:T(8,128)(2,1)S(1)} %get-tuple-element.93.refs_12_.refs_24_), channel_id=1, source_target_pairs={{0,24},{4,28},{8,16},{12,20},{16,8},{20,12},{24,0},{28,4},{1,25},{... | collective-permute-start | bytes 196616 | tf_op jit(solution)/shard_map/ppermute | solution.py:152
  126.3 6.5 %collective-permute-start.58 = (bf16[2,32,512]{2,1,0:T(8,128)(2,1)S(1)}, bf16[2,32,512]{2,1,0:T(8,128)(2,1)S(1)}, u32[]{:S(2)}, u32[]{:S(2)}) collective-permute-start(bf16[2,32,512]{2,1,0:T(8,128)(2,1)S(1)} %get-tuple-element.107.refs_35_), channel_id=1, source_target_pairs={{0,24},{4,28},{8,16},{12,20},{16,8},{20,12},{24,0},{28,4},{1,25},{... | collective-permute-start | bytes 196616 | tf_op jit(solution)/shard_map/ppermute | solution.py:212
  (51 other events, 317.4 us)

commit v3 on v2

--- a/solution.py
+++ b/solution.py
@@ -21,15 +21,36 @@
     return sorted(range(1, n), key=lambda k: -bin(k).count("1") * n - k)
 
 
-def pick(step, delays, slot_delay, slot_cluster, old, new, put):
-    for delay in range(delays):
-
-        @pl.when(slot_delay == delay)
-        def _(delay=delay):
-            if delay < step:
-                put([ref[slot_cluster] for ref in new[step - 1 - delay]])
-            else:
-                put([ref[delay - step, slot_cluster] for ref in old])
+FIRST, PIECE, SECOND, DELAY, LIVE = range(5)
+
+
+def table_kernel(pairs_ref, table_ref):
+    slots = pairs_ref.shape[0]
+    me, col = lax.axis_index("pairs"), lax.axis_index("cols")
+    for s in range(slots):
+        for i in range(5):
+            value = pairs_ref[s, i]
+            table_ref[s, i] = value ^ me if i == PIECE else value
+    for i in range(5):
+        table_ref[slots, i] = col
+
+
+def pick(step, table_ref, s, old, new, put):
+    live = table_ref[s, LIVE] == 1
+    delay = table_ref[s, DELAY]
+
+    def zero_dead(blocks):
+        put([jnp.where(live, x, jnp.zeros_like(x)) for x in blocks])
+
+    for j in range(step):
+
+        @pl.when(delay == j)
+        def _(j=j):
+            zero_dead(new(step - 1 - j))
+
+    @pl.when(delay >= step)
+    def _():
+        zero_dead(old(delay - step))
 
 
 def turn_kernel(tile_ref, turned_ref):
@@ -43,12 +64,12 @@
             turned_ref[s, :, pl.ds(start, part)] = tile_ref[s, pl.ds(start, part), :].T
 
 
-def backward_kernel(step, groups, cols, pairs_ref, place_ref, tile_ref, *refs):
+def backward_kernel(step, groups, cols, table_ref, tile_ref, *refs):
     old = refs[:cols]
     new = [refs[cols * (1 + j) : cols * (2 + j)] for j in range(step)]
     same_ref, other_ref, rows_ref, sum_ref = refs[-4:]
     slots, _, width = tile_ref.shape
-    me, col = place_ref[0], place_ref[1]
+    col = table_ref[slots, 0]
     sum_ref[...] = jnp.zeros_like(sum_ref)
     for s in range(slots):
 
@@ -57,54 +78,55 @@
                 start = pl.multiple_of((col ^ k) * width, width)
                 rows_ref[s, :, pl.ds(start, width)] = blocks[k]
 
-        pick(step, old[0].shape[0], pairs_ref[s, 3], pairs_ref[s, 0], old, new, put)
-    for s in range(slots):
-
-        @pl.when(pairs_ref[s, 4] == 1)
-        def _(s=s):
-            piece = pairs_ref[s, 1] ^ me
-            sum_ref[piece, pairs_ref[s, 2]] += jnp.dot(
-                rows_ref[s], tile_ref[s], preferred_element_type=F32
-            )
+        first = table_ref[s, FIRST]
+        pick(
+            step,
+            table_ref,
+            s,
+            lambda d, first=first: [ref[d, first] for ref in old],
+            lambda j, first=first: [ref[first] for ref in new[j]],
+            put,
+        )
+    for s in range(slots):
+        sum_ref[table_ref[s, PIECE], table_ref[s, SECOND]] += jnp.dot(
+            rows_ref[s], tile_ref[s], preferred_element_type=F32
+        )
 
     for k in range(groups // CORES):
         same_ref[k] = sum_ref[CORES * k]
         other_ref[k] = sum_ref[CORES * k + 1].astype(other_ref.dtype)
 
 
-def forward_kernel(step, groups, cols, pairs_ref, place_ref, turned_ref, *refs):
+def forward_kernel(step, groups, cols, table_ref, turned_ref, *refs):
     old = refs[:groups]
     new = [refs[groups * (1 + j) : groups * (2 + j)] for j in range(step)]
     outs, near_ref, sum_ref = refs[-2 - cols : -2], refs[-2], refs[-1]
     slots, width, _ = turned_ref.shape
-    me, col = place_ref[0], place_ref[1]
+    col = table_ref[slots, 0]
     sum_ref[...] = jnp.zeros_like(sum_ref)
     for s in range(slots):
-        piece = pairs_ref[s, 1] ^ me
+
+        def put(blocks, s=s):
+            near_ref[s] = blocks[0]
+
+        second = table_ref[s, SECOND]
         for p in range(groups):
 
-            @pl.when(piece == p)
-            def _(s=s, p=p):
-                def put(blocks):
-                    near_ref[s] = blocks[0]
-
+            @pl.when(table_ref[s, PIECE] == p)
+            def _(s=s, p=p, second=second, put=put):
                 pick(
                     step,
-                    old[0].shape[0],
-                    pairs_ref[s, 3],
-                    pairs_ref[s, 2],
-                    [old[p]],
-                    [[n[p]] for n in new],
+                    table_ref,
+                    s,
+                    lambda d: [old[p][d, second]],
+                    lambda j: [new[j][p][second]],
                     put,
                 )
 
     for s in range(slots):
-
-        @pl.when(pairs_ref[s, 4] == 1)
-        def _(s=s):
-            sum_ref[pairs_ref[s, 0]] += jnp.dot(
-                near_ref[s], turned_ref[s], preferred_element_type=F32
-            )
+        sum_ref[table_ref[s, FIRST]] += jnp.dot(
+            near_ref[s], turned_ref[s], preferred_element_type=F32
+        )
 
     for k in range(cols):
         start = pl.multiple_of((col ^ k) * width, width)
@@ -118,7 +140,6 @@
     delays, clusters, excite, width = history.shape
     slots = pair_list.shape[0]
     block = (clusters, excite, width)
-    place = jnp.stack([lax.axis_index("pairs"), lax.axis_index("cols")]).astype(jnp.int32)
 
     smem = pl.BlockSpec(memory_space=pltpu.SMEM)
     vmem = pl.BlockSpec(memory_space=pltpu.VMEM)
@@ -130,16 +151,14 @@
         transcendentals=0,
     )
     limit = pltpu.CompilerParams(vmem_limit_bytes=16 * 2**20)
-    turned = pl.pallas_call(
-        turn_kernel,
-        out_shape=pltpu.VMEM((slots, width, rows), BF16),
-        in_specs=[vmem],
-        out_specs=vmem,
-        cost_estimate=cost,
-        compiler_params=limit,
-        name="turn",
-    )(near_tile_block)
-
+    table = pl.pallas_call(
+        table_kernel,
+        out_shape=pltpu.SMEM((slots + 1, 5), jnp.int32),
+        in_specs=[smem],
+        out_specs=smem,
+        compiler_params=pltpu.CompilerParams(vmem_limit_bytes=2**20),
+        name="table",
+    )(pair_list)
     def spread_cols(x):
         got = {0: x}
         for k in far_first(cols):
@@ -162,7 +181,7 @@
                 jax.ShapeDtypeStruct((planes, *block), F32),
                 jax.ShapeDtypeStruct((planes, *block), BF16),
             ),
-            in_specs=[smem, smem]
+            in_specs=[smem]
             + [vmem] * (1 + cols * (1 + step)),
             out_specs=(vmem, vmem),
             scratch_shapes=[
@@ -172,14 +191,14 @@
             cost_estimate=cost,
             compiler_params=limit,
             name=f"backward{step}",
-        )(pair_list, place, near_tile_block, *old, *[x for n in new for x in n])
+        )(table, near_tile_block, *old, *[x for n in new for x in n])
 
     def forward(step, old, new, after):
         return pl.pallas_call(
             functools.partial(forward_kernel, step, groups, cols),
             out_shape=[jax.ShapeDtypeStruct(block, F32)]
             + [jax.ShapeDtypeStruct(block, BF16)] * (cols - 1),
-            in_specs=[smem, smem]
+            in_specs=[smem]
             + [vmem] * (1 + groups * (1 + step))
             + [anywhere] * len(after),
             out_specs=[vmem] * cols,
@@ -190,18 +209,28 @@
             cost_estimate=cost,
             compiler_params=limit,
             name=f"forward{step}",
-        )(pair_list, place, turned, *old, *[x for n in new for x in n], *after)
+        )(table, turned, *old, *[x for n in new for x in n], *after)
 
     rounded = history.astype(BF16)
     planes_next = spread_planes(rounded)
     cols_next = spread_cols(rounded)
+    cols_next[-1], tile = lax.optimization_barrier((cols_next[-1], near_tile_block))
+    turned = pl.pallas_call(
+        turn_kernel,
+        out_shape=pltpu.VMEM((slots, width, rows), BF16),
+        in_specs=[vmem],
+        out_specs=vmem,
+        cost_estimate=cost,
+        compiler_params=limit,
+        name="turn",
+    )(tile)
     rows_of, near_of, results = [], [], []
     for step in range(STEPS):
+        if step == 0:
+            cols_next, turned, table = lax.optimization_barrier((cols_next, turned, table))
         rows_of.append(cols_next)
         same, other = backward(step, rows_of[0], rows_of[1:])
-        if step == 0:
-            planes_next, same, turned = lax.optimization_barrier((planes_next, same, turned))
-        else:
+        if step:
             planes_next, same, other = lax.optimization_barrier((planes_next, same, other))
         mate = lax.ppermute(other, "pairs", swapped(groups, 1))
         near_of.append(spread_cores(planes_next))

time: 139 us -> 129 us (0.928); the launches traced: 137 us -> 129 us
  Pallas kernels: 36.7 us -> 28.9 us
    pallas_call x4, Pallas kernels: 14.9 us -> 10.5 us  [backward(): pl.pallas_call(functools.partial(backward_kernel, step, groups, cols), ou...]
    ppermute x12, waiting for transfers between devices: 0.03 us -> 4.23 us  [spread_planes(): got[k] = lax.ppermute(x, 'pairs', swapped(groups, CORES * k))]
    ppermute x12, waiting for transfers between devices: 5.43 us -> 1.23 us  [spread_cols(): got[k] = lax.ppermute(x, 'cols', swapped(cols, k))]
    pallas_call x4, Pallas kernels: 15.7 us -> 11.7 us  [forward(): pl.pallas_call(functools.partial(forward_kernel, step, groups, cols), out...]
  transfers between devices with their start and end apart: 68 -> 68, of which waited for: 21 -> 24; matrix products, arithmetic and copies ran while one was open for 0% -> 0% of each run, Pallas kernels for 24% -> 20%
where the time goes in v3:
time: 129 us
  starting transfers between devices  70.7 us (55%)
  Pallas kernels  28.9 us (22%)
  waiting for transfers between devices  21.3 us (17%)
  local copies, waits for them, and re-layouts  5.29 us (4%)
  other arithmetic  2.49 us (2%)
    ppermute x12, starting transfers between devices, spread_planes(): got[k] = lax.ppermute(x, 'pairs', swapped(groups, CORES * k))  19.3 us
    ppermute x12, starting transfers between devices, shards(): lax.ppermute(sent[k], 'pairs', swapped(groups, CORES * k)).astype(F32)  17.7 us
    ppermute x12, starting transfers between devices, spread_cols(): got[k] = lax.ppermute(x, 'cols', swapped(cols, k))  15.3 us
    ppermute x12, starting transfers between devices, shards(): field += lax.ppermute(parts[k], 'cols', swapped(cols, k)).astype(F32)  14.2 us
    pallas_call x4, Pallas kernels, forward(): pl.pallas_call(functools.partial(forward_kernel, step, groups, cols), out...  11.7 us
    ppermute x12, waiting for transfers between devices, shards(): field += lax.ppermute(parts[k], 'cols', swapped(cols, k)).astype(F32)  10.9 us
    pallas_call x4, Pallas kernels, backward(): pl.pallas_call(functools.partial(backward_kernel, step, groups, cols), ou...  10.5 us
    pallas_call x1, Pallas kernels, shards(): pl.pallas_call(turn_kernel, out_shape=pltpu.VMEM((slots, width, rows), BF...  6.08 us
  transfers between devices with their start and end apart: 68, of which 24 were waited for; matrix products, arithmetic and copies ran while one was open for 0% of the time, Pallas kernels for 20%

profile of v3, /device:TPU:0, one launch (start us, length us, event | category | flops | bytes accessed | tf_op | source)
XLA Modules:
  0.0 129.0 jit_solution(9302545181776847715)
XLA Ops:
  1.1 4.0 %collective-permute-start.2 = (bf16[4,2,32,512]{3,2,1,0:T(8,128)(2,1)S(1)}, bf16[4,2,32,512]{3,2,1,0:T(8,128)(2,1)S(1)}, u32[]{:S(2)}, u32[]{:S(2)}) collective-permute-start(bf16[4,2,32,512]{3,2,1,0:T(8,128)(2,1)S(1)} %convert_element_type.208.refs_0_), channel_id=1, source_target_pairs={{0,3},{1,2},{2,1},{3,0},{4,7},{5,6},{6,5},{7,4},{8,11},{9,10},{10,... | collective-permute-start | bytes 786440 | tf_op jit(solution)/shard_map/ppermute | solution.py:165
  5.7 4.0 %collective-permute-start.12 = (bf16[4,2,32,512]{3,2,1,0:T(8,128)(2,1)S(1)}, bf16[4,2,32,512]{3,2,1,0:T(8,128)(2,1)S(1)}, u32[]{:S(2)}, u32[]{:S(2)}) collective-permute-start(bf16[4,2,32,512]{3,2,1,0:T(8,128)(2,1)S(1)} %convert_element_type.208.refs_0_), channel_id=1, source_target_pairs={{0,24},{4,28},{8,16},{12,20},{16,8},{20,12},{24,0},{28,4},{1,25},{... | collective-permute-start | bytes 786440 | tf_op jit(solution)/shard_map/ppermute | solution.py:171
  14.3 4.6 %copy-done = bf16[6,2048,512]{2,1,0:T(8,128)(2,1)S(1)} copy-done((bf16[6,2048,512]{2,1,0:T(8,128)(2,1)S(1)}, bf16[6,2048,512]{2,1,0:T(8,128)(2,1)}, u32[]{:S(2)}) %copy-start) | copy-done | bytes 12582936
  18.9 6.1 %turn.1.turned_ref = bf16[6,512,2048]{2,1,0:T(8,128)(2,1)S(1)} custom-call(bf16[6,2048,512]{2,1,0:T(8,128)(2,1)S(1)} %copy-done), custom_call_target="tpu_custom_call" | custom-call | flops 402653184 | bytes 12582912 | tf_op jit(solution)/shard_map/turn/pallas_call | solution.py:218
  25.0 2.5 %backward0.1 = (f32[4,2,32,512]{3,2,1,0:T(8,128)S(1)}, bf16[4,2,32,512]{3,2,1,0:T(8,128)(2,1)S(1)}) custom-call(s32[7,5]{1,0:T(8,128)S(4)} %table.1.table_ref, bf16[6,2048,512]{2,1,0:T(8,128)(2,1)S(1)} %copy-done, bf16[4,2,32,512]{3,2,1,0:T(8,128)(2,1)S(1)} %convert_element_type.208.refs_0_, bf16[4,2,32,512]{3,2,1,0:T(8,128)(2,1)S(1)} %collective-permute-done.refs_1_, ...), custom_call_target="tpu_custom_call" | custom-call | flops 402653184 | bytes 12582912 | tf_op jit(solution)/shard_map/backward0/pallas_call | solution.py:178
  28.2 2.9 %collective-permute-done.10.refs_4_ = bf16[4,2,32,512]{3,2,1,0:T(8,128)(2,1)S(1)} collective-permute-done((bf16[4,2,32,512]{3,2,1,0:T(8,128)(2,1)S(1)}, bf16[4,2,32,512]{3,2,1,0:T(8,128)(2,1)S(1)}, u32[]{:S(2)}, u32[]{:S(2)}) %collective-permute-start.10) | collective-permute-done | bytes 262176 | tf_op jit(solution)/shard_map/ppermute | solution.py:171
  31.7 2.5 %collective-permute-start.4 = (bf16[2,32,512]{2,1,0:T(8,128)(2,1)S(1)}, bf16[2,32,512]{2,1,0:T(8,128)(2,1)S(1)}, u32[]{:S(2)}, u32[]{:S(2)}) collective-permute-start(bf16[2,32,512]{2,1,0:T(8,128)(2,1)S(1)} %get-tuple-element.123.refs_11_), channel_id=1, source_target_pairs={{0,24},{4,28},{8,16},{12,20},{16,8},{20,12},{24,0},{28,4},{1,25},{... | collective-permute-start | bytes 196616 | tf_op jit(solution)/shard_map/ppermute | solution.py:241
  36.2 2.9 %forward0.1 = (f32[2,32,512]{2,1,0:T(8,128)S(1)}, bf16[2,32,512]{2,1,0:T(8,128)(2,1)S(1)}, bf16[2,32,512]{2,1,0:T(8,128)(2,1)S(1)}, bf16[2,32,512]{2,1,0:T(8,128)(2,1)S(1)}) custom-call(s32[7,5]{1,0:T(8,128)S(4)} %table.1.table_ref, bf16[6,512,2048]{2,1,0:T(8,128)(2,1)S(1)} %turn.1.turned_ref, bf16[4,2,32,512]{3,2,1,0:T(8,128)(2,1)S(1)} %convert_element_type.208.refs_0_, ...), custom_call_target="tpu_custom_call" | custom-call | flops 402653184 | bytes 12582912 | tf_op jit(solution)/shard_map/forward0/pallas_call | solution.py:197
  39.2 2.5 %collective-permute-start.14 = (bf16[2,32,512]{2,1,0:T(8,128)(2,1)S(1)}, bf16[2,32,512]{2,1,0:T(8,128)(2,1)S(1)}, u32[]{:S(2)}, u32[]{:S(2)}) collective-permute-start(bf16[2,32,512]{2,1,0:T(8,128)(2,1)S(1)} %get-tuple-element.66), channel_id=1, source_target_pairs={{0,3},{1,2},{2,1},{3,0},{4,7},{5,6},{6,5},{7,4},{8,11},{9,10},{10,... | collective-permute-start | bytes 196616 | tf_op jit(solution)/shard_map/ppermute | solution.py:245
  50.1 2.5 %collective-permute-start.19 = (bf16[2,32,512]{2,1,0:T(8,128)(2,1)S(1)}, bf16[2,32,512]{2,1,0:T(8,128)(2,1)S(1)}, u32[]{:S(2)}, u32[]{:S(2)}) collective-permute-start(bf16[2,32,512]{2,1,0:T(8,128)(2,1)S(1)} %get-tuple-element.73.refs_4_.refs_8_), channel_id=1, source_target_pairs={{0,24},{4,28},{8,16},{12,20},{16,8},{20,12},{24,0},{28,4},{1,25},{... | collective-permute-start | bytes 196616 | tf_op jit(solution)/shard_map/ppermute | solution.py:171
  54.5 2.6 %backward1.1 = (f32[4,2,32,512]{3,2,1,0:T(8,128)S(1)}, bf16[4,2,32,512]{3,2,1,0:T(8,128)(2,1)S(1)}) custom-call(s32[7,5]{1,0:T(8,128)S(4)} %table.1.table_ref, bf16[6,2048,512]{2,1,0:T(8,128)(2,1)S(1)} %bitcast.59, bf16[4,2,32,512]{3,2,1,0:T(8,128)(2,1)S(1)} %convert_element_type.208.refs_0_, bf16[4,2,32,512]{3,2,1,0:T(8,128)(2,1)S(1)} %collective-permute-done.refs_1_, ...), custom_call_target="tpu_custom_call" | custom-call | flops 402653184 | bytes 12582912 | tf_op jit(solution)/shard_map/backward1/pallas_call | solution.py:178
  59.4 2.4 %collective-permute-start.24 = (bf16[2,32,512]{2,1,0:T(8,128)(2,1)S(1)}, bf16[2,32,512]{2,1,0:T(8,128)(2,1)S(1)}, u32[]{:S(2)}, u32[]{:S(2)}) collective-permute-start(bf16[2,32,512]{2,1,0:T(8,128)(2,1)S(1)} %get-tuple-element.119.refs_19_), channel_id=1, source_target_pairs={{0,24},{4,28},{8,16},{12,20},{16,8},{20,12},{24,0},{28,4},{1,25},{... | collective-permute-start | bytes 196616 | tf_op jit(solution)/shard_map/ppermute | solution.py:241
  63.8 3.0 %forward1.1 = (f32[2,32,512]{2,1,0:T(8,128)S(1)}, bf16[2,32,512]{2,1,0:T(8,128)(2,1)S(1)}, bf16[2,32,512]{2,1,0:T(8,128)(2,1)S(1)}, bf16[2,32,512]{2,1,0:T(8,128)(2,1)S(1)}) custom-call(s32[7,5]{1,0:T(8,128)S(4)} %table.1.table_ref, bf16[6,512,2048]{2,1,0:T(8,128)(2,1)S(1)} %turn.1.turned_ref, bf16[4,2,32,512]{3,2,1,0:T(8,128)(2,1)S(1)} %convert_element_type.208.refs_0_, ...), custom_call_target="tpu_custom_call" | custom-call | flops 402653184 | bytes 12582912 | tf_op jit(solution)/shard_map/forward1/pallas_call | solution.py:197
  70.4 2.3 %collective-permute-done.31 = bf16[2,32,512]{2,1,0:T(8,128)(2,1)S(1)} collective-permute-done((bf16[2,32,512]{2,1,0:T(8,128)(2,1)S(1)}, bf16[2,32,512]{2,1,0:T(8,128)(2,1)S(1)}, u32[]{:S(2)}, u32[]{:S(2)}) %collective-permute-start.31) | collective-permute-done | bytes 65568 | tf_op jit(solution)/shard_map/ppermute | solution.py:245
  73.2 2.5 %collective-permute-start.39 = (bf16[2,32,512]{2,1,0:T(8,128)(2,1)S(1)}, bf16[2,32,512]{2,1,0:T(8,128)(2,1)S(1)}, u32[]{:S(2)}, u32[]{:S(2)}) collective-permute-start(bf16[2,32,512]{2,1,0:T(8,128)(2,1)S(1)} %get-tuple-element.85.refs_8_.refs_16_), channel_id=1, source_target_pairs={{0,3},{1,2},{2,1},{3,0},{4,7},{5,6},{6,5},{7,4},{8,11},{9,10},{10,... | collective-permute-start | bytes 196616 | tf_op jit(solution)/shard_map/ppermute | solution.py:165
  76.8 2.3 %collective-permute-start.36 = (bf16[2,32,512]{2,1,0:T(8,128)(2,1)S(1)}, bf16[2,32,512]{2,1,0:T(8,128)(2,1)S(1)}, u32[]{:S(2)}, u32[]{:S(2)}) collective-permute-start(bf16[2,32,512]{2,1,0:T(8,128)(2,1)S(1)} %get-tuple-element.85.refs_8_.refs_16_), channel_id=1, source_target_pairs={{0,24},{4,28},{8,16},{12,20},{16,8},{20,12},{24,0},{28,4},{1,25},{... | collective-permute-start | bytes 196616 | tf_op jit(solution)/shard_map/ppermute | solution.py:171
  81.2 2.8 %backward2.1 = (f32[4,2,32,512]{3,2,1,0:T(8,128)S(1)}, bf16[4,2,32,512]{3,2,1,0:T(8,128)(2,1)S(1)}) custom-call(s32[7,5]{1,0:T(8,128)S(4)} %table.1.table_ref, bf16[6,2048,512]{2,1,0:T(8,128)(2,1)S(1)} %bitcast.59, bf16[4,2,32,512]{3,2,1,0:T(8,128)(2,1)S(1)} %convert_element_type.208.refs_0_, bf16[4,2,32,512]{3,2,1,0:T(8,128)(2,1)S(1)} %collective-permute-done.refs_1_, ...), custom_call_target="tpu_custom_call" | custom-call | flops 402653184 | bytes 12582912 | tf_op jit(solution)/shard_map/backward2/pallas_call | solution.py:178
  85.9 2.4 %collective-permute-start.41 = (bf16[2,32,512]{2,1,0:T(8,128)(2,1)S(1)}, bf16[2,32,512]{2,1,0:T(8,128)(2,1)S(1)}, u32[]{:S(2)}, u32[]{:S(2)}) collective-permute-start(bf16[2,32,512]{2,1,0:T(8,128)(2,1)S(1)} %get-tuple-element.115.refs_27_), channel_id=1, source_target_pairs={{0,24},{4,28},{8,16},{12,20},{16,8},{20,12},{24,0},{28,4},{1,25},{... | collective-permute-start | bytes 196616 | tf_op jit(solution)/shard_map/ppermute | solution.py:241
  90.3 2.9 %forward2.1 = (f32[2,32,512]{2,1,0:T(8,128)S(1)}, bf16[2,32,512]{2,1,0:T(8,128)(2,1)S(1)}, bf16[2,32,512]{2,1,0:T(8,128)(2,1)S(1)}, bf16[2,32,512]{2,1,0:T(8,128)(2,1)S(1)}) custom-call(s32[7,5]{1,0:T(8,128)S(4)} %table.1.table_ref, bf16[6,512,2048]{2,1,0:T(8,128)(2,1)S(1)} %turn.1.turned_ref, bf16[4,2,32,512]{3,2,1,0:T(8,128)(2,1)S(1)} %convert_element_type.208.refs_0_, ...), custom_call_target="tpu_custom_call" | custom-call | flops 402653184 | bytes 12582912 | tf_op jit(solution)/shard_map/forward2/pallas_call | solution.py:197
  93.2 2.5 %collective-permute-start.48 = (bf16[2,32,512]{2,1,0:T(8,128)(2,1)S(1)}, bf16[2,32,512]{2,1,0:T(8,128)(2,1)S(1)}, u32[]{:S(2)}, u32[]{:S(2)}) collective-permute-start(bf16[2,32,512]{2,1,0:T(8,128)(2,1)S(1)} %get-tuple-element.90), channel_id=1, source_target_pairs={{0,3},{1,2},{2,1},{3,0},{4,7},{5,6},{6,5},{7,4},{8,11},{9,10},{10,... | collective-permute-start | bytes 196616 | tf_op jit(solution)/shard_map/ppermute | solution.py:245
  104.1 2.3 %collective-permute-start.53 = (bf16[2,32,512]{2,1,0:T(8,128)(2,1)S(1)}, bf16[2,32,512]{2,1,0:T(8,128)(2,1)S(1)}, u32[]{:S(2)}, u32[]{:S(2)}) collective-permute-start(bf16[2,32,512]{2,1,0:T(8,128)(2,1)S(1)} %get-tuple-element.97.refs_12_.refs_24_), channel_id=1, source_target_pairs={{0,24},{4,28},{8,16},{12,20},{16,8},{20,12},{24,0},{28,4},{1,25},{... | collective-permute-start | bytes 196616 | tf_op jit(solution)/shard_map/ppermute | solution.py:171
  108.5 2.6 %backward3.1 = (f32[4,2,32,512]{3,2,1,0:T(8,128)S(1)}, bf16[4,2,32,512]{3,2,1,0:T(8,128)(2,1)S(1)}) custom-call(s32[7,5]{1,0:T(8,128)S(4)} %table.1.table_ref, bf16[6,2048,512]{2,1,0:T(8,128)(2,1)S(1)} %bitcast.59, bf16[4,2,32,512]{3,2,1,0:T(8,128)(2,1)S(1)} %convert_element_type.208.refs_0_, bf16[4,2,32,512]{3,2,1,0:T(8,128)(2,1)S(1)} %collective-permute-done.refs_1_, ...), custom_call_target="tpu_custom_call" | custom-call | flops 402653184 | bytes 12582912 | tf_op jit(solution)/shard_map/backward3/pallas_call | solution.py:178
  113.9 2.9 %forward3.1 = (f32[2,32,512]{2,1,0:T(8,128)S(1)}, bf16[2,32,512]{2,1,0:T(8,128)(2,1)S(1)}, bf16[2,32,512]{2,1,0:T(8,128)(2,1)S(1)}, bf16[2,32,512]{2,1,0:T(8,128)(2,1)S(1)}) custom-call(s32[7,5]{1,0:T(8,128)S(4)} %table.1.table_ref, bf16[6,512,2048]{2,1,0:T(8,128)(2,1)S(1)} %turn.1.turned_ref, bf16[4,2,32,512]{3,2,1,0:T(8,128)(2,1)S(1)} %convert_element_type.208.refs_0_, ...), custom_call_target="tpu_custom_call" | custom-call | flops 402653184 | bytes 12582912 | tf_op jit(solution)/shard_map/forward3/pallas_call | solution.py:197
  118.3 2.3 %collective-permute-start.58 = (bf16[2,32,512]{2,1,0:T(8,128)(2,1)S(1)}, bf16[2,32,512]{2,1,0:T(8,128)(2,1)S(1)}, u32[]{:S(2)}, u32[]{:S(2)}) collective-permute-start(bf16[2,32,512]{2,1,0:T(8,128)(2,1)S(1)} %get-tuple-element.111.refs_35_), channel_id=1, source_target_pairs={{0,24},{4,28},{8,16},{12,20},{16,8},{20,12},{24,0},{28,4},{1,25},{... | collective-permute-start | bytes 196616 | tf_op jit(solution)/shard_map/ppermute | solution.py:241
  (147 shorter events, 58.5 us)
Async XLA Ops:
  1.1 11.1 %collective-permute-start.2 = (bf16[4,2,32,512]{3,2,1,0:T(8,128)(2,1)S(1)}, bf16[4,2,32,512]{3,2,1,0:T(8,128)(2,1)S(1)}, u32[]{:S(2)}, u32[]{:S(2)}) collective-permute-start(bf16[4,2,32,512]{3,2,1,0:T(8,128)(2,1)S(1)} %convert_element_type.208.refs_0_), channel_id=1, source_target_pairs={{0,3},{1,2},{2,1},{3,0},{4,7},{5,6},{6,5},{7,4},{8,11},{9,10},{10,... | collective-permute-start | bytes 786440 | tf_op jit(solution)/shard_map/ppermute | solution.py:165
  5.0 20.0 %collective-permute-start.1 = (bf16[4,2,32,512]{3,2,1,0:T(8,128)(2,1)S(1)}, bf16[4,2,32,512]{3,2,1,0:T(8,128)(2,1)S(1)}, u32[]{:S(2)}, u32[]{:S(2)}) collective-permute-start(bf16[4,2,32,512]{3,2,1,0:T(8,128)(2,1)S(1)} %convert_element_type.208.refs_0_), channel_id=1, source_target_pairs={{0,2},{1,3},{2,0},{3,1},{4,6},{5,7},{6,4},{7,5},{8,10},{9,11},{10,... | collective-permute-start | bytes 786440 | tf_op jit(solution)/shard_map/ppermute | solution.py:165
  5.5 19.5 %collective-permute-start = (bf16[4,2,32,512]{3,2,1,0:T(8,128)(2,1)S(1)}, bf16[4,2,32,512]{3,2,1,0:T(8,128)(2,1)S(1)}, u32[]{:S(2)}, u32[]{:S(2)}) collective-permute-start(bf16[4,2,32,512]{3,2,1,0:T(8,128)(2,1)S(1)} %convert_element_type.208.refs_0_), channel_id=1, source_target_pairs={{0,1},{1,0},{2,3},{3,2},{4,5},{5,4},{6,7},{7,6},{8,9},{9,8},{10,11... | collective-permute-start | bytes 786440 | tf_op jit(solution)/shard_map/ppermute | solution.py:165
  5.7 22.5 %collective-permute-start.12 = (bf16[4,2,32,512]{3,2,1,0:T(8,128)(2,1)S(1)}, bf16[4,2,32,512]{3,2,1,0:T(8,128)(2,1)S(1)}, u32[]{:S(2)}, u32[]{:S(2)}) collective-permute-start(bf16[4,2,32,512]{3,2,1,0:T(8,128)(2,1)S(1)} %convert_element_type.208.refs_0_), channel_id=1, source_target_pairs={{0,24},{4,28},{8,16},{12,20},{16,8},{20,12},{24,0},{28,4},{1,25},{... | collective-permute-start | bytes 786440 | tf_op jit(solution)/shard_map/ppermute | solution.py:171
  9.7 21.5 %collective-permute-start.10 = (bf16[4,2,32,512]{3,2,1,0:T(8,128)(2,1)S(1)}, bf16[4,2,32,512]{3,2,1,0:T(8,128)(2,1)S(1)}, u32[]{:S(2)}, u32[]{:S(2)}) collective-permute-start(bf16[4,2,32,512]{3,2,1,0:T(8,128)(2,1)S(1)} %convert_element_type.208.refs_0_), channel_id=1, source_target_pairs={{0,16},{4,20},{8,24},{12,28},{16,0},{20,4},{24,8},{28,12},{1,17},{... | collective-permute-start | bytes 786440 | tf_op jit(solution)/shard_map/ppermute | solution.py:171
  12.2 18.9 %collective-permute-start.8 = (bf16[4,2,32,512]{3,2,1,0:T(8,128)(2,1)S(1)}, bf16[4,2,32,512]{3,2,1,0:T(8,128)(2,1)S(1)}, u32[]{:S(2)}, u32[]{:S(2)}) collective-permute-start(bf16[4,2,32,512]{3,2,1,0:T(8,128)(2,1)S(1)} %convert_element_type.208.refs_0_), channel_id=1, source_target_pairs={{0,8},{4,12},{8,0},{12,4},{16,24},{20,28},{24,16},{28,20},{1,9},{5... | collective-permute-start | bytes 786440 | tf_op jit(solution)/shard_map/ppermute | solution.py:171
  27.7 6.6 %collective-permute-start.7 = (bf16[4,2,32,512]{3,2,1,0:T(8,128)(2,1)S(1)}, bf16[4,2,32,512]{3,2,1,0:T(8,128)(2,1)S(1)}, u32[]{:S(2)}, u32[]{:S(2)}) collective-permute-start(bf16[4,2,32,512]{3,2,1,0:T(8,128)(2,1)S(1)} %convert_element_type.208.refs_0_), channel_id=1, source_target_pairs={{0,4},{4,0},{8,12},{12,8},{16,20},{20,16},{24,28},{28,24},{1,5},{5... | collective-permute-start | bytes 786440 | tf_op jit(solution)/shard_map/ppermute | solution.py:175
  28.2 6.1 %collective-permute-start.13 = (bf16[4,2,32,512]{3,2,1,0:T(8,128)(2,1)S(1)}, bf16[4,2,32,512]{3,2,1,0:T(8,128)(2,1)S(1)}, u32[]{:S(2)}, u32[]{:S(2)}) collective-permute-start(bf16[4,2,32,512]{3,2,1,0:T(8,128)(2,1)S(1)} %collective-permute-done.12.refs_6_), channel_id=1, source_target_pairs={{0,4},{4,0},{8,12},{12,8},{16,20},{20,16},{24,28},{28,24},{1,5},{5... | collective-permute-start | bytes 786440 | tf_op jit(solution)/shard_map/ppermute | solution.py:175
  31.7 10.4 %collective-permute-start.4 = (bf16[2,32,512]{2,1,0:T(8,128)(2,1)S(1)}, bf16[2,32,512]{2,1,0:T(8,128)(2,1)S(1)}, u32[]{:S(2)}, u32[]{:S(2)}) collective-permute-start(bf16[2,32,512]{2,1,0:T(8,128)(2,1)S(1)} %get-tuple-element.123.refs_11_), channel_id=1, source_target_pairs={{0,24},{4,28},{8,16},{12,20},{16,8},{20,12},{24,0},{28,4},{1,25},{... | collective-permute-start | bytes 196616 | tf_op jit(solution)/shard_map/ppermute | solution.py:241
  34.3 8.4 %collective-permute-start.6 = (bf16[2,32,512]{2,1,0:T(8,128)(2,1)S(1)}, bf16[2,32,512]{2,1,0:T(8,128)(2,1)S(1)}, u32[]{:S(2)}, u32[]{:S(2)}) collective-permute-start(bf16[2,32,512]{2,1,0:T(8,128)(2,1)S(1)} %get-tuple-element.124.refs_9_), channel_id=1, source_target_pairs={{0,8},{4,12},{8,0},{12,4},{16,24},{20,28},{24,16},{28,20},{1,9},{5... | collective-permute-start | bytes 196616 | tf_op jit(solution)/shard_map/ppermute | solution.py:241
  34.3 8.4 %collective-permute-start.5 = (bf16[2,32,512]{2,1,0:T(8,128)(2,1)S(1)}, bf16[2,32,512]{2,1,0:T(8,128)(2,1)S(1)}, u32[]{:S(2)}, u32[]{:S(2)}) collective-permute-start(bf16[2,32,512]{2,1,0:T(8,128)(2,1)S(1)} %get-tuple-element.125.refs_10_), channel_id=1, source_target_pairs={{0,16},{4,20},{8,24},{12,28},{16,0},{20,4},{24,8},{28,12},{1,17},{... | collective-permute-start | bytes 196616 | tf_op jit(solution)/shard_map/ppermute | solution.py:241
  48.1 6.4 %collective-permute-start.21 = (bf16[2,32,512]{2,1,0:T(8,128)(2,1)S(1)}, bf16[2,32,512]{2,1,0:T(8,128)(2,1)S(1)}, u32[]{:S(2)}, u32[]{:S(2)}) collective-permute-start(bf16[2,32,512]{2,1,0:T(8,128)(2,1)S(1)} %get-tuple-element.73.refs_4_.refs_8_), channel_id=1, source_target_pairs={{0,2},{1,3},{2,0},{3,1},{4,6},{5,7},{6,4},{7,5},{8,10},{9,11},{10,... | collective-permute-start | bytes 196616 | tf_op jit(solution)/shard_map/ppermute | solution.py:165
  50.1 7.0 %collective-permute-start.19 = (bf16[2,32,512]{2,1,0:T(8,128)(2,1)S(1)}, bf16[2,32,512]{2,1,0:T(8,128)(2,1)S(1)}, u32[]{:S(2)}, u32[]{:S(2)}) collective-permute-start(bf16[2,32,512]{2,1,0:T(8,128)(2,1)S(1)} %get-tuple-element.73.refs_4_.refs_8_), channel_id=1, source_target_pairs={{0,24},{4,28},{8,16},{12,20},{16,8},{20,12},{24,0},{28,4},{1,25},{... | collective-permute-start | bytes 196616 | tf_op jit(solution)/shard_map/ppermute | solution.py:171
  59.4 9.5 %collective-permute-start.24 = (bf16[2,32,512]{2,1,0:T(8,128)(2,1)S(1)}, bf16[2,32,512]{2,1,0:T(8,128)(2,1)S(1)}, u32[]{:S(2)}, u32[]{:S(2)}) collective-permute-start(bf16[2,32,512]{2,1,0:T(8,128)(2,1)S(1)} %get-tuple-element.119.refs_19_), channel_id=1, source_target_pairs={{0,24},{4,28},{8,16},{12,20},{16,8},{20,12},{24,0},{28,4},{1,25},{... | collective-permute-start | bytes 196616 | tf_op jit(solution)/shard_map/ppermute | solution.py:241
  61.7 8.7 %collective-permute-start.26 = (bf16[2,32,512]{2,1,0:T(8,128)(2,1)S(1)}, bf16[2,32,512]{2,1,0:T(8,128)(2,1)S(1)}, u32[]{:S(2)}, u32[]{:S(2)}) collective-permute-start(bf16[2,32,512]{2,1,0:T(8,128)(2,1)S(1)} %get-tuple-element.120.refs_17_), channel_id=1, source_target_pairs={{0,8},{4,12},{8,0},{12,4},{16,24},{20,28},{24,16},{28,20},{1,9},{5... | collective-permute-start | bytes 196616 | tf_op jit(solution)/shard_map/ppermute | solution.py:241
  62.0 8.4 %collective-permute-start.25 = (bf16[2,32,512]{2,1,0:T(8,128)(2,1)S(1)}, bf16[2,32,512]{2,1,0:T(8,128)(2,1)S(1)}, u32[]{:S(2)}, u32[]{:S(2)}) collective-permute-start(bf16[2,32,512]{2,1,0:T(8,128)(2,1)S(1)} %get-tuple-element.121.refs_18_), channel_id=1, source_target_pairs={{0,16},{4,20},{8,24},{12,28},{16,0},{20,4},{24,8},{28,12},{1,17},{... | collective-permute-start | bytes 196616 | tf_op jit(solution)/shard_map/ppermute | solution.py:241
  76.8 7.2 %collective-permute-start.36 = (bf16[2,32,512]{2,1,0:T(8,128)(2,1)S(1)}, bf16[2,32,512]{2,1,0:T(8,128)(2,1)S(1)}, u32[]{:S(2)}, u32[]{:S(2)}) collective-permute-start(bf16[2,32,512]{2,1,0:T(8,128)(2,1)S(1)} %get-tuple-element.85.refs_8_.refs_16_), channel_id=1, source_target_pairs={{0,24},{4,28},{8,16},{12,20},{16,8},{20,12},{24,0},{28,4},{1,25},{... | collective-permute-start | bytes 196616 | tf_op jit(solution)/shard_map/ppermute | solution.py:171
  85.9 10.4 %collective-permute-start.41 = (bf16[2,32,512]{2,1,0:T(8,128)(2,1)S(1)}, bf16[2,32,512]{2,1,0:T(8,128)(2,1)S(1)}, u32[]{:S(2)}, u32[]{:S(2)}) collective-permute-start(bf16[2,32,512]{2,1,0:T(8,128)(2,1)S(1)} %get-tuple-element.115.refs_27_), channel_id=1, source_target_pairs={{0,24},{4,28},{8,16},{12,20},{16,8},{20,12},{24,0},{28,4},{1,25},{... | collective-permute-start | bytes 196616 | tf_op jit(solution)/shard_map/ppermute | solution.py:241
  88.2 8.5 %collective-permute-start.43 = (bf16[2,32,512]{2,1,0:T(8,128)(2,1)S(1)}, bf16[2,32,512]{2,1,0:T(8,128)(2,1)S(1)}, u32[]{:S(2)}, u32[]{:S(2)}) collective-permute-start(bf16[2,32,512]{2,1,0:T(8,128)(2,1)S(1)} %get-tuple-element.116.refs_25_), channel_id=1, source_target_pairs={{0,8},{4,12},{8,0},{12,4},{16,24},{20,28},{24,16},{28,20},{1,9},{5... | collective-permute-start | bytes 196616 | tf_op jit(solution)/shard_map/ppermute | solution.py:241
  88.5 8.2 %collective-permute-start.42 = (bf16[2,32,512]{2,1,0:T(8,128)(2,1)S(1)}, bf16[2,32,512]{2,1,0:T(8,128)(2,1)S(1)}, u32[]{:S(2)}, u32[]{:S(2)}) collective-permute-start(bf16[2,32,512]{2,1,0:T(8,128)(2,1)S(1)} %get-tuple-element.117.refs_26_), channel_id=1, source_target_pairs={{0,16},{4,20},{8,24},{12,28},{16,0},{20,4},{24,8},{28,12},{1,17},{... | collective-permute-start | bytes 196616 | tf_op jit(solution)/shard_map/ppermute | solution.py:241
  102.1 6.4 %collective-permute-start.55 = (bf16[2,32,512]{2,1,0:T(8,128)(2,1)S(1)}, bf16[2,32,512]{2,1,0:T(8,128)(2,1)S(1)}, u32[]{:S(2)}, u32[]{:S(2)}) collective-permute-start(bf16[2,32,512]{2,1,0:T(8,128)(2,1)S(1)} %get-tuple-element.97.refs_12_.refs_24_), channel_id=1, source_target_pairs={{0,2},{1,3},{2,0},{3,1},{4,6},{5,7},{6,4},{7,5},{8,10},{9,11},{10,... | collective-permute-start | bytes 196616 | tf_op jit(solution)/shard_map/ppermute | solution.py:165
  104.1 7.0 %collective-permute-start.53 = (bf16[2,32,512]{2,1,0:T(8,128)(2,1)S(1)}, bf16[2,32,512]{2,1,0:T(8,128)(2,1)S(1)}, u32[]{:S(2)}, u32[]{:S(2)}) collective-permute-start(bf16[2,32,512]{2,1,0:T(8,128)(2,1)S(1)} %get-tuple-element.97.refs_12_.refs_24_), channel_id=1, source_target_pairs={{0,24},{4,28},{8,16},{12,20},{16,8},{20,12},{24,0},{28,4},{1,25},{... | collective-permute-start | bytes 196616 | tf_op jit(solution)/shard_map/ppermute | solution.py:171
  116.8 6.1 %collective-permute-start.65 = (bf16[2,32,512]{2,1,0:T(8,128)(2,1)S(1)}, bf16[2,32,512]{2,1,0:T(8,128)(2,1)S(1)}, u32[]{:S(2)}, u32[]{:S(2)}) collective-permute-start(bf16[2,32,512]{2,1,0:T(8,128)(2,1)S(1)} %get-tuple-element.102), channel_id=1, source_target_pairs={{0,3},{1,2},{2,1},{3,0},{4,7},{5,6},{6,5},{7,4},{8,11},{9,10},{10,... | collective-permute-start | bytes 196616 | tf_op jit(solution)/shard_map/ppermute | solution.py:245
  118.3 7.1 %collective-permute-start.58 = (bf16[2,32,512]{2,1,0:T(8,128)(2,1)S(1)}, bf16[2,32,512]{2,1,0:T(8,128)(2,1)S(1)}, u32[]{:S(2)}, u32[]{:S(2)}) collective-permute-start(bf16[2,32,512]{2,1,0:T(8,128)(2,1)S(1)} %get-tuple-element.111.refs_35_), channel_id=1, source_target_pairs={{0,24},{4,28},{8,16},{12,20},{16,8},{20,12},{24,0},{28,4},{1,25},{... | collective-permute-start | bytes 196616 | tf_op jit(solution)/shard_map/ppermute | solution.py:241
  (51 other events, 318.0 us)

commit v4 on v3

--- a/solution.py
+++ b/solution.py
@@ -35,6 +35,18 @@
         table_ref[slots, i] = col
 
 
+def choose(index, low, high, do):
+    if high - low == 1:
+        do(low)
+        return
+    middle = (low + high) // 2
+    lax.cond(
+        index < middle,
+        lambda: choose(index, low, middle, do),
+        lambda: choose(index, middle, high, do),
+    )
+
+
 def pick(step, table_ref, s, old, new, put):
     live = table_ref[s, LIVE] == 1
     delay = table_ref[s, DELAY]
@@ -42,15 +54,10 @@
     def zero_dead(blocks):
         put([jnp.where(live, x, jnp.zeros_like(x)) for x in blocks])
 
-    for j in range(step):
-
-        @pl.when(delay == j)
-        def _(j=j):
-            zero_dead(new(step - 1 - j))
-
-    @pl.when(delay >= step)
-    def _():
-        zero_dead(old(delay - step))
+    def from_step(j):
+        zero_dead(new(step - 1 - j) if j < step else old(delay - step))
+
+    choose(jnp.minimum(delay, step), 0, step + 1, from_step)
 
 
 def turn_kernel(tile_ref, turned_ref):
@@ -110,18 +117,18 @@
             near_ref[s] = blocks[0]
 
         second = table_ref[s, SECOND]
-        for p in range(groups):
-
-            @pl.when(table_ref[s, PIECE] == p)
-            def _(s=s, p=p, second=second, put=put):
-                pick(
-                    step,
-                    table_ref,
-                    s,
-                    lambda d: [old[p][d, second]],
-                    lambda j: [new[j][p][second]],
-                    put,
-                )
+
+        def from_piece(p, s=s, second=second, put=put):
+            pick(
+                step,
+                table_ref,
+                s,
+                lambda d: [old[p][d, second]],
+                lambda j: [new[j][p][second]],
+                put,
+            )
+
+        choose(table_ref[s, PIECE], 0, groups, from_piece)
 
     for s in range(slots):
         sum_ref[table_ref[s, FIRST]] += jnp.dot(
@@ -227,7 +234,7 @@
     rows_of, near_of, results = [], [], []
     for step in range(STEPS):
         if step == 0:
-            cols_next, turned, table = lax.optimization_barrier((cols_next, turned, table))
+            cols_next, planes_next[-1], turned, table = lax.optimization_barrier((cols_next, planes_next[-1], turned, table))
         rows_of.append(cols_next)
         same, other = backward(step, rows_of[0], rows_of[1:])
         if step:

time: 129 us -> 126 us (0.977)
  Pallas kernels: 28.9 us -> 27 us
  waiting for transfers between devices: 21.3 us -> 19.9 us
    pallas_call x4, Pallas kernels: 11.7 us -> 10.2 us  [forward(): pl.pallas_call(functools.partial(forward_kernel, step, groups, cols), out...]
  transfers between devices with their start and end apart: 68 -> 68, of which waited for: 24 -> 24; matrix products, arithmetic and copies ran while one was open for 0% -> 0% of each run, Pallas kernels for 20% -> 19%
where the time goes in v4:
time: 126 us
  starting transfers between devices  71.1 us (56%)
  Pallas kernels  27 us (21%)
  waiting for transfers between devices  19.9 us (16%)
  local copies, waits for them, and re-layouts  5.29 us (4%)
  other arithmetic  2.49 us (2%)
    ppermute x12, starting transfers between devices, spread_planes(): got[k] = lax.ppermute(x, 'pairs', swapped(groups, CORES * k))  19.3 us
    ppermute x12, starting transfers between devices, shards(): lax.ppermute(sent[k], 'pairs', swapped(groups, CORES * k)).astype(F32)  17.7 us
    ppermute x12, starting transfers between devices, spread_cols(): got[k] = lax.ppermute(x, 'cols', swapped(cols, k))  15.7 us
    ppermute x12, starting transfers between devices, shards(): field += lax.ppermute(parts[k], 'cols', swapped(cols, k)).astype(F32)  14.2 us
    ppermute x12, waiting for transfers between devices, shards(): field += lax.ppermute(parts[k], 'cols', swapped(cols, k)).astype(F32)  10.9 us
    pallas_call x4, Pallas kernels, forward(): pl.pallas_call(functools.partial(forward_kernel, step, groups, cols), out...  10.2 us
    pallas_call x4, Pallas kernels, backward(): pl.pallas_call(functools.partial(backward_kernel, step, groups, cols), ou...  10.1 us
    pallas_call x1, Pallas kernels, shards(): pl.pallas_call(turn_kernel, out_shape=pltpu.VMEM((slots, width, rows), BF...  6.08 us
  transfers between devices with their start and end apart: 68, of which 24 were waited for; matrix products, arithmetic and copies ran while one was open for 0% of the time, Pallas kernels for 19%

profile of v4, /device:TPU:0, one launch (start us, length us, event | category | flops | bytes accessed | tf_op | source)
XLA Modules:
  0.0 126.1 jit_solution(16060836079650099703)
XLA Ops:
  1.1 4.0 %collective-permute-start.2 = (bf16[4,2,32,512]{3,2,1,0:T(8,128)(2,1)S(1)}, bf16[4,2,32,512]{3,2,1,0:T(8,128)(2,1)S(1)}, u32[]{:S(2)}, u32[]{:S(2)}) collective-permute-start(bf16[4,2,32,512]{3,2,1,0:T(8,128)(2,1)S(1)} %convert_element_type.208.refs_0_), channel_id=1, source_target_pairs={{0,3},{1,2},{2,1},{3,0},{4,7},{5,6},{6,5},{7,4},{8,11},{9,10},{10,... | collective-permute-start | bytes 786440 | tf_op jit(solution)/shard_map/ppermute | solution.py:172
  5.0 3.6 %collective-permute-start.3 = (bf16[4,2,32,512]{3,2,1,0:T(8,128)(2,1)S(1)}, bf16[4,2,32,512]{3,2,1,0:T(8,128)(2,1)S(1)}, u32[]{:S(2)}, u32[]{:S(2)}) collective-permute-start(bf16[4,2,32,512]{3,2,1,0:T(8,128)(2,1)S(1)} %convert_element_type.208.refs_0_), channel_id=1, source_target_pairs={{0,24},{4,28},{8,16},{12,20},{16,8},{20,12},{24,0},{28,4},{1,25},{... | collective-permute-start | bytes 786440 | tf_op jit(solution)/shard_map/ppermute | solution.py:178
  11.8 2.5 %collective-permute-start.9 = (bf16[4,2,32,512]{3,2,1,0:T(8,128)(2,1)S(1)}, bf16[4,2,32,512]{3,2,1,0:T(8,128)(2,1)S(1)}, u32[]{:S(2)}, u32[]{:S(2)}) collective-permute-start(bf16[4,2,32,512]{3,2,1,0:T(8,128)(2,1)S(1)} %convert_element_type.208.refs_0_), channel_id=1, source_target_pairs={{0,8},{4,12},{8,0},{12,4},{16,24},{20,28},{24,16},{28,20},{1,9},{5... | collective-permute-start | bytes 786440 | tf_op jit(solution)/shard_map/ppermute | solution.py:178
  14.3 4.6 %copy-done = bf16[6,2048,512]{2,1,0:T(8,128)(2,1)S(1)} copy-done((bf16[6,2048,512]{2,1,0:T(8,128)(2,1)S(1)}, bf16[6,2048,512]{2,1,0:T(8,128)(2,1)}, u32[]{:S(2)}) %copy-start) | copy-done | bytes 12582936
  18.9 6.1 %turn.1.turned_ref = bf16[6,512,2048]{2,1,0:T(8,128)(2,1)S(1)} custom-call(bf16[6,2048,512]{2,1,0:T(8,128)(2,1)S(1)} %copy-done), custom_call_target="tpu_custom_call" | custom-call | flops 402653184 | bytes 12582912 | tf_op jit(solution)/shard_map/turn/pallas_call | solution.py:225
  25.0 2.1 %backward0.1 = (f32[4,2,32,512]{3,2,1,0:T(8,128)S(1)}, bf16[4,2,32,512]{3,2,1,0:T(8,128)(2,1)S(1)}) custom-call(s32[7,5]{1,0:T(8,128)S(4)} %table.1.table_ref, bf16[6,2048,512]{2,1,0:T(8,128)(2,1)S(1)} %copy-done, bf16[4,2,32,512]{3,2,1,0:T(8,128)(2,1)S(1)} %convert_element_type.208.refs_0_, bf16[4,2,32,512]{3,2,1,0:T(8,128)(2,1)S(1)} %collective-permute-done.refs_1_, ...), custom_call_target="tpu_custom_call" | custom-call | flops 402653184 | bytes 12582912 | tf_op jit(solution)/shard_map/backward0/pallas_call | solution.py:185
  27.9 2.8 %collective-permute-done.11.refs_4_ = bf16[4,2,32,512]{3,2,1,0:T(8,128)(2,1)S(1)} collective-permute-done((bf16[4,2,32,512]{3,2,1,0:T(8,128)(2,1)S(1)}, bf16[4,2,32,512]{3,2,1,0:T(8,128)(2,1)S(1)}, u32[]{:S(2)}, u32[]{:S(2)}) %collective-permute-start.11) | collective-permute-done | bytes 262176 | tf_op jit(solution)/shard_map/ppermute | solution.py:178
  31.3 2.5 %collective-permute-start.5 = (bf16[2,32,512]{2,1,0:T(8,128)(2,1)S(1)}, bf16[2,32,512]{2,1,0:T(8,128)(2,1)S(1)}, u32[]{:S(2)}, u32[]{:S(2)}) collective-permute-start(bf16[2,32,512]{2,1,0:T(8,128)(2,1)S(1)} %get-tuple-element.125.refs_11_), channel_id=1, source_target_pairs={{0,24},{4,28},{8,16},{12,20},{16,8},{20,12},{24,0},{28,4},{1,25},{... | collective-permute-start | bytes 196616 | tf_op jit(solution)/shard_map/ppermute | solution.py:248
  35.7 2.5 %forward0.1 = (f32[2,32,512]{2,1,0:T(8,128)S(1)}, bf16[2,32,512]{2,1,0:T(8,128)(2,1)S(1)}, bf16[2,32,512]{2,1,0:T(8,128)(2,1)S(1)}, bf16[2,32,512]{2,1,0:T(8,128)(2,1)S(1)}) custom-call(s32[7,5]{1,0:T(8,128)S(4)} %table.1.table_ref, bf16[6,512,2048]{2,1,0:T(8,128)(2,1)S(1)} %turn.1.turned_ref, bf16[4,2,32,512]{3,2,1,0:T(8,128)(2,1)S(1)} %convert_element_type.208.refs_0_, ...), custom_call_target="tpu_custom_call" | custom-call | flops 402653184 | bytes 12582912 | tf_op jit(solution)/shard_map/forward0/pallas_call | solution.py:204
  48.3 2.5 %collective-permute-start.19 = (bf16[2,32,512]{2,1,0:T(8,128)(2,1)S(1)}, bf16[2,32,512]{2,1,0:T(8,128)(2,1)S(1)}, u32[]{:S(2)}, u32[]{:S(2)}) collective-permute-start(bf16[2,32,512]{2,1,0:T(8,128)(2,1)S(1)} %get-tuple-element.75.refs_4_.refs_8_), channel_id=1, source_target_pairs={{0,24},{4,28},{8,16},{12,20},{16,8},{20,12},{24,0},{28,4},{1,25},{... | collective-permute-start | bytes 196616 | tf_op jit(solution)/shard_map/ppermute | solution.py:178
  52.7 2.6 %backward1.1 = (f32[4,2,32,512]{3,2,1,0:T(8,128)S(1)}, bf16[4,2,32,512]{3,2,1,0:T(8,128)(2,1)S(1)}) custom-call(s32[7,5]{1,0:T(8,128)S(4)} %table.1.table_ref, bf16[6,2048,512]{2,1,0:T(8,128)(2,1)S(1)} %bitcast.59, bf16[4,2,32,512]{3,2,1,0:T(8,128)(2,1)S(1)} %convert_element_type.208.refs_0_, bf16[4,2,32,512]{3,2,1,0:T(8,128)(2,1)S(1)} %collective-permute-done.refs_1_, ...), custom_call_target="tpu_custom_call" | custom-call | flops 402653184 | bytes 12582912 | tf_op jit(solution)/shard_map/backward1/pallas_call | solution.py:185
  57.5 2.4 %collective-permute-start.24 = (bf16[2,32,512]{2,1,0:T(8,128)(2,1)S(1)}, bf16[2,32,512]{2,1,0:T(8,128)(2,1)S(1)}, u32[]{:S(2)}, u32[]{:S(2)}) collective-permute-start(bf16[2,32,512]{2,1,0:T(8,128)(2,1)S(1)} %get-tuple-element.121.refs_19_), channel_id=1, source_target_pairs={{0,24},{4,28},{8,16},{12,20},{16,8},{20,12},{24,0},{28,4},{1,25},{... | collective-permute-start | bytes 196616 | tf_op jit(solution)/shard_map/ppermute | solution.py:248
  62.0 2.6 %forward1.1 = (f32[2,32,512]{2,1,0:T(8,128)S(1)}, bf16[2,32,512]{2,1,0:T(8,128)(2,1)S(1)}, bf16[2,32,512]{2,1,0:T(8,128)(2,1)S(1)}, bf16[2,32,512]{2,1,0:T(8,128)(2,1)S(1)}) custom-call(s32[7,5]{1,0:T(8,128)S(4)} %table.1.table_ref, bf16[6,512,2048]{2,1,0:T(8,128)(2,1)S(1)} %turn.1.turned_ref, bf16[4,2,32,512]{3,2,1,0:T(8,128)(2,1)S(1)} %convert_element_type.208.refs_0_, ...), custom_call_target="tpu_custom_call" | custom-call | flops 402653184 | bytes 12582912 | tf_op jit(solution)/shard_map/forward1/pallas_call | solution.py:204
  68.1 2.2 %collective-permute-done.31 = bf16[2,32,512]{2,1,0:T(8,128)(2,1)S(1)} collective-permute-done((bf16[2,32,512]{2,1,0:T(8,128)(2,1)S(1)}, bf16[2,32,512]{2,1,0:T(8,128)(2,1)S(1)}, u32[]{:S(2)}, u32[]{:S(2)}) %collective-permute-start.31) | collective-permute-done | bytes 65568 | tf_op jit(solution)/shard_map/ppermute | solution.py:252
  75.5 2.3 %collective-permute-start.36 = (bf16[2,32,512]{2,1,0:T(8,128)(2,1)S(1)}, bf16[2,32,512]{2,1,0:T(8,128)(2,1)S(1)}, u32[]{:S(2)}, u32[]{:S(2)}) collective-permute-start(bf16[2,32,512]{2,1,0:T(8,128)(2,1)S(1)} %get-tuple-element.87.refs_8_.refs_16_), channel_id=1, source_target_pairs={{0,24},{4,28},{8,16},{12,20},{16,8},{20,12},{24,0},{28,4},{1,25},{... | collective-permute-start | bytes 196616 | tf_op jit(solution)/shard_map/ppermute | solution.py:178
  77.8 2.1 %collective-permute-start.34 = (bf16[2,32,512]{2,1,0:T(8,128)(2,1)S(1)}, bf16[2,32,512]{2,1,0:T(8,128)(2,1)S(1)}, u32[]{:S(2)}, u32[]{:S(2)}) collective-permute-start(bf16[2,32,512]{2,1,0:T(8,128)(2,1)S(1)} %get-tuple-element.87.refs_8_.refs_16_), channel_id=1, source_target_pairs={{0,8},{4,12},{8,0},{12,4},{16,24},{20,28},{24,16},{28,20},{1,9},{5... | collective-permute-start | bytes 196616 | tf_op jit(solution)/shard_map/ppermute | solution.py:178
  79.9 2.8 %backward2.1 = (f32[4,2,32,512]{3,2,1,0:T(8,128)S(1)}, bf16[4,2,32,512]{3,2,1,0:T(8,128)(2,1)S(1)}) custom-call(s32[7,5]{1,0:T(8,128)S(4)} %table.1.table_ref, bf16[6,2048,512]{2,1,0:T(8,128)(2,1)S(1)} %bitcast.59, bf16[4,2,32,512]{3,2,1,0:T(8,128)(2,1)S(1)} %convert_element_type.208.refs_0_, bf16[4,2,32,512]{3,2,1,0:T(8,128)(2,1)S(1)} %collective-permute-done.refs_1_, ...), custom_call_target="tpu_custom_call" | custom-call | flops 402653184 | bytes 12582912 | tf_op jit(solution)/shard_map/backward2/pallas_call | solution.py:185
  84.6 2.4 %collective-permute-start.41 = (bf16[2,32,512]{2,1,0:T(8,128)(2,1)S(1)}, bf16[2,32,512]{2,1,0:T(8,128)(2,1)S(1)}, u32[]{:S(2)}, u32[]{:S(2)}) collective-permute-start(bf16[2,32,512]{2,1,0:T(8,128)(2,1)S(1)} %get-tuple-element.117.refs_27_), channel_id=1, source_target_pairs={{0,24},{4,28},{8,16},{12,20},{16,8},{20,12},{24,0},{28,4},{1,25},{... | collective-permute-start | bytes 196616 | tf_op jit(solution)/shard_map/ppermute | solution.py:248
  89.0 2.6 %forward2.1 = (f32[2,32,512]{2,1,0:T(8,128)S(1)}, bf16[2,32,512]{2,1,0:T(8,128)(2,1)S(1)}, bf16[2,32,512]{2,1,0:T(8,128)(2,1)S(1)}, bf16[2,32,512]{2,1,0:T(8,128)(2,1)S(1)}) custom-call(s32[7,5]{1,0:T(8,128)S(4)} %table.1.table_ref, bf16[6,512,2048]{2,1,0:T(8,128)(2,1)S(1)} %turn.1.turned_ref, bf16[4,2,32,512]{3,2,1,0:T(8,128)(2,1)S(1)} %convert_element_type.208.refs_0_, ...), custom_call_target="tpu_custom_call" | custom-call | flops 402653184 | bytes 12582912 | tf_op jit(solution)/shard_map/forward2/pallas_call | solution.py:204
  101.6 2.3 %collective-permute-start.53 = (bf16[2,32,512]{2,1,0:T(8,128)(2,1)S(1)}, bf16[2,32,512]{2,1,0:T(8,128)(2,1)S(1)}, u32[]{:S(2)}, u32[]{:S(2)}) collective-permute-start(bf16[2,32,512]{2,1,0:T(8,128)(2,1)S(1)} %get-tuple-element.99.refs_12_.refs_24_), channel_id=1, source_target_pairs={{0,24},{4,28},{8,16},{12,20},{16,8},{20,12},{24,0},{28,4},{1,25},{... | collective-permute-start | bytes 196616 | tf_op jit(solution)/shard_map/ppermute | solution.py:178
  103.9 2.1 %collective-permute-start.51 = (bf16[2,32,512]{2,1,0:T(8,128)(2,1)S(1)}, bf16[2,32,512]{2,1,0:T(8,128)(2,1)S(1)}, u32[]{:S(2)}, u32[]{:S(2)}) collective-permute-start(bf16[2,32,512]{2,1,0:T(8,128)(2,1)S(1)} %get-tuple-element.99.refs_12_.refs_24_), channel_id=1, source_target_pairs={{0,8},{4,12},{8,0},{12,4},{16,24},{20,28},{24,16},{28,20},{1,9},{5... | collective-permute-start | bytes 196616 | tf_op jit(solution)/shard_map/ppermute | solution.py:178
  106.0 2.6 %backward3.1 = (f32[4,2,32,512]{3,2,1,0:T(8,128)S(1)}, bf16[4,2,32,512]{3,2,1,0:T(8,128)(2,1)S(1)}) custom-call(s32[7,5]{1,0:T(8,128)S(4)} %table.1.table_ref, bf16[6,2048,512]{2,1,0:T(8,128)(2,1)S(1)} %bitcast.59, bf16[4,2,32,512]{3,2,1,0:T(8,128)(2,1)S(1)} %convert_element_type.208.refs_0_, bf16[4,2,32,512]{3,2,1,0:T(8,128)(2,1)S(1)} %collective-permute-done.refs_1_, ...), custom_call_target="tpu_custom_call" | custom-call | flops 402653184 | bytes 12582912 | tf_op jit(solution)/shard_map/backward3/pallas_call | solution.py:185
  111.3 2.6 %forward3.1 = (f32[2,32,512]{2,1,0:T(8,128)S(1)}, bf16[2,32,512]{2,1,0:T(8,128)(2,1)S(1)}, bf16[2,32,512]{2,1,0:T(8,128)(2,1)S(1)}, bf16[2,32,512]{2,1,0:T(8,128)(2,1)S(1)}) custom-call(s32[7,5]{1,0:T(8,128)S(4)} %table.1.table_ref, bf16[6,512,2048]{2,1,0:T(8,128)(2,1)S(1)} %turn.1.turned_ref, bf16[4,2,32,512]{3,2,1,0:T(8,128)(2,1)S(1)} %convert_element_type.208.refs_0_, ...), custom_call_target="tpu_custom_call" | custom-call | flops 402653184 | bytes 12582912 | tf_op jit(solution)/shard_map/forward3/pallas_call | solution.py:204
  115.4 2.3 %collective-permute-start.58 = (bf16[2,32,512]{2,1,0:T(8,128)(2,1)S(1)}, bf16[2,32,512]{2,1,0:T(8,128)(2,1)S(1)}, u32[]{:S(2)}, u32[]{:S(2)}) collective-permute-start(bf16[2,32,512]{2,1,0:T(8,128)(2,1)S(1)} %get-tuple-element.113.refs_35_), channel_id=1, source_target_pairs={{0,24},{4,28},{8,16},{12,20},{16,8},{20,12},{24,0},{28,4},{1,25},{... | collective-permute-start | bytes 196616 | tf_op jit(solution)/shard_map/ppermute | solution.py:248
  (147 shorter events, 58.9 us)
Async XLA Ops:
  1.1 10.7 %collective-permute-start.2 = (bf16[4,2,32,512]{3,2,1,0:T(8,128)(2,1)S(1)}, bf16[4,2,32,512]{3,2,1,0:T(8,128)(2,1)S(1)}, u32[]{:S(2)}, u32[]{:S(2)}) collective-permute-start(bf16[4,2,32,512]{3,2,1,0:T(8,128)(2,1)S(1)} %convert_element_type.208.refs_0_), channel_id=1, source_target_pairs={{0,3},{1,2},{2,1},{3,0},{4,7},{5,6},{6,5},{7,4},{8,11},{9,10},{10,... | collective-permute-start | bytes 786440 | tf_op jit(solution)/shard_map/ppermute | solution.py:172
  5.0 20.0 %collective-permute-start.3 = (bf16[4,2,32,512]{3,2,1,0:T(8,128)(2,1)S(1)}, bf16[4,2,32,512]{3,2,1,0:T(8,128)(2,1)S(1)}, u32[]{:S(2)}, u32[]{:S(2)}) collective-permute-start(bf16[4,2,32,512]{3,2,1,0:T(8,128)(2,1)S(1)} %convert_element_type.208.refs_0_), channel_id=1, source_target_pairs={{0,24},{4,28},{8,16},{12,20},{16,8},{20,12},{24,0},{28,4},{1,25},{... | collective-permute-start | bytes 786440 | tf_op jit(solution)/shard_map/ppermute | solution.py:178
  8.6 16.4 %collective-permute-start.1 = (bf16[4,2,32,512]{3,2,1,0:T(8,128)(2,1)S(1)}, bf16[4,2,32,512]{3,2,1,0:T(8,128)(2,1)S(1)}, u32[]{:S(2)}, u32[]{:S(2)}) collective-permute-start(bf16[4,2,32,512]{3,2,1,0:T(8,128)(2,1)S(1)} %convert_element_type.208.refs_0_), channel_id=1, source_target_pairs={{0,2},{1,3},{2,0},{3,1},{4,6},{5,7},{6,4},{7,5},{8,10},{9,11},{10,... | collective-permute-start | bytes 786440 | tf_op jit(solution)/shard_map/ppermute | solution.py:172
  9.1 15.9 %collective-permute-start = (bf16[4,2,32,512]{3,2,1,0:T(8,128)(2,1)S(1)}, bf16[4,2,32,512]{3,2,1,0:T(8,128)(2,1)S(1)}, u32[]{:S(2)}, u32[]{:S(2)}) collective-permute-start(bf16[4,2,32,512]{3,2,1,0:T(8,128)(2,1)S(1)} %convert_element_type.208.refs_0_), channel_id=1, source_target_pairs={{0,1},{1,0},{2,3},{3,2},{4,5},{5,4},{6,7},{7,6},{8,9},{9,8},{10,11... | collective-permute-start | bytes 786440 | tf_op jit(solution)/shard_map/ppermute | solution.py:172
  9.7 21.0 %collective-permute-start.11 = (bf16[4,2,32,512]{3,2,1,0:T(8,128)(2,1)S(1)}, bf16[4,2,32,512]{3,2,1,0:T(8,128)(2,1)S(1)}, u32[]{:S(2)}, u32[]{:S(2)}) collective-permute-start(bf16[4,2,32,512]{3,2,1,0:T(8,128)(2,1)S(1)} %convert_element_type.208.refs_0_), channel_id=1, source_target_pairs={{0,16},{4,20},{8,24},{12,28},{16,0},{20,4},{24,8},{28,12},{1,17},{... | collective-permute-start | bytes 786440 | tf_op jit(solution)/shard_map/ppermute | solution.py:178
  11.8 18.9 %collective-permute-start.9 = (bf16[4,2,32,512]{3,2,1,0:T(8,128)(2,1)S(1)}, bf16[4,2,32,512]{3,2,1,0:T(8,128)(2,1)S(1)}, u32[]{:S(2)}, u32[]{:S(2)}) collective-permute-start(bf16[4,2,32,512]{3,2,1,0:T(8,128)(2,1)S(1)} %convert_element_type.208.refs_0_), channel_id=1, source_target_pairs={{0,8},{4,12},{8,0},{12,4},{16,24},{20,28},{24,16},{28,20},{1,9},{5... | collective-permute-start | bytes 786440 | tf_op jit(solution)/shard_map/ppermute | solution.py:178
  27.3 6.5 %collective-permute-start.8 = (bf16[4,2,32,512]{3,2,1,0:T(8,128)(2,1)S(1)}, bf16[4,2,32,512]{3,2,1,0:T(8,128)(2,1)S(1)}, u32[]{:S(2)}, u32[]{:S(2)}) collective-permute-start(bf16[4,2,32,512]{3,2,1,0:T(8,128)(2,1)S(1)} %convert_element_type.208.refs_0_), channel_id=1, source_target_pairs={{0,4},{4,0},{8,12},{12,8},{16,20},{20,16},{24,28},{28,24},{1,5},{5... | collective-permute-start | bytes 786440 | tf_op jit(solution)/shard_map/ppermute | solution.py:182
  27.8 7.9 %collective-permute-start.13 = (bf16[4,2,32,512]{3,2,1,0:T(8,128)(2,1)S(1)}, bf16[4,2,32,512]{3,2,1,0:T(8,128)(2,1)S(1)}, u32[]{:S(2)}, u32[]{:S(2)}) collective-permute-start(bf16[4,2,32,512]{3,2,1,0:T(8,128)(2,1)S(1)} %collective-permute-done.3.refs_6_), channel_id=1, source_target_pairs={{0,4},{4,0},{8,12},{12,8},{16,20},{20,16},{24,28},{28,24},{1,5},{5... | collective-permute-start | bytes 786440 | tf_op jit(solution)/shard_map/ppermute | solution.py:182
  31.3 9.1 %collective-permute-start.5 = (bf16[2,32,512]{2,1,0:T(8,128)(2,1)S(1)}, bf16[2,32,512]{2,1,0:T(8,128)(2,1)S(1)}, u32[]{:S(2)}, u32[]{:S(2)}) collective-permute-start(bf16[2,32,512]{2,1,0:T(8,128)(2,1)S(1)} %get-tuple-element.125.refs_11_), channel_id=1, source_target_pairs={{0,24},{4,28},{8,16},{12,20},{16,8},{20,12},{24,0},{28,4},{1,25},{... | collective-permute-start | bytes 196616 | tf_op jit(solution)/shard_map/ppermute | solution.py:248
  33.8 8.0 %collective-permute-start.7 = (bf16[2,32,512]{2,1,0:T(8,128)(2,1)S(1)}, bf16[2,32,512]{2,1,0:T(8,128)(2,1)S(1)}, u32[]{:S(2)}, u32[]{:S(2)}) collective-permute-start(bf16[2,32,512]{2,1,0:T(8,128)(2,1)S(1)} %get-tuple-element.126.refs_9_), channel_id=1, source_target_pairs={{0,8},{4,12},{8,0},{12,4},{16,24},{20,28},{24,16},{28,20},{1,9},{5... | collective-permute-start | bytes 196616 | tf_op jit(solution)/shard_map/ppermute | solution.py:248
  33.8 8.0 %collective-permute-start.6 = (bf16[2,32,512]{2,1,0:T(8,128)(2,1)S(1)}, bf16[2,32,512]{2,1,0:T(8,128)(2,1)S(1)}, u32[]{:S(2)}, u32[]{:S(2)}) collective-permute-start(bf16[2,32,512]{2,1,0:T(8,128)(2,1)S(1)} %get-tuple-element.127.refs_10_), channel_id=1, source_target_pairs={{0,16},{4,20},{8,24},{12,28},{16,0},{20,4},{24,8},{28,12},{1,17},{... | collective-permute-start | bytes 196616 | tf_op jit(solution)/shard_map/ppermute | solution.py:248
  46.2 6.5 %collective-permute-start.21 = (bf16[2,32,512]{2,1,0:T(8,128)(2,1)S(1)}, bf16[2,32,512]{2,1,0:T(8,128)(2,1)S(1)}, u32[]{:S(2)}, u32[]{:S(2)}) collective-permute-start(bf16[2,32,512]{2,1,0:T(8,128)(2,1)S(1)} %get-tuple-element.75.refs_4_.refs_8_), channel_id=1, source_target_pairs={{0,2},{1,3},{2,0},{3,1},{4,6},{5,7},{6,4},{7,5},{8,10},{9,11},{10,... | collective-permute-start | bytes 196616 | tf_op jit(solution)/shard_map/ppermute | solution.py:172
  48.3 7.0 %collective-permute-start.19 = (bf16[2,32,512]{2,1,0:T(8,128)(2,1)S(1)}, bf16[2,32,512]{2,1,0:T(8,128)(2,1)S(1)}, u32[]{:S(2)}, u32[]{:S(2)}) collective-permute-start(bf16[2,32,512]{2,1,0:T(8,128)(2,1)S(1)} %get-tuple-element.75.refs_4_.refs_8_), channel_id=1, source_target_pairs={{0,24},{4,28},{8,16},{12,20},{16,8},{20,12},{24,0},{28,4},{1,25},{... | collective-permute-start | bytes 196616 | tf_op jit(solution)/shard_map/ppermute | solution.py:178
  57.5 10.1 %collective-permute-start.24 = (bf16[2,32,512]{2,1,0:T(8,128)(2,1)S(1)}, bf16[2,32,512]{2,1,0:T(8,128)(2,1)S(1)}, u32[]{:S(2)}, u32[]{:S(2)}) collective-permute-start(bf16[2,32,512]{2,1,0:T(8,128)(2,1)S(1)} %get-tuple-element.121.refs_19_), channel_id=1, source_target_pairs={{0,24},{4,28},{8,16},{12,20},{16,8},{20,12},{24,0},{28,4},{1,25},{... | collective-permute-start | bytes 196616 | tf_op jit(solution)/shard_map/ppermute | solution.py:248
  59.9 8.2 %collective-permute-start.26 = (bf16[2,32,512]{2,1,0:T(8,128)(2,1)S(1)}, bf16[2,32,512]{2,1,0:T(8,128)(2,1)S(1)}, u32[]{:S(2)}, u32[]{:S(2)}) collective-permute-start(bf16[2,32,512]{2,1,0:T(8,128)(2,1)S(1)} %get-tuple-element.122.refs_17_), channel_id=1, source_target_pairs={{0,8},{4,12},{8,0},{12,4},{16,24},{20,28},{24,16},{28,20},{1,9},{5... | collective-permute-start | bytes 196616 | tf_op jit(solution)/shard_map/ppermute | solution.py:248
  60.2 7.9 %collective-permute-start.25 = (bf16[2,32,512]{2,1,0:T(8,128)(2,1)S(1)}, bf16[2,32,512]{2,1,0:T(8,128)(2,1)S(1)}, u32[]{:S(2)}, u32[]{:S(2)}) collective-permute-start(bf16[2,32,512]{2,1,0:T(8,128)(2,1)S(1)} %get-tuple-element.123.refs_18_), channel_id=1, source_target_pairs={{0,16},{4,20},{8,24},{12,28},{16,0},{20,4},{24,8},{28,12},{1,17},{... | collective-permute-start | bytes 196616 | tf_op jit(solution)/shard_map/ppermute | solution.py:248
  72.5 7.4 %collective-permute-start.38 = (bf16[2,32,512]{2,1,0:T(8,128)(2,1)S(1)}, bf16[2,32,512]{2,1,0:T(8,128)(2,1)S(1)}, u32[]{:S(2)}, u32[]{:S(2)}) collective-permute-start(bf16[2,32,512]{2,1,0:T(8,128)(2,1)S(1)} %get-tuple-element.87.refs_8_.refs_16_), channel_id=1, source_target_pairs={{0,2},{1,3},{2,0},{3,1},{4,6},{5,7},{6,4},{7,5},{8,10},{9,11},{10,... | collective-permute-start | bytes 196616 | tf_op jit(solution)/shard_map/ppermute | solution.py:172
  75.5 7.2 %collective-permute-start.36 = (bf16[2,32,512]{2,1,0:T(8,128)(2,1)S(1)}, bf16[2,32,512]{2,1,0:T(8,128)(2,1)S(1)}, u32[]{:S(2)}, u32[]{:S(2)}) collective-permute-start(bf16[2,32,512]{2,1,0:T(8,128)(2,1)S(1)} %get-tuple-element.87.refs_8_.refs_16_), channel_id=1, source_target_pairs={{0,24},{4,28},{8,16},{12,20},{16,8},{20,12},{24,0},{28,4},{1,25},{... | collective-permute-start | bytes 196616 | tf_op jit(solution)/shard_map/ppermute | solution.py:178
  84.6 9.1 %collective-permute-start.41 = (bf16[2,32,512]{2,1,0:T(8,128)(2,1)S(1)}, bf16[2,32,512]{2,1,0:T(8,128)(2,1)S(1)}, u32[]{:S(2)}, u32[]{:S(2)}) collective-permute-start(bf16[2,32,512]{2,1,0:T(8,128)(2,1)S(1)} %get-tuple-element.117.refs_27_), channel_id=1, source_target_pairs={{0,24},{4,28},{8,16},{12,20},{16,8},{20,12},{24,0},{28,4},{1,25},{... | collective-permute-start | bytes 196616 | tf_op jit(solution)/shard_map/ppermute | solution.py:248
  86.9 8.2 %collective-permute-start.43 = (bf16[2,32,512]{2,1,0:T(8,128)(2,1)S(1)}, bf16[2,32,512]{2,1,0:T(8,128)(2,1)S(1)}, u32[]{:S(2)}, u32[]{:S(2)}) collective-permute-start(bf16[2,32,512]{2,1,0:T(8,128)(2,1)S(1)} %get-tuple-element.118.refs_25_), channel_id=1, source_target_pairs={{0,8},{4,12},{8,0},{12,4},{16,24},{20,28},{24,16},{28,20},{1,9},{5... | collective-permute-start | bytes 196616 | tf_op jit(solution)/shard_map/ppermute | solution.py:248
  87.2 7.9 %collective-permute-start.42 = (bf16[2,32,512]{2,1,0:T(8,128)(2,1)S(1)}, bf16[2,32,512]{2,1,0:T(8,128)(2,1)S(1)}, u32[]{:S(2)}, u32[]{:S(2)}) collective-permute-start(bf16[2,32,512]{2,1,0:T(8,128)(2,1)S(1)} %get-tuple-element.119.refs_26_), channel_id=1, source_target_pairs={{0,16},{4,20},{8,24},{12,28},{16,0},{20,4},{24,8},{28,12},{1,17},{... | collective-permute-start | bytes 196616 | tf_op jit(solution)/shard_map/ppermute | solution.py:248
  99.5 6.4 %collective-permute-start.55 = (bf16[2,32,512]{2,1,0:T(8,128)(2,1)S(1)}, bf16[2,32,512]{2,1,0:T(8,128)(2,1)S(1)}, u32[]{:S(2)}, u32[]{:S(2)}) collective-permute-start(bf16[2,32,512]{2,1,0:T(8,128)(2,1)S(1)} %get-tuple-element.99.refs_12_.refs_24_), channel_id=1, source_target_pairs={{0,2},{1,3},{2,0},{3,1},{4,6},{5,7},{6,4},{7,5},{8,10},{9,11},{10,... | collective-permute-start | bytes 196616 | tf_op jit(solution)/shard_map/ppermute | solution.py:172
  101.6 7.0 %collective-permute-start.53 = (bf16[2,32,512]{2,1,0:T(8,128)(2,1)S(1)}, bf16[2,32,512]{2,1,0:T(8,128)(2,1)S(1)}, u32[]{:S(2)}, u32[]{:S(2)}) collective-permute-start(bf16[2,32,512]{2,1,0:T(8,128)(2,1)S(1)} %get-tuple-element.99.refs_12_.refs_24_), channel_id=1, source_target_pairs={{0,24},{4,28},{8,16},{12,20},{16,8},{20,12},{24,0},{28,4},{1,25},{... | collective-permute-start | bytes 196616 | tf_op jit(solution)/shard_map/ppermute | solution.py:178
  115.4 8.1 %collective-permute-start.58 = (bf16[2,32,512]{2,1,0:T(8,128)(2,1)S(1)}, bf16[2,32,512]{2,1,0:T(8,128)(2,1)S(1)}, u32[]{:S(2)}, u32[]{:S(2)}) collective-permute-start(bf16[2,32,512]{2,1,0:T(8,128)(2,1)S(1)} %get-tuple-element.113.refs_35_), channel_id=1, source_target_pairs={{0,24},{4,28},{8,16},{12,20},{16,8},{20,12},{24,0},{28,4},{1,25},{... | collective-permute-start | bytes 196616 | tf_op jit(solution)/shard_map/ppermute | solution.py:248
  (51 other events, 308.4 us)

commit v5 on v4

--- a/solution.py
+++ b/solution.py
@@ -105,8 +105,12 @@
 
 
 def forward_kernel(step, groups, cols, table_ref, turned_ref, *refs):
-    old = refs[:groups]
-    new = [refs[groups * (1 + j) : groups * (2 + j)] for j in range(step)]
+    planes = groups // CORES
+    old, new = refs[:groups], []
+    for j in range(step):
+        first = groups + (planes + 1) * j
+        mates = refs[first + planes]
+        new.append([r for k in range(planes) for r in (refs[first + k], mates.at[k])])
     outs, near_ref, sum_ref = refs[-2 - cols : -2], refs[-2], refs[-1]
     slots, width, _ = turned_ref.shape
     col = table_ref[slots, 0]
@@ -206,7 +210,7 @@
             out_shape=[jax.ShapeDtypeStruct(block, F32)]
             + [jax.ShapeDtypeStruct(block, BF16)] * (cols - 1),
             in_specs=[smem]
-            + [vmem] * (1 + groups * (1 + step))
+            + [vmem] * (1 + groups + (planes + 1) * step)
             + [anywhere] * len(after),
             out_specs=[vmem] * cols,
             scratch_shapes=[
@@ -234,13 +238,17 @@
     rows_of, near_of, results = [], [], []
     for step in range(STEPS):
         if step == 0:
-            cols_next, planes_next[-1], turned, table = lax.optimization_barrier((cols_next, planes_next[-1], turned, table))
+            cols_next, planes_next[-2], turned, table = lax.optimization_barrier((cols_next, planes_next[-2], turned, table))
         rows_of.append(cols_next)
         same, other = backward(step, rows_of[0], rows_of[1:])
         if step:
             planes_next, same, other = lax.optimization_barrier((planes_next, same, other))
         mate = lax.ppermute(other, "pairs", swapped(groups, 1))
-        near_of.append(spread_cores(planes_next))
+        if step == 0:
+            near_of.append(spread_cores(planes_next))
+        else:
+            mates = lax.ppermute(jnp.stack(planes_next), "pairs", swapped(groups, 1))
+            near_of.append([*planes_next, mates])
         sent = [same[k] + mate[k].astype(F32) for k in range(planes)]
         sent[1:] = [x.astype(BF16) for x in sent[1:]]
         field = sent[0]

time: 126 us -> 126 us (level)
  starting transfers between devices: 71.1 us -> 69.8 us
    ppermute x16 -> x4, starting transfers between devices: 4.15 us -> 1.09 us  [spread_cores(): lax.ppermute(x, 'pairs', swapped(groups, 1))]
    ppermute x0 -> x3, starting transfers between devices: none -> 1.71 us  [shards(): mates = lax.ppermute(jnp.stack(planes_next), 'pairs', swapped(groups, 1))]
    ppermute x4, waiting for transfers between devices: 1.53 us -> 3.19 us  [shards(): mate = lax.ppermute(other, 'pairs', swapped(groups, 1))]
  transfers between devices with their start and end apart: 68 -> 59, of which waited for: 24 -> 22; matrix products, arithmetic and copies ran while one was open for 0% -> 0% of each run, Pallas kernels for 19% -> 20%
where the time goes in v5:
time: 126 us; the launch traced here: 125 us
  starting transfers between devices  69.8 us (55%)
  Pallas kernels  27.1 us (22%)
  waiting for transfers between devices  20.4 us (16%)
  local copies, waits for them, and re-layouts  5.29 us (4%)
  other arithmetic  2.6 us (2%)
    ppermute x12, starting transfers between devices, spread_planes(): got[k] = lax.ppermute(x, 'pairs', swapped(groups, CORES * k))  19.1 us
    ppermute x12, starting transfers between devices, shards(): lax.ppermute(sent[k], 'pairs', swapped(groups, CORES * k)).astype(F32)  18 us
    ppermute x12, starting transfers between devices, spread_cols(): got[k] = lax.ppermute(x, 'cols', swapped(cols, k))  15.7 us
    ppermute x12, starting transfers between devices, shards(): field += lax.ppermute(parts[k], 'cols', swapped(cols, k)).astype(F32)  14.2 us
    ppermute x12, waiting for transfers between devices, shards(): field += lax.ppermute(parts[k], 'cols', swapped(cols, k)).astype(F32)  10.5 us
    pallas_call x4, Pallas kernels, forward(): pl.pallas_call(functools.partial(forward_kernel, step, groups, cols), out...  10.3 us
    pallas_call x4, Pallas kernels, backward(): pl.pallas_call(functools.partial(backward_kernel, step, groups, cols), ou...  10.1 us
    pallas_call x1, Pallas kernels, shards(): pl.pallas_call(turn_kernel, out_shape=pltpu.VMEM((slots, width, rows), BF...  6.08 us
  transfers between devices with their start and end apart: 59, of which 22 were waited for; matrix products, arithmetic and copies ran while one was open for 0% of the time, Pallas kernels for 20%

profile of v5, /device:TPU:0, one launch (start us, length us, event | category | flops | bytes accessed | tf_op | source)
XLA Modules:
  0.0 125.5 jit_solution(2566905413879725478)
XLA Ops:
  1.1 4.0 %collective-permute-start.2 = (bf16[4,2,32,512]{3,2,1,0:T(8,128)(2,1)S(1)}, bf16[4,2,32,512]{3,2,1,0:T(8,128)(2,1)S(1)}, u32[]{:S(2)}, u32[]{:S(2)}) collective-permute-start(bf16[4,2,32,512]{3,2,1,0:T(8,128)(2,1)S(1)} %convert_element_type.208.refs_0_), channel_id=1, source_target_pairs={{0,3},{1,2},{2,1},{3,0},{4,7},{5,6},{6,5},{7,4},{8,11},{9,10},{10,... | collective-permute-start | bytes 786440 | tf_op jit(solution)/shard_map/ppermute | solution.py:176
  5.0 2.6 %collective-permute-start.3 = (bf16[4,2,32,512]{3,2,1,0:T(8,128)(2,1)S(1)}, bf16[4,2,32,512]{3,2,1,0:T(8,128)(2,1)S(1)}, u32[]{:S(2)}, u32[]{:S(2)}) collective-permute-start(bf16[4,2,32,512]{3,2,1,0:T(8,128)(2,1)S(1)} %convert_element_type.208.refs_0_), channel_id=1, source_target_pairs={{0,16},{4,20},{8,24},{12,28},{16,0},{20,4},{24,8},{28,12},{1,17},{... | collective-permute-start | bytes 786440 | tf_op jit(solution)/shard_map/ppermute | solution.py:182
  11.9 2.0 %collective-permute-start.9 = (bf16[4,2,32,512]{3,2,1,0:T(8,128)(2,1)S(1)}, bf16[4,2,32,512]{3,2,1,0:T(8,128)(2,1)S(1)}, u32[]{:S(2)}, u32[]{:S(2)}) collective-permute-start(bf16[4,2,32,512]{3,2,1,0:T(8,128)(2,1)S(1)} %convert_element_type.208.refs_0_), channel_id=1, source_target_pairs={{0,8},{4,12},{8,0},{12,4},{16,24},{20,28},{24,16},{28,20},{1,9},{5... | collective-permute-start | bytes 786440 | tf_op jit(solution)/shard_map/ppermute | solution.py:182
  13.9 4.6 %copy-done = bf16[6,2048,512]{2,1,0:T(8,128)(2,1)S(1)} copy-done((bf16[6,2048,512]{2,1,0:T(8,128)(2,1)S(1)}, bf16[6,2048,512]{2,1,0:T(8,128)(2,1)}, u32[]{:S(2)}) %copy-start) | copy-done | bytes 12582936
  18.5 6.1 %turn.1.turned_ref = bf16[6,512,2048]{2,1,0:T(8,128)(2,1)S(1)} custom-call(bf16[6,2048,512]{2,1,0:T(8,128)(2,1)S(1)} %copy-done), custom_call_target="tpu_custom_call" | custom-call | flops 402653184 | bytes 12582912 | tf_op jit(solution)/shard_map/turn/pallas_call | solution.py:229
  26.2 2.1 %backward0.1 = (f32[4,2,32,512]{3,2,1,0:T(8,128)S(1)}, bf16[4,2,32,512]{3,2,1,0:T(8,128)(2,1)S(1)}) custom-call(s32[7,5]{1,0:T(8,128)S(4)} %table.1.table_ref, bf16[6,2048,512]{2,1,0:T(8,128)(2,1)S(1)} %copy-done, bf16[4,2,32,512]{3,2,1,0:T(8,128)(2,1)S(1)} %convert_element_type.208.refs_0_, bf16[4,2,32,512]{3,2,1,0:T(8,128)(2,1)S(1)} %collective-permute-done.refs_1_, ...), custom_call_target="tpu_custom_call" | custom-call | flops 402653184 | bytes 12582912 | tf_op jit(solution)/shard_map/backward0/pallas_call | solution.py:189
  30.0 3.2 %collective-permute-start.5 = (bf16[2,32,512]{2,1,0:T(8,128)(2,1)S(1)}, bf16[2,32,512]{2,1,0:T(8,128)(2,1)S(1)}, u32[]{:S(2)}, u32[]{:S(2)}) collective-permute-start(bf16[2,32,512]{2,1,0:T(8,128)(2,1)S(1)} %get-tuple-element.125.refs_11_), channel_id=1, source_target_pairs={{0,24},{4,28},{8,16},{12,20},{16,8},{20,12},{24,0},{28,4},{1,25},{... | collective-permute-start | bytes 196616 | tf_op jit(solution)/shard_map/ppermute | solution.py:256
  34.7 2.5 %forward0.1 = (f32[2,32,512]{2,1,0:T(8,128)S(1)}, bf16[2,32,512]{2,1,0:T(8,128)(2,1)S(1)}, bf16[2,32,512]{2,1,0:T(8,128)(2,1)S(1)}, bf16[2,32,512]{2,1,0:T(8,128)(2,1)S(1)}) custom-call(s32[7,5]{1,0:T(8,128)S(4)} %table.1.table_ref, bf16[6,512,2048]{2,1,0:T(8,128)(2,1)S(1)} %turn.1.turned_ref, bf16[4,2,32,512]{3,2,1,0:T(8,128)(2,1)S(1)} %convert_element_type.208.refs_0_, ...), custom_call_target="tpu_custom_call" | custom-call | flops 402653184 | bytes 12582912 | tf_op jit(solution)/shard_map/forward0/pallas_call | solution.py:208
  40.9 2.0 %collective-permute-done.14 = bf16[2,32,512]{2,1,0:T(8,128)(2,1)S(1)} collective-permute-done((bf16[2,32,512]{2,1,0:T(8,128)(2,1)S(1)}, bf16[2,32,512]{2,1,0:T(8,128)(2,1)S(1)}, u32[]{:S(2)}, u32[]{:S(2)}) %collective-permute-start.14) | collective-permute-done | bytes 65568 | tf_op jit(solution)/shard_map/ppermute | solution.py:260
  47.3 3.3 %collective-permute-start.19 = (bf16[2,32,512]{2,1,0:T(8,128)(2,1)S(1)}, bf16[2,32,512]{2,1,0:T(8,128)(2,1)S(1)}, u32[]{:S(2)}, u32[]{:S(2)}) collective-permute-start(bf16[2,32,512]{2,1,0:T(8,128)(2,1)S(1)} %get-tuple-element.75.refs_4_.refs_8_), channel_id=1, source_target_pairs={{0,24},{4,28},{8,16},{12,20},{16,8},{20,12},{24,0},{28,4},{1,25},{... | collective-permute-start | bytes 196616 | tf_op jit(solution)/shard_map/ppermute | solution.py:182
  51.7 2.6 %backward1.1 = (f32[4,2,32,512]{3,2,1,0:T(8,128)S(1)}, bf16[4,2,32,512]{3,2,1,0:T(8,128)(2,1)S(1)}) custom-call(s32[7,5]{1,0:T(8,128)S(4)} %table.1.table_ref, bf16[6,2048,512]{2,1,0:T(8,128)(2,1)S(1)} %bitcast.71, bf16[4,2,32,512]{3,2,1,0:T(8,128)(2,1)S(1)} %convert_element_type.208.refs_0_, bf16[4,2,32,512]{3,2,1,0:T(8,128)(2,1)S(1)} %collective-permute-done.refs_1_, ...), custom_call_target="tpu_custom_call" | custom-call | flops 402653184 | bytes 12582912 | tf_op jit(solution)/shard_map/backward1/pallas_call | solution.py:189
  57.4 2.0 %collective-permute-start.24 = (bf16[2,32,512]{2,1,0:T(8,128)(2,1)S(1)}, bf16[2,32,512]{2,1,0:T(8,128)(2,1)S(1)}, u32[]{:S(2)}, u32[]{:S(2)}) collective-permute-start(bf16[2,32,512]{2,1,0:T(8,128)(2,1)S(1)} %get-tuple-element.121.refs_16_), channel_id=1, source_target_pairs={{0,24},{4,28},{8,16},{12,20},{16,8},{20,12},{24,0},{28,4},{1,25},{... | collective-permute-start | bytes 196616 | tf_op jit(solution)/shard_map/ppermute | solution.py:256
  61.8 2.6 %forward1.1 = (f32[2,32,512]{2,1,0:T(8,128)S(1)}, bf16[2,32,512]{2,1,0:T(8,128)(2,1)S(1)}, bf16[2,32,512]{2,1,0:T(8,128)(2,1)S(1)}, bf16[2,32,512]{2,1,0:T(8,128)(2,1)S(1)}) custom-call(s32[7,5]{1,0:T(8,128)S(4)} %table.1.table_ref, bf16[6,512,2048]{2,1,0:T(8,128)(2,1)S(1)} %turn.1.turned_ref, bf16[4,2,32,512]{3,2,1,0:T(8,128)(2,1)S(1)} %convert_element_type.208.refs_0_, ...), custom_call_target="tpu_custom_call" | custom-call | flops 402653184 | bytes 12582912 | tf_op jit(solution)/shard_map/forward1/pallas_call | solution.py:208
  68.0 2.3 %collective-permute-done.28 = bf16[2,32,512]{2,1,0:T(8,128)(2,1)S(1)} collective-permute-done((bf16[2,32,512]{2,1,0:T(8,128)(2,1)S(1)}, bf16[2,32,512]{2,1,0:T(8,128)(2,1)S(1)}, u32[]{:S(2)}, u32[]{:S(2)}) %collective-permute-start.28) | collective-permute-done | bytes 65568 | tf_op jit(solution)/shard_map/ppermute | solution.py:260
  75.3 1.9 %collective-permute-start.33 = (bf16[2,32,512]{2,1,0:T(8,128)(2,1)S(1)}, bf16[2,32,512]{2,1,0:T(8,128)(2,1)S(1)}, u32[]{:S(2)}, u32[]{:S(2)}) collective-permute-start(bf16[2,32,512]{2,1,0:T(8,128)(2,1)S(1)} %get-tuple-element.87.refs_8_.refs_13_), channel_id=1, source_target_pairs={{0,24},{4,28},{8,16},{12,20},{16,8},{20,12},{24,0},{28,4},{1,25},{... | collective-permute-start | bytes 196616 | tf_op jit(solution)/shard_map/ppermute | solution.py:182
  77.3 2.4 %collective-permute-start.31 = (bf16[2,32,512]{2,1,0:T(8,128)(2,1)S(1)}, bf16[2,32,512]{2,1,0:T(8,128)(2,1)S(1)}, u32[]{:S(2)}, u32[]{:S(2)}) collective-permute-start(bf16[2,32,512]{2,1,0:T(8,128)(2,1)S(1)} %get-tuple-element.87.refs_8_.refs_13_), channel_id=1, source_target_pairs={{0,8},{4,12},{8,0},{12,4},{16,24},{20,28},{24,16},{28,20},{1,9},{5... | collective-permute-start | bytes 196616 | tf_op jit(solution)/shard_map/ppermute | solution.py:182
  79.7 2.8 %backward2.1 = (f32[4,2,32,512]{3,2,1,0:T(8,128)S(1)}, bf16[4,2,32,512]{3,2,1,0:T(8,128)(2,1)S(1)}) custom-call(s32[7,5]{1,0:T(8,128)S(4)} %table.1.table_ref, bf16[6,2048,512]{2,1,0:T(8,128)(2,1)S(1)} %bitcast.71, bf16[4,2,32,512]{3,2,1,0:T(8,128)(2,1)S(1)} %convert_element_type.208.refs_0_, bf16[4,2,32,512]{3,2,1,0:T(8,128)(2,1)S(1)} %collective-permute-done.refs_1_, ...), custom_call_target="tpu_custom_call" | custom-call | flops 402653184 | bytes 12582912 | tf_op jit(solution)/shard_map/backward2/pallas_call | solution.py:189
  84.4 2.0 %collective-permute-start.38 = (bf16[2,32,512]{2,1,0:T(8,128)(2,1)S(1)}, bf16[2,32,512]{2,1,0:T(8,128)(2,1)S(1)}, u32[]{:S(2)}, u32[]{:S(2)}) collective-permute-start(bf16[2,32,512]{2,1,0:T(8,128)(2,1)S(1)} %get-tuple-element.117.refs_21_), channel_id=1, source_target_pairs={{0,24},{4,28},{8,16},{12,20},{16,8},{20,12},{24,0},{28,4},{1,25},{... | collective-permute-start | bytes 196616 | tf_op jit(solution)/shard_map/ppermute | solution.py:256
  86.7 2.2 %collective-permute-start.39 = (bf16[2,32,512]{2,1,0:T(8,128)(2,1)S(1)}, bf16[2,32,512]{2,1,0:T(8,128)(2,1)S(1)}, u32[]{:S(2)}, u32[]{:S(2)}) collective-permute-start(bf16[2,32,512]{2,1,0:T(8,128)(2,1)S(1)} %get-tuple-element.119.refs_20_), channel_id=1, source_target_pairs={{0,16},{4,20},{8,24},{12,28},{16,0},{20,4},{24,8},{28,12},{1,17},{... | collective-permute-start | bytes 196616 | tf_op jit(solution)/shard_map/ppermute | solution.py:256
  88.9 2.6 %forward2.1 = (f32[2,32,512]{2,1,0:T(8,128)S(1)}, bf16[2,32,512]{2,1,0:T(8,128)(2,1)S(1)}, bf16[2,32,512]{2,1,0:T(8,128)(2,1)S(1)}, bf16[2,32,512]{2,1,0:T(8,128)(2,1)S(1)}) custom-call(s32[7,5]{1,0:T(8,128)S(4)} %table.1.table_ref, bf16[6,512,2048]{2,1,0:T(8,128)(2,1)S(1)} %turn.1.turned_ref, bf16[4,2,32,512]{3,2,1,0:T(8,128)(2,1)S(1)} %convert_element_type.208.refs_0_, ...), custom_call_target="tpu_custom_call" | custom-call | flops 402653184 | bytes 12582912 | tf_op jit(solution)/shard_map/forward2/pallas_call | solution.py:208
  103.4 2.5 %collective-permute-start.45 = (bf16[2,32,512]{2,1,0:T(8,128)(2,1)S(1)}, bf16[2,32,512]{2,1,0:T(8,128)(2,1)S(1)}, u32[]{:S(2)}, u32[]{:S(2)}) collective-permute-start(bf16[2,32,512]{2,1,0:T(8,128)(2,1)S(1)} %get-tuple-element.99.refs_12_.refs_18_), channel_id=1, source_target_pairs={{0,8},{4,12},{8,0},{12,4},{16,24},{20,28},{24,16},{28,20},{1,9},{5... | collective-permute-start | bytes 196616 | tf_op jit(solution)/shard_map/ppermute | solution.py:182
  105.8 2.6 %backward3.1 = (f32[4,2,32,512]{3,2,1,0:T(8,128)S(1)}, bf16[4,2,32,512]{3,2,1,0:T(8,128)(2,1)S(1)}) custom-call(s32[7,5]{1,0:T(8,128)S(4)} %table.1.table_ref, bf16[6,2048,512]{2,1,0:T(8,128)(2,1)S(1)} %bitcast.71, bf16[4,2,32,512]{3,2,1,0:T(8,128)(2,1)S(1)} %convert_element_type.208.refs_0_, bf16[4,2,32,512]{3,2,1,0:T(8,128)(2,1)S(1)} %collective-permute-done.refs_1_, ...), custom_call_target="tpu_custom_call" | custom-call | flops 402653184 | bytes 12582912 | tf_op jit(solution)/shard_map/backward3/pallas_call | solution.py:189
  110.8 2.6 %forward3.1 = (f32[2,32,512]{2,1,0:T(8,128)S(1)}, bf16[2,32,512]{2,1,0:T(8,128)(2,1)S(1)}, bf16[2,32,512]{2,1,0:T(8,128)(2,1)S(1)}, bf16[2,32,512]{2,1,0:T(8,128)(2,1)S(1)}) custom-call(s32[7,5]{1,0:T(8,128)S(4)} %table.1.table_ref, bf16[6,512,2048]{2,1,0:T(8,128)(2,1)S(1)} %turn.1.turned_ref, bf16[4,2,32,512]{3,2,1,0:T(8,128)(2,1)S(1)} %convert_element_type.208.refs_0_, ...), custom_call_target="tpu_custom_call" | custom-call | flops 402653184 | bytes 12582912 | tf_op jit(solution)/shard_map/forward3/pallas_call | solution.py:208
  119.2 2.2 %collective-permute-start.53 = (bf16[2,32,512]{2,1,0:T(8,128)(2,1)S(1)}, bf16[2,32,512]{2,1,0:T(8,128)(2,1)S(1)}, u32[]{:S(2)}, u32[]{:S(2)}) collective-permute-start(bf16[2,32,512]{2,1,0:T(8,128)(2,1)S(1)} %get-tuple-element.115.refs_25_), channel_id=1, source_target_pairs={{0,16},{4,20},{8,24},{12,28},{16,0},{20,4},{24,8},{28,12},{1,17},{... | collective-permute-start | bytes 196616 | tf_op jit(solution)/shard_map/ppermute | solution.py:256
  (132 shorter events, 59.7 us)
Async XLA Ops:
  1.1 10.9 %collective-permute-start.2 = (bf16[4,2,32,512]{3,2,1,0:T(8,128)(2,1)S(1)}, bf16[4,2,32,512]{3,2,1,0:T(8,128)(2,1)S(1)}, u32[]{:S(2)}, u32[]{:S(2)}) collective-permute-start(bf16[4,2,32,512]{3,2,1,0:T(8,128)(2,1)S(1)} %convert_element_type.208.refs_0_), channel_id=1, source_target_pairs={{0,3},{1,2},{2,1},{3,0},{4,7},{5,6},{6,5},{7,4},{8,11},{9,10},{10,... | collective-permute-start | bytes 786440 | tf_op jit(solution)/shard_map/ppermute | solution.py:176
  5.0 21.1 %collective-permute-start.3 = (bf16[4,2,32,512]{3,2,1,0:T(8,128)(2,1)S(1)}, bf16[4,2,32,512]{3,2,1,0:T(8,128)(2,1)S(1)}, u32[]{:S(2)}, u32[]{:S(2)}) collective-permute-start(bf16[4,2,32,512]{3,2,1,0:T(8,128)(2,1)S(1)} %convert_element_type.208.refs_0_), channel_id=1, source_target_pairs={{0,16},{4,20},{8,24},{12,28},{16,0},{20,4},{24,8},{28,12},{1,17},{... | collective-permute-start | bytes 786440 | tf_op jit(solution)/shard_map/ppermute | solution.py:182
  7.6 18.5 %collective-permute-start.1 = (bf16[4,2,32,512]{3,2,1,0:T(8,128)(2,1)S(1)}, bf16[4,2,32,512]{3,2,1,0:T(8,128)(2,1)S(1)}, u32[]{:S(2)}, u32[]{:S(2)}) collective-permute-start(bf16[4,2,32,512]{3,2,1,0:T(8,128)(2,1)S(1)} %convert_element_type.208.refs_0_), channel_id=1, source_target_pairs={{0,2},{1,3},{2,0},{3,1},{4,6},{5,7},{6,4},{7,5},{8,10},{9,11},{10,... | collective-permute-start | bytes 786440 | tf_op jit(solution)/shard_map/ppermute | solution.py:176
  8.1 18.0 %collective-permute-start = (bf16[4,2,32,512]{3,2,1,0:T(8,128)(2,1)S(1)}, bf16[4,2,32,512]{3,2,1,0:T(8,128)(2,1)S(1)}, u32[]{:S(2)}, u32[]{:S(2)}) collective-permute-start(bf16[4,2,32,512]{3,2,1,0:T(8,128)(2,1)S(1)} %convert_element_type.208.refs_0_), channel_id=1, source_target_pairs={{0,1},{1,0},{2,3},{3,2},{4,5},{5,4},{6,7},{7,6},{8,9},{9,8},{10,11... | collective-permute-start | bytes 786440 | tf_op jit(solution)/shard_map/ppermute | solution.py:176
  8.7 20.3 %collective-permute-start.12 = (bf16[4,2,32,512]{3,2,1,0:T(8,128)(2,1)S(1)}, bf16[4,2,32,512]{3,2,1,0:T(8,128)(2,1)S(1)}, u32[]{:S(2)}, u32[]{:S(2)}) collective-permute-start(bf16[4,2,32,512]{3,2,1,0:T(8,128)(2,1)S(1)} %convert_element_type.208.refs_0_), channel_id=1, source_target_pairs={{0,24},{4,28},{8,16},{12,20},{16,8},{20,12},{24,0},{28,4},{1,25},{... | collective-permute-start | bytes 786440 | tf_op jit(solution)/shard_map/ppermute | solution.py:182
  11.9 17.5 %collective-permute-start.9 = (bf16[4,2,32,512]{3,2,1,0:T(8,128)(2,1)S(1)}, bf16[4,2,32,512]{3,2,1,0:T(8,128)(2,1)S(1)}, u32[]{:S(2)}, u32[]{:S(2)}) collective-permute-start(bf16[4,2,32,512]{3,2,1,0:T(8,128)(2,1)S(1)} %convert_element_type.208.refs_0_), channel_id=1, source_target_pairs={{0,8},{4,12},{8,0},{12,4},{16,24},{20,28},{24,16},{28,20},{1,9},{5... | collective-permute-start | bytes 786440 | tf_op jit(solution)/shard_map/ppermute | solution.py:182
  30.0 9.4 %collective-permute-start.5 = (bf16[2,32,512]{2,1,0:T(8,128)(2,1)S(1)}, bf16[2,32,512]{2,1,0:T(8,128)(2,1)S(1)}, u32[]{:S(2)}, u32[]{:S(2)}) collective-permute-start(bf16[2,32,512]{2,1,0:T(8,128)(2,1)S(1)} %get-tuple-element.125.refs_11_), channel_id=1, source_target_pairs={{0,24},{4,28},{8,16},{12,20},{16,8},{20,12},{24,0},{28,4},{1,25},{... | collective-permute-start | bytes 196616 | tf_op jit(solution)/shard_map/ppermute | solution.py:256
  33.2 7.7 %collective-permute-start.7 = (bf16[2,32,512]{2,1,0:T(8,128)(2,1)S(1)}, bf16[2,32,512]{2,1,0:T(8,128)(2,1)S(1)}, u32[]{:S(2)}, u32[]{:S(2)}) collective-permute-start(bf16[2,32,512]{2,1,0:T(8,128)(2,1)S(1)} %get-tuple-element.126.refs_9_), channel_id=1, source_target_pairs={{0,8},{4,12},{8,0},{12,4},{16,24},{20,28},{24,16},{28,20},{1,9},{5... | collective-permute-start | bytes 196616 | tf_op jit(solution)/shard_map/ppermute | solution.py:256
  34.4 6.4 %collective-permute-start.6 = (bf16[2,32,512]{2,1,0:T(8,128)(2,1)S(1)}, bf16[2,32,512]{2,1,0:T(8,128)(2,1)S(1)}, u32[]{:S(2)}, u32[]{:S(2)}) collective-permute-start(bf16[2,32,512]{2,1,0:T(8,128)(2,1)S(1)} %get-tuple-element.127.refs_10_), channel_id=1, source_target_pairs={{0,16},{4,20},{8,24},{12,28},{16,0},{20,4},{24,8},{28,12},{1,17},{... | collective-permute-start | bytes 196616 | tf_op jit(solution)/shard_map/ppermute | solution.py:256
  43.7 6.9 %collective-permute-start.22 = (bf16[2,32,512]{2,1,0:T(8,128)(2,1)S(1)}, bf16[2,32,512]{2,1,0:T(8,128)(2,1)S(1)}, u32[]{:S(2)}, u32[]{:S(2)}) collective-permute-start(bf16[2,32,512]{2,1,0:T(8,128)(2,1)S(1)} %get-tuple-element.75.refs_4_.refs_8_), channel_id=1, source_target_pairs={{0,3},{1,2},{2,1},{3,0},{4,7},{5,6},{6,5},{7,4},{8,11},{9,10},{10,... | collective-permute-start | bytes 196616 | tf_op jit(solution)/shard_map/ppermute | solution.py:176
  45.2 6.5 %collective-permute-start.21 = (bf16[2,32,512]{2,1,0:T(8,128)(2,1)S(1)}, bf16[2,32,512]{2,1,0:T(8,128)(2,1)S(1)}, u32[]{:S(2)}, u32[]{:S(2)}) collective-permute-start(bf16[2,32,512]{2,1,0:T(8,128)(2,1)S(1)} %get-tuple-element.75.refs_4_.refs_8_), channel_id=1, source_target_pairs={{0,2},{1,3},{2,0},{3,1},{4,6},{5,7},{6,4},{7,5},{8,10},{9,11},{10,... | collective-permute-start | bytes 196616 | tf_op jit(solution)/shard_map/ppermute | solution.py:176
  47.3 7.0 %collective-permute-start.19 = (bf16[2,32,512]{2,1,0:T(8,128)(2,1)S(1)}, bf16[2,32,512]{2,1,0:T(8,128)(2,1)S(1)}, u32[]{:S(2)}, u32[]{:S(2)}) collective-permute-start(bf16[2,32,512]{2,1,0:T(8,128)(2,1)S(1)} %get-tuple-element.75.refs_4_.refs_8_), channel_id=1, source_target_pairs={{0,24},{4,28},{8,16},{12,20},{16,8},{20,12},{24,0},{28,4},{1,25},{... | collective-permute-start | bytes 196616 | tf_op jit(solution)/shard_map/ppermute | solution.py:182
  55.8 6.0 %collective-permute-start.27 = (bf16[4,2,32,512]{3,2,1,0:T(8,128)(2,1)S(1)}, bf16[4,2,32,512]{3,2,1,0:T(8,128)(2,1)S(1)}, u32[]{:S(2)}, u32[]{:S(2)}) collective-permute-start(bf16[4,2,32,512]{3,2,1,0:T(8,128)(2,1)S(1)} %pad_maximum_fusion.1), channel_id=1, source_target_pairs={{0,4},{4,0},{8,12},{12,8},{16,20},{20,16},{24,28},{28,24},{1,5},{5... | collective-permute-start | bytes 786440 | tf_op jit(solution)/shard_map/ppermute | solution.py:250
  57.4 10.0 %collective-permute-start.24 = (bf16[2,32,512]{2,1,0:T(8,128)(2,1)S(1)}, bf16[2,32,512]{2,1,0:T(8,128)(2,1)S(1)}, u32[]{:S(2)}, u32[]{:S(2)}) collective-permute-start(bf16[2,32,512]{2,1,0:T(8,128)(2,1)S(1)} %get-tuple-element.121.refs_16_), channel_id=1, source_target_pairs={{0,24},{4,28},{8,16},{12,20},{16,8},{20,12},{24,0},{28,4},{1,25},{... | collective-permute-start | bytes 196616 | tf_op jit(solution)/shard_map/ppermute | solution.py:256
  59.4 8.6 %collective-permute-start.26 = (bf16[2,32,512]{2,1,0:T(8,128)(2,1)S(1)}, bf16[2,32,512]{2,1,0:T(8,128)(2,1)S(1)}, u32[]{:S(2)}, u32[]{:S(2)}) collective-permute-start(bf16[2,32,512]{2,1,0:T(8,128)(2,1)S(1)} %get-tuple-element.122.refs_14_), channel_id=1, source_target_pairs={{0,8},{4,12},{8,0},{12,4},{16,24},{20,28},{24,16},{28,20},{1,9},{5... | collective-permute-start | bytes 196616 | tf_op jit(solution)/shard_map/ppermute | solution.py:256
  60.0 7.9 %collective-permute-start.25 = (bf16[2,32,512]{2,1,0:T(8,128)(2,1)S(1)}, bf16[2,32,512]{2,1,0:T(8,128)(2,1)S(1)}, u32[]{:S(2)}, u32[]{:S(2)}) collective-permute-start(bf16[2,32,512]{2,1,0:T(8,128)(2,1)S(1)} %get-tuple-element.123.refs_15_), channel_id=1, source_target_pairs={{0,16},{4,20},{8,24},{12,28},{16,0},{20,4},{24,8},{28,12},{1,17},{... | collective-permute-start | bytes 196616 | tf_op jit(solution)/shard_map/ppermute | solution.py:256
  72.9 6.9 %collective-permute-start.35 = (bf16[2,32,512]{2,1,0:T(8,128)(2,1)S(1)}, bf16[2,32,512]{2,1,0:T(8,128)(2,1)S(1)}, u32[]{:S(2)}, u32[]{:S(2)}) collective-permute-start(bf16[2,32,512]{2,1,0:T(8,128)(2,1)S(1)} %get-tuple-element.87.refs_8_.refs_13_), channel_id=1, source_target_pairs={{0,2},{1,3},{2,0},{3,1},{4,6},{5,7},{6,4},{7,5},{8,10},{9,11},{10,... | collective-permute-start | bytes 196616 | tf_op jit(solution)/shard_map/ppermute | solution.py:176
  75.3 7.2 %collective-permute-start.33 = (bf16[2,32,512]{2,1,0:T(8,128)(2,1)S(1)}, bf16[2,32,512]{2,1,0:T(8,128)(2,1)S(1)}, u32[]{:S(2)}, u32[]{:S(2)}) collective-permute-start(bf16[2,32,512]{2,1,0:T(8,128)(2,1)S(1)} %get-tuple-element.87.refs_8_.refs_13_), channel_id=1, source_target_pairs={{0,24},{4,28},{8,16},{12,20},{16,8},{20,12},{24,0},{28,4},{1,25},{... | collective-permute-start | bytes 196616 | tf_op jit(solution)/shard_map/ppermute | solution.py:182
  84.4 9.1 %collective-permute-start.38 = (bf16[2,32,512]{2,1,0:T(8,128)(2,1)S(1)}, bf16[2,32,512]{2,1,0:T(8,128)(2,1)S(1)}, u32[]{:S(2)}, u32[]{:S(2)}) collective-permute-start(bf16[2,32,512]{2,1,0:T(8,128)(2,1)S(1)} %get-tuple-element.117.refs_21_), channel_id=1, source_target_pairs={{0,24},{4,28},{8,16},{12,20},{16,8},{20,12},{24,0},{28,4},{1,25},{... | collective-permute-start | bytes 196616 | tf_op jit(solution)/shard_map/ppermute | solution.py:256
  86.4 8.6 %collective-permute-start.40 = (bf16[2,32,512]{2,1,0:T(8,128)(2,1)S(1)}, bf16[2,32,512]{2,1,0:T(8,128)(2,1)S(1)}, u32[]{:S(2)}, u32[]{:S(2)}) collective-permute-start(bf16[2,32,512]{2,1,0:T(8,128)(2,1)S(1)} %get-tuple-element.118.refs_19_), channel_id=1, source_target_pairs={{0,8},{4,12},{8,0},{12,4},{16,24},{20,28},{24,16},{28,20},{1,9},{5... | collective-permute-start | bytes 196616 | tf_op jit(solution)/shard_map/ppermute | solution.py:256
  86.7 8.3 %collective-permute-start.39 = (bf16[2,32,512]{2,1,0:T(8,128)(2,1)S(1)}, bf16[2,32,512]{2,1,0:T(8,128)(2,1)S(1)}, u32[]{:S(2)}, u32[]{:S(2)}) collective-permute-start(bf16[2,32,512]{2,1,0:T(8,128)(2,1)S(1)} %get-tuple-element.119.refs_20_), channel_id=1, source_target_pairs={{0,16},{4,20},{8,24},{12,28},{16,0},{20,4},{24,8},{28,12},{1,17},{... | collective-permute-start | bytes 196616 | tf_op jit(solution)/shard_map/ppermute | solution.py:256
  99.4 6.4 %collective-permute-start.49 = (bf16[2,32,512]{2,1,0:T(8,128)(2,1)S(1)}, bf16[2,32,512]{2,1,0:T(8,128)(2,1)S(1)}, u32[]{:S(2)}, u32[]{:S(2)}) collective-permute-start(bf16[2,32,512]{2,1,0:T(8,128)(2,1)S(1)} %get-tuple-element.99.refs_12_.refs_18_), channel_id=1, source_target_pairs={{0,2},{1,3},{2,0},{3,1},{4,6},{5,7},{6,4},{7,5},{8,10},{9,11},{10,... | collective-permute-start | bytes 196616 | tf_op jit(solution)/shard_map/ppermute | solution.py:176
  101.4 7.0 %collective-permute-start.47 = (bf16[2,32,512]{2,1,0:T(8,128)(2,1)S(1)}, bf16[2,32,512]{2,1,0:T(8,128)(2,1)S(1)}, u32[]{:S(2)}, u32[]{:S(2)}) collective-permute-start(bf16[2,32,512]{2,1,0:T(8,128)(2,1)S(1)} %get-tuple-element.99.refs_12_.refs_18_), channel_id=1, source_target_pairs={{0,24},{4,28},{8,16},{12,20},{16,8},{20,12},{24,0},{28,4},{1,25},{... | collective-permute-start | bytes 196616 | tf_op jit(solution)/shard_map/ppermute | solution.py:182
  114.9 7.7 %collective-permute-start.52 = (bf16[2,32,512]{2,1,0:T(8,128)(2,1)S(1)}, bf16[2,32,512]{2,1,0:T(8,128)(2,1)S(1)}, u32[]{:S(2)}, u32[]{:S(2)}) collective-permute-start(bf16[2,32,512]{2,1,0:T(8,128)(2,1)S(1)} %get-tuple-element.113.refs_26_), channel_id=1, source_target_pairs={{0,24},{4,28},{8,16},{12,20},{16,8},{20,12},{24,0},{28,4},{1,25},{... | collective-permute-start | bytes 196616 | tf_op jit(solution)/shard_map/ppermute | solution.py:256
  (42 other events, 277.4 us)
